TPU v7x, 32 devices: a whole 2x2x4 slice. The times are simulated.
32 devices in a mesh: ctx: 4 (over y, x), pipe: 8 (over z, core).
Axes of the slice: x: 2, y: 2, z: 4, core: 2. Of those that a mesh axis runs over, the one named last changes fastest.
Arguments:
- q_in: bfloat16 [8, 1024, 128], P('pipe', 'ctx'), may hold values from -6 to 6
- k_in: bfloat16 [8, 1024, 128], P('pipe', 'ctx'), may hold values from -6 to 6
- v_in: bfloat16 [8, 1024, 1024], P('pipe', 'ctx'), may hold values from -6 to 6
- gate_in: bfloat16 [8, 1024, 1024], P('pipe', 'ctx'), may hold values from -6 to 6
- out_grad: bfloat16 [8, 1024, 1024], P('pipe', 'ctx'), may hold values from -6 to 6
- conv_weight: bfloat16 [8, 3, 1024], P('pipe'), may hold values from -3.5 to 3.5
- bounds: int32 [8, 4], P('pipe'), may hold values from 0 to 256, as said below
Outputs:
- q_grad: bfloat16 [8, 1024, 128], P('pipe', 'ctx')
- k_grad: bfloat16 [8, 1024, 128], P('pipe', 'ctx')
- v_grad: bfloat16 [8, 1024, 1024], P('pipe', 'ctx')
- gate_grad: bfloat16 [8, 1024, 1024], P('pipe', 'ctx')
Inputs may be any that keep to these rules, and one draw needn't show every extreme that they name: bounds[s, c] is the offset within slice c of section s's sequence (of 256 tokens) at which a new document begins, or 256 where none begins at an offset of that slice; in slice 0 a document begins at offset 0 whatever bounds[s, 0] holds.
All inputs are finite; a program needn't handle non-finite values.
Results may differ from a plain program's by a relative error of at most 0.0015.
Values may be sent and summed in bfloat16 or wider, within the bound.
No kernel may reach another device: no remote copies, remote signals or barrier semaphores. Data moves between devices by JAX's collectives and lax.ppermute only.
A program may use at most 128 MiB of HBM per device.

v0:
```python
import functools

import jax
import jax.numpy as jnp
from jax import lax
from jax.experimental import pallas as pl
from jax.experimental.pallas import tpu as pltpu
from jax.sharding import PartitionSpec as P

HEADS = 8
F = 16
DV = 128
CONV = 3
TOK = 256
ROWS = TOK + 2 * F
BF16 = jnp.bfloat16
F32 = jnp.float32
VMEM_LIMIT = 56 * 1024 * 1024

ANY = pl.BlockSpec(memory_space=pl.ANY)
SMEM = pl.BlockSpec(memory_space=pltpu.SMEM)
VMEM = pl.BlockSpec(memory_space=pltpu.VMEM)


def first_head(place, count):
    return (place * HEADS) // count


def phases_of(count):
    return max(1, HEADS // count)


def senders_of(count):
    return range(0, count, max(1, count // HEADS))


def pack_kernel(count, info, q_ref, k_ref, v_ref, gate_ref, grad_ref, *rest):
    phases = phases_of(count)
    blocks = phases * count
    packed, grads = rest[:blocks], rest[blocks : 2 * blocks]
    turned, sem, sem_turned = rest[2 * blocks :]
    me = info[0]
    copies = []
    for phase in range(phases):
        for partner in range(count):
            head = first_head(me ^ partner, count) + phase
            lanes = pl.ds(pl.multiple_of(head * DV, DV), DV)
            where = phase * count + partner
            out = packed[where]
            copies.append((v_ref.at[0, :, lanes], out.at[0:TOK, 0:DV]))
            copies.append((gate_ref.at[0, :, lanes], out.at[0:TOK, DV : 2 * DV]))
            copies.append((grad_ref.at[0, :, lanes], grads[where]))
    copies = [pltpu.make_async_copy(a, b, sem.at[n]) for n, (a, b) in enumerate(copies)]
    for copy in copies:
        copy.start()
    turned[0] = q_ref[0].astype(F32).T.astype(BF16)
    turned[1] = k_ref[0].astype(F32).T.astype(BF16)
    small = []
    for phase in range(phases):
        for partner in range(count):
            head = first_head(me ^ partner, count) + phase
            rows = pl.ds(pl.multiple_of(head * F, F), F)
            out = packed[phase * count + partner]
            for side in range(2):
                small.append((turned.at[side, rows], out.at[TOK + side * F : TOK + (side + 1) * F]))
    small = [pltpu.make_async_copy(a, b, sem_turned.at[n]) for n, (a, b) in enumerate(small)]
    for copy in small:
        copy.start()
    for copy in copies + small:
        copy.wait()


def pack(count, info, q_in, k_in, v_in, gate_in, grad):
    blocks = phases_of(count) * count
    out = pl.pallas_call(
        functools.partial(pack_kernel, count),
        out_shape=[jax.ShapeDtypeStruct((ROWS, 2 * DV), BF16)] * blocks
        + [jax.ShapeDtypeStruct((TOK, DV), BF16)] * blocks,
        in_specs=[SMEM, VMEM, VMEM, ANY, ANY, ANY],
        out_specs=[VMEM] * (2 * blocks),
        scratch_shapes=[
            pltpu.VMEM((2, HEADS * F, TOK), BF16),
            pltpu.SemaphoreType.DMA((3 * blocks,)),
            pltpu.SemaphoreType.DMA((2 * blocks,)),
        ],
        compiler_params=pltpu.CompilerParams(vmem_limit_bytes=VMEM_LIMIT),
    )(info, q_in, k_in, v_in, gate_in, grad)
    return out[:blocks], out[blocks:]


def nn(a, b):
    return lax.dot_general(a, b, (((1,), (0,)), ((), ())), preferred_element_type=F32)


def nt(a, b):
    return lax.dot_general(a, b, (((1,), (1,)), ((), ())), preferred_element_type=F32)


def halves(x):
    high = x.astype(BF16)
    return high, (x - high.astype(F32)).astype(BF16)


def iota(shape, dim):
    return lax.broadcasted_iota(jnp.int32, shape, dim)


def each(low, high, body):
    if isinstance(low, int) and isinstance(high, int) and high - low <= 4:
        for step in range(low, high):
            body(step)
    else:

        def one(step, carry):
            body(step)
            return carry

        lax.fori_loop(low, high, one, 0)


def attend_kernel(count, phase, info, taps_ref, *rest):
    senders = senders_of(count)
    packed, grads = rest[:count], rest[count : 2 * count]
    outs = rest[2 * count : 2 * count + len(senders)]
    (block, grad, gates, mixed_grads, high_s, low_s, base_s, num_s, dq_s, dk_s, dv_s, stage,
     sem_in, sem_grad, sem_out) = rest[2 * count + len(senders) :]
    me = info[0]
    arriving = []
    for partner in range(count):
        arriving.append(
            pltpu.make_async_copy(packed[partner], block.at[me ^ partner], sem_in.at[partner])
        )
        arriving.append(
            pltpu.make_async_copy(grads[partner], grad.at[me ^ partner], sem_grad.at[partner])
        )
    for copy in arriving:
        copy.start()
    head = first_head(me, count) + phase
    taps = taps_ref[0, :, pl.ds(pl.multiple_of(head * DV, DV), DV)].astype(F32)
    dk_s[...] = jnp.zeros_like(dk_s)
    dv_s[...] = jnp.zeros_like(dv_s)
    gates[0:8] = jnp.zeros((8, DV), F32)
    mixed_grads[:, count * TOK : count * TOK + 8] = jnp.zeros((CONV, 8, DV), F32)
    for copy in arriving:
        copy.wait()

    def spread(j):
        gates[pl.ds(8 + j * TOK, TOK)] = block[j, 0:TOK, DV : 2 * DV].astype(F32)

    each(0, count, spread)

    def opening(i):
        bound = info[1 + i]
        return jnp.where(bound < TOK, i * TOK + bound, 0)

    def earlier(i):
        if isinstance(i, int):
            last = jnp.int32(0)
            for j in range(i):
                last = jnp.maximum(last, opening(j))
            return last
        return lax.fori_loop(0, i, lambda j, last: jnp.maximum(last, opening(j)), jnp.int32(0))

    def doc_start(i, shape):
        token = iota(shape, 0)
        return jnp.where(token >= info[1 + i], opening(i), earlier(i))

    def row_block(i):
        bound = info[1 + i]
        before = earlier(i)
        in_old = iota((TOK, 2 * DV), 0) < bound
        in_old_lanes = iota((2 * DV, TOK), 1) < bound
        row, col = iota((TOK, TOK), 0), iota((TOK, TOK), 1)
        same = (col <= row) & ((col >= bound) | (row < bound))
        query_t = block[i, TOK : TOK + F] * BF16(0.25)
        query = query_t.astype(F32).T.astype(BF16)
        ones = jnp.ones((TOK, DV), BF16)

        def keys(j):
            return block[j, TOK + F : TOK + 2 * F]

        def kernel_of(j):
            base = 1.0 + nn(query, keys(j))
            return base, 0.5 * base * base + 0.5

        base, kern = kernel_of(i)
        high, low = halves(jnp.where(same, kern, 0.0))
        base_s[i] = base
        high_s[i] = high
        low_s[i] = low
        values_one = jnp.concatenate([block[i, 0:TOK, 0:DV], ones], axis=1)
        own = nn(high, values_one) + nn(low, values_one)
        num_s[...] = jnp.zeros_like(num_s)

        def forward(j):
            base, kern = kernel_of(j)
            high, low = halves(kern)
            base_s[j] = base
            high_s[j] = high
            low_s[j] = low
            values_one = jnp.concatenate([block[j, 0:TOK, 0:DV], ones], axis=1)
            values_one = jnp.where(
                iota((TOK, 2 * DV), 0) + j * TOK >= before, values_one.astype(F32), 0.0
            ).astype(BF16)
            num_s[...] += nn(high, values_one) + nn(low, values_one)

        each(0, i, forward)
        total = own + jnp.where(in_old, num_s[...], 0.0)
        num, den = total[:, 0:DV], total[:, DV:]

        position = iota((TOK, DV), 0) + i * TOK
        depth = position - doc_start(i, (TOK, DV))
        mixed = taps[0:1] * gates[pl.ds(8 + i * TOK, TOK)]
        for shift in range(1, CONV):
            moved = gates[pl.ds(8 - shift + i * TOK, TOK)]
            mixed += jnp.where(depth >= shift, taps[shift : shift + 1] * moved, 0.0)
        incoming = grad[i].astype(F32)
        gate = 1.0 / (1.0 + jnp.exp(-mixed))
        attended = num / den
        d_num = incoming * mixed * gate / den
        d_den = -jnp.sum(d_num * attended, axis=1, keepdims=True)
        mixed_grad = incoming * attended * gate * (1.0 + mixed * (1.0 - gate))
        mixed_grads[0, pl.ds(i * TOK, TOK)] = mixed_grad
        for shift in range(1, CONV):
            mixed_grads[shift, pl.ds(i * TOK, TOK)] = jnp.where(depth >= shift, mixed_grad, 0.0)
        d_high, d_low = halves(d_num)
        d_pair = jnp.concatenate([d_high, d_low], axis=1)
        d_pair_f32 = d_pair.astype(F32)
        d_pair_t = d_pair_f32.T
        d_pair_old = jnp.where(in_old, d_pair_f32, 0.0).astype(BF16)
        d_pair_old_t = jnp.where(in_old_lanes, d_pair_t, 0.0).astype(BF16)
        d_pair_t = d_pair_t.astype(BF16)
        d_den_old = jnp.where(iota((TOK, 1), 0) < bound, d_den, 0.0)

        def twice(j):
            value = block[j, 0:TOK, 0:DV]
            return jnp.concatenate([value, value], axis=1)

        slope = (nt(d_pair, twice(i)) + d_den) * base_s[i]
        s_high, s_low = halves(jnp.where(same, slope, 0.0))
        dv_s[i] += nn(d_pair_t, high_s[i]) + nn(d_pair_t, low_s[i])
        dk_s[i] += nn(query_t, s_high) + nn(query_t, s_low)
        dq_s[i] = nt(keys(i), s_high) + nt(keys(i), s_low)

        def backward(j):
            allowed = iota((TOK, TOK), 1) + j * TOK >= before
            slope = (nt(d_pair_old, twice(j)) + d_den_old) * base_s[j]
            s_high, s_low = halves(jnp.where(allowed, slope, 0.0))
            dv_s[j] += jnp.where(
                allowed, nn(d_pair_old_t, high_s[j]) + nn(d_pair_old_t, low_s[j]), 0.0
            )
            dk_s[j] += nn(query_t, s_high) + nn(query_t, s_low)
            dq_s[i] += nt(keys(j), s_high) + nt(keys(j), s_low)

        each(0, i, backward)

    each(0, count, row_block)

    def finish(j):
        total = dv_s[j, 0:DV] + dv_s[j, DV : 2 * DV]
        stage[j, 0:TOK, 0:DV] = total.T.astype(BF16)
        back = taps[0:1] * mixed_grads[0, pl.ds(j * TOK, TOK)]
        for shift in range(1, CONV):
            back += taps[shift : shift + 1] * mixed_grads[shift, pl.ds(j * TOK + shift, TOK)]
        stage[j, 0:TOK, DV : 2 * DV] = back.astype(BF16)
        stage[j, TOK : TOK + F] = (0.25 * dq_s[j]).astype(BF16)
        stage[j, TOK + F : TOK + 2 * F] = dk_s[j].astype(BF16)

    each(0, count, finish)
    leaving = [
        pltpu.make_async_copy(stage.at[me ^ partner], out, sem_out.at[n])
        for n, (partner, out) in enumerate(zip(senders, outs))
    ]
    for copy in leaving:
        copy.start()
    for copy in leaving:
        copy.wait()


def attend(count, phase, info, taps, packed, grads):
    outs = len(senders_of(count))
    return pl.pallas_call(
        functools.partial(attend_kernel, count, phase),
        out_shape=[jax.ShapeDtypeStruct((ROWS, 2 * DV), BF16)] * outs,
        in_specs=[SMEM, VMEM] + [ANY] * (2 * count),
        out_specs=[ANY] * outs,
        scratch_shapes=[
            pltpu.VMEM((count, ROWS, 2 * DV), BF16),
            pltpu.VMEM((count, TOK, DV), BF16),
            pltpu.VMEM((count * TOK + 8, DV), F32),
            pltpu.VMEM((CONV, count * TOK + 8, DV), F32),
            pltpu.VMEM((count, TOK, TOK), BF16),
            pltpu.VMEM((count, TOK, TOK), BF16),
            pltpu.VMEM((count, TOK, TOK), F32),
            pltpu.VMEM((TOK, 2 * DV), F32),
            pltpu.VMEM((count, F, TOK), F32),
            pltpu.VMEM((count, F, TOK), F32),
            pltpu.VMEM((count, 2 * DV, TOK), F32),
            pltpu.VMEM((count, ROWS, 2 * DV), BF16),
            pltpu.SemaphoreType.DMA((count,)),
            pltpu.SemaphoreType.DMA((count,)),
            pltpu.SemaphoreType.DMA((outs,)),
        ],
        compiler_params=pltpu.CompilerParams(vmem_limit_bytes=VMEM_LIMIT),
    )(info, taps, *packed, *grads)


def unpack_kernel(count, info, *rest):
    phases, senders = phases_of(count), senders_of(count)
    blocks = phases * len(senders)
    arrived = rest[:blocks]
    q_ref, k_ref, v_ref, gate_ref, turned, sem, sem_turned = rest[blocks:]
    me = info[0]
    copies, small = [], []
    for phase in range(phases):
        for n, partner in enumerate(senders):
            block = arrived[phase * len(senders) + n]
            head = first_head(me ^ partner, count) + phase
            lanes = pl.ds(pl.multiple_of(head * DV, DV), DV)
            rows = pl.ds(pl.multiple_of(head * F, F), F)
            for side in range(2):
                small.append(
                    (block.at[TOK + side * F : TOK + (side + 1) * F], turned.at[side, rows])
                )
            copies.append((block.at[0:TOK, 0:DV], v_ref.at[0, :, lanes]))
            copies.append((block.at[0:TOK, DV : 2 * DV], gate_ref.at[0, :, lanes]))
    small = [pltpu.make_async_copy(a, b, sem_turned.at[n]) for n, (a, b) in enumerate(small)]
    copies = [pltpu.make_async_copy(a, b, sem.at[n]) for n, (a, b) in enumerate(copies)]
    for copy in small + copies:
        copy.start()
    for copy in small:
        copy.wait()
    q_ref[0] = turned[0].astype(F32).T.astype(BF16)
    k_ref[0] = turned[1].astype(F32).T.astype(BF16)
    for copy in copies:
        copy.wait()


def unpack(count, info, arrived):
    blocks = len(arrived)
    return pl.pallas_call(
        functools.partial(unpack_kernel, count),
        out_shape=[jax.ShapeDtypeStruct((1, TOK, HEADS * F), BF16)] * 2
        + [jax.ShapeDtypeStruct((1, TOK, HEADS * DV), BF16)] * 2,
        in_specs=[SMEM] + [ANY] * blocks,
        out_specs=[VMEM] * 4,
        scratch_shapes=[
            pltpu.VMEM((2, HEADS * F, TOK), BF16),
            pltpu.SemaphoreType.DMA((2 * blocks,)),
            pltpu.SemaphoreType.DMA((2 * blocks,)),
        ],
        compiler_params=pltpu.CompilerParams(vmem_limit_bytes=VMEM_LIMIT),
    )(info, *arrived)


def on_device(count, sections, q_in, k_in, v_in, gate_in, out_grad, conv_weight, bounds):
    me = lax.axis_index("ctx")
    info = jnp.concatenate([me.astype(jnp.int32)[None], bounds[0]])
    phases, senders = phases_of(count), senders_of(count)

    def across(value, partner):
        if partner == 0:
            return value
        return lax.ppermute(value, "ctx", [(c, c ^ partner) for c in range(count)])

    def across_back(value, partner):
        pairs = [
            (c * sections + s, (c ^ partner) * sections + (s - 1) % sections)
            for c in range(count)
            for s in range(sections)
        ]
        return lax.ppermute(value, ("ctx", "pipe"), pairs)

    packed, grads = pack(count, info, q_in, k_in, v_in, gate_in, out_grad)
    arrived = []
    for phase in range(phases):
        mine = packed[phase * count : (phase + 1) * count]
        theirs = grads[phase * count : (phase + 1) * count]
        mine = [across(block, partner) for partner, block in enumerate(mine)]
        theirs = [across_back(block, partner) for partner, block in enumerate(theirs)]
        results = attend(count, phase, info, conv_weight, mine, theirs)
        arrived += [across_back(block, partner) for partner, block in zip(senders, results)]
    return tuple(unpack(count, info, arrived))


def solution(mesh):
    count, sections = mesh.shape["ctx"], mesh.shape["pipe"]
    split = P("pipe", "ctx", None)
    in_specs = (split,) * 5 + (P("pipe", None, None), P("pipe", None))
    return jax.shard_map(
        functools.partial(on_device, count, sections),
        mesh=mesh,
        in_specs=in_specs,
        out_specs=(split,) * 4,
        check_vma=False,
    )
```

profile of v0, /device:TPU:0, one launch (start us, length us, event | category | flops | bytes accessed | tf_op | source)
XLA Modules:
  0.0 72.5 jit_solution(15229360886861823545)
XLA Ops:
  0.6 0.6 copy-done.22
  1.3 0.6 pad_add_fusion.info
  1.9 3.9 %shard_map.102 = (bf16[288,256]{1,0:T(8,128)(2,1)}, bf16[288,256]{1,0:T(8,128)(2,1)}, bf16[288,256]{1,0:T(8,128)(2,1)}, bf16[288,256]{1,0:T(8,128)(2,1)}, bf16[2...) custom-call(s32[5]{0:T(128)} %pad_add_fusion.info, ...), custom_call_target="tpu_custom_call" | custom-call | tf_op jit(solution)/shard_map/pallas_call | solution.py:75
  5.8 4.5 %collective-permute-start.3 = (bf16[256,128]{1,0:T(8,128)(2,1)}, bf16[256,128]{1,0:T(8,128)(2,1)S(1)}, u32[]{:S(2)}, u32[]{:S(2)}) collective-permute-start(bf16[256,128]{1,0:T(8,128)(2,1)} %get-tuple-element.32), channel_id=1, source_target_pairs={{0,7},{1,0},{2,1},{3,2},{4,3},{5,4},{6,5},{7,6},{8,15},{9,8},{10,9... | collective-permute-start | bytes 196616 | tf_op jit(solution)/shard_map/ppermute | solution.py:372
  10.3 1.6 %collective-permute-start.4 = (bf16[256,128]{1,0:T(8,128)(2,1)}, bf16[256,128]{1,0:T(8,128)(2,1)S(1)}, u32[]{:S(2)}, u32[]{:S(2)}) collective-permute-start(bf16[256,128]{1,0:T(8,128)(2,1)} %get-tuple-element.33), channel_id=1, source_target_pairs={{0,15},{1,8},{2,9},{3,10},{4,11},{5,12},{6,13},{7,14},{8,7},{9,0},... | collective-permute-start | bytes 196616 | tf_op jit(solution)/shard_map/ppermute | solution.py:372
  11.9 1.2 %collective-permute-start.5 = (bf16[256,128]{1,0:T(8,128)(2,1)}, bf16[256,128]{1,0:T(8,128)(2,1)S(1)}, u32[]{:S(2)}, u32[]{:S(2)}) collective-permute-start(bf16[256,128]{1,0:T(8,128)(2,1)} %get-tuple-element.34), channel_id=1, source_target_pairs={{0,23},{1,16},{2,17},{3,18},{4,19},{5,20},{6,21},{7,22},{8,31},{9,... | collective-permute-start | bytes 196616 | tf_op jit(solution)/shard_map/ppermute | solution.py:372
  13.1 0.5 collective-permute-start
  13.6 1.1 %collective-permute-start.6 = (bf16[256,128]{1,0:T(8,128)(2,1)}, bf16[256,128]{1,0:T(8,128)(2,1)S(1)}, u32[]{:S(2)}, u32[]{:S(2)}) collective-permute-start(bf16[256,128]{1,0:T(8,128)(2,1)} %get-tuple-element.35), channel_id=1, source_target_pairs={{0,31},{1,24},{2,25},{3,26},{4,27},{5,28},{6,29},{7,30},{8,23},{9,... | collective-permute-start | bytes 196616 | tf_op jit(solution)/shard_map/ppermute | solution.py:372
  14.7 0.0 collective-permute-done.3.rest_4_
  14.7 1.3 %collective-permute-start.14 = (bf16[256,128]{1,0:T(8,128)(2,1)}, bf16[256,128]{1,0:T(8,128)(2,1)S(1)}, u32[]{:S(2)}, u32[]{:S(2)}) collective-permute-start(bf16[256,128]{1,0:T(8,128)(2,1)} %get-tuple-element.44), channel_id=1, source_target_pairs={{0,7},{1,0},{2,1},{3,2},{4,3},{5,4},{6,5},{7,6},{8,15},{9,8},{10,9... | collective-permute-start | bytes 196616 | tf_op jit(solution)/shard_map/ppermute | solution.py:372
  16.0 0.0 collective-permute-done.4.rest_5_
  16.0 1.5 %collective-permute-start.1 = (bf16[288,256]{1,0:T(8,128)(2,1)}, bf16[288,256]{1,0:T(8,128)(2,1)S(1)}, u32[]{:S(2)}, u32[]{:S(2)}) collective-permute-start(bf16[288,256]{1,0:T(8,128)(2,1)} %get-tuple-element.30), channel_id=1, source_target_pairs={{0,16},{8,24},{16,0},{24,8},{1,17},{9,25},{17,1},{25,9},{2,18},{10... | collective-permute-start | bytes 442376 | tf_op jit(solution)/shard_map/ppermute | solution.py:364
  17.5 0.0 collective-permute-done.5.rest_6_
  17.5 1.4 %collective-permute-start.2 = (bf16[288,256]{1,0:T(8,128)(2,1)}, bf16[288,256]{1,0:T(8,128)(2,1)S(1)}, u32[]{:S(2)}, u32[]{:S(2)}) collective-permute-start(bf16[288,256]{1,0:T(8,128)(2,1)} %get-tuple-element.31), channel_id=1, source_target_pairs={{0,24},{8,16},{16,8},{24,0},{1,25},{9,17},{17,9},{25,1},{2,26},{10... | collective-permute-start | bytes 442376 | tf_op jit(solution)/shard_map/ppermute | solution.py:364
  19.0 1.9 %collective-permute-done.6.rest_7_ = bf16[256,128]{1,0:T(8,128)(2,1)S(1)} collective-permute-done((bf16[256,128]{1,0:T(8,128)(2,1)}, bf16[256,128]{1,0:T(8,128)(2,1)S(1)}, u32[]{:S(2)}, u32[]{:S(2)}) %collective-permute-start.6) | collective-permute-done | bytes 65568 | tf_op jit(solution)/shard_map/ppermute | solution.py:372
  20.9 0.6 collective-permute-start.11
  21.5 1.2 %collective-permute-start.15 = (bf16[256,128]{1,0:T(8,128)(2,1)}, bf16[256,128]{1,0:T(8,128)(2,1)S(1)}, u32[]{:S(2)}, u32[]{:S(2)}) collective-permute-start(bf16[256,128]{1,0:T(8,128)(2,1)} %get-tuple-element.45), channel_id=1, source_target_pairs={{0,15},{1,8},{2,9},{3,10},{4,11},{5,12},{6,13},{7,14},{8,7},{9,0},... | collective-permute-start | bytes 196616 | tf_op jit(solution)/shard_map/ppermute | solution.py:372
  22.7 6.0 %collective-permute-done.15.rest_5_ = bf16[256,128]{1,0:T(8,128)(2,1)S(1)} collective-permute-done((bf16[256,128]{1,0:T(8,128)(2,1)}, bf16[256,128]{1,0:T(8,128)(2,1)S(1)}, u32[]{:S(2)}, u32[]{:S(2)}) %collective-permute-start.15) | collective-permute-done | bytes 65568 | tf_op jit(solution)/shard_map/ppermute | solution.py:372
  28.7 0.6 collective-permute-start.16
  29.3 0.0 collective-permute-done.rest_1_
  29.3 1.0 %collective-permute-start.17 = (bf16[256,128]{1,0:T(8,128)(2,1)}, bf16[256,128]{1,0:T(8,128)(2,1)S(1)}, u32[]{:S(2)}, u32[]{:S(2)}) collective-permute-start(bf16[256,128]{1,0:T(8,128)(2,1)} %get-tuple-element.47), channel_id=1, source_target_pairs={{0,31},{1,24},{2,25},{3,26},{4,27},{5,28},{6,29},{7,30},{8,23},{9,... | collective-permute-start | bytes 196616 | tf_op jit(solution)/shard_map/ppermute | solution.py:372
  30.3 0.0 collective-permute-done.1.rest_2_
  30.3 1.2 %collective-permute-start.12 = (bf16[288,256]{1,0:T(8,128)(2,1)}, bf16[288,256]{1,0:T(8,128)(2,1)S(1)}, u32[]{:S(2)}, u32[]{:S(2)}) collective-permute-start(bf16[288,256]{1,0:T(8,128)(2,1)} %get-tuple-element.42), channel_id=1, source_target_pairs={{0,16},{8,24},{16,0},{24,8},{1,17},{9,25},{17,1},{25,9},{2,18},{10... | collective-permute-start | bytes 442376 | tf_op jit(solution)/shard_map/ppermute | solution.py:364
  31.5 1.7 %collective-permute-start.13 = (bf16[288,256]{1,0:T(8,128)(2,1)}, bf16[288,256]{1,0:T(8,128)(2,1)S(1)}, u32[]{:S(2)}, u32[]{:S(2)}) collective-permute-start(bf16[288,256]{1,0:T(8,128)(2,1)} %get-tuple-element.43), channel_id=1, source_target_pairs={{0,24},{8,16},{16,8},{24,0},{1,25},{9,17},{17,9},{25,1},{2,26},{10... | collective-permute-start | bytes 442376 | tf_op jit(solution)/shard_map/ppermute | solution.py:364
  33.3 8.7 %shard_map.103 = (bf16[288,256]{1,0:T(8,128)(2,1)}, bf16[288,256]{1,0:T(8,128)(2,1)}, bf16[288,256]{1,0:T(8,128)(2,1)}, bf16[288,256]{1,0:T(8,128)(2,1)}) custom-call(s32[5]{0:T(128)} %pad_add_fusion.info, bf16[1,3,1024]{2,1,0:T(4,128)(2,1)} %taps_ref.3, bf16[288,256]{1,0:T(8,128)(2,1)} %get-tuple-element.28.rest_0_, bf16[288,256]{1,0:T(8,128)(2,1)} %copy-done.3, ...), custom_call_target="tpu_custom_call" | custom-call | tf_op jit(solution)/shard_map/pallas_call | solution.py:282
  42.0 0.0 copy-start.19
  42.0 0.1 collective-permute-start.7
  42.1 0.0 collective-permute-done.17.rest_7_
  42.1 0.0 copy-start.21
  42.1 0.5 collective-permute-start.8
  42.6 0.9 %collective-permute-start.9 = (bf16[288,256]{1,0:T(8,128)(2,1)}, bf16[288,256]{1,0:T(8,128)(2,1)S(1)}, u32[]{:S(2)}, u32[]{:S(2)}) collective-permute-start(bf16[288,256]{1,0:T(8,128)(2,1)} %get-tuple-element.38), channel_id=1, source_target_pairs={{0,23},{1,16},{2,17},{3,18},{4,19},{5,20},{6,21},{7,22},{8,31},{9,... | collective-permute-start | bytes 442376 | tf_op jit(solution)/shard_map/ppermute | solution.py:372
  43.4 0.0 collective-permute-done.12.rest_2_
  43.4 2.7 %collective-permute-start.10 = (bf16[288,256]{1,0:T(8,128)(2,1)}, bf16[288,256]{1,0:T(8,128)(2,1)S(1)}, u32[]{:S(2)}, u32[]{:S(2)}) collective-permute-start(bf16[288,256]{1,0:T(8,128)(2,1)} %get-tuple-element.39), channel_id=1, source_target_pairs={{0,31},{1,24},{2,25},{3,26},{4,27},{5,28},{6,29},{7,30},{8,23},{9,... | collective-permute-start | bytes 442376 | tf_op jit(solution)/shard_map/ppermute | solution.py:372
  46.1 0.0 collective-permute-done.13.rest_3_
  46.2 0.6 copy-done.8
  46.8 8.6 %shard_map.104 = (bf16[288,256]{1,0:T(8,128)(2,1)}, bf16[288,256]{1,0:T(8,128)(2,1)}, bf16[288,256]{1,0:T(8,128)(2,1)}, bf16[288,256]{1,0:T(8,128)(2,1)}) custom-call(s32[5]{0:T(128)} %pad_add_fusion.info, bf16[1,3,1024]{2,1,0:T(4,128)(2,1)} %taps_ref.3, bf16[288,256]{1,0:T(8,128)(2,1)} %get-tuple-element.40.rest_0_, bf16[288,256]{1,0:T(8,128)(2,1)} %copy-done, ...), custom_call_target="tpu_custom_call" | custom-call | tf_op jit(solution)/shard_map/pallas_call | solution.py:282
  55.4 0.4 collective-permute-start.18
  55.8 0.0 collective-permute-done.7.rest_0_
  55.8 2.4 %collective-permute-start.19 = (bf16[288,256]{1,0:T(8,128)(2,1)}, bf16[288,256]{1,0:T(8,128)(2,1)S(1)}, u32[]{:S(2)}, u32[]{:S(2)}) collective-permute-start(bf16[288,256]{1,0:T(8,128)(2,1)} %get-tuple-element.49), channel_id=1, source_target_pairs={{0,15},{1,8},{2,9},{3,10},{4,11},{5,12},{6,13},{7,14},{8,7},{9,0},... | collective-permute-start | bytes 442376 | tf_op jit(solution)/shard_map/ppermute | solution.py:372
  58.2 0.0 collective-permute-done.8.rest_1_
  58.2 1.4 %collective-permute-start.20 = (bf16[288,256]{1,0:T(8,128)(2,1)}, bf16[288,256]{1,0:T(8,128)(2,1)S(1)}, u32[]{:S(2)}, u32[]{:S(2)}) collective-permute-start(bf16[288,256]{1,0:T(8,128)(2,1)} %get-tuple-element.50), channel_id=1, source_target_pairs={{0,23},{1,16},{2,17},{3,18},{4,19},{5,20},{6,21},{7,22},{8,31},{9,... | collective-permute-start | bytes 442376 | tf_op jit(solution)/shard_map/ppermute | solution.py:372
  59.6 1.2 %collective-permute-start.21 = (bf16[288,256]{1,0:T(8,128)(2,1)}, bf16[288,256]{1,0:T(8,128)(2,1)S(1)}, u32[]{:S(2)}, u32[]{:S(2)}) collective-permute-start(bf16[288,256]{1,0:T(8,128)(2,1)} %get-tuple-element.51), channel_id=1, source_target_pairs={{0,31},{1,24},{2,25},{3,26},{4,27},{5,28},{6,29},{7,30},{8,23},{9,... | collective-permute-start | bytes 442376 | tf_op jit(solution)/shard_map/ppermute | solution.py:372
  60.8 0.0 collective-permute-done.10.rest_3_
  60.8 1.4 %collective-permute-done.19.rest_5_ = bf16[288,256]{1,0:T(8,128)(2,1)S(1)} collective-permute-done((bf16[288,256]{1,0:T(8,128)(2,1)}, bf16[288,256]{1,0:T(8,128)(2,1)S(1)}, u32[]{:S(2)}, u32[]{:S(2)}) %collective-permute-start.19) | collective-permute-done | bytes 147488 | tf_op jit(solution)/shard_map/ppermute | solution.py:372
  62.2 5.5 %collective-permute-done.20.rest_6_ = bf16[288,256]{1,0:T(8,128)(2,1)S(1)} collective-permute-done((bf16[288,256]{1,0:T(8,128)(2,1)}, bf16[288,256]{1,0:T(8,128)(2,1)S(1)}, u32[]{:S(2)}, u32[]{:S(2)}) %collective-permute-start.20) | collective-permute-done | bytes 147488 | tf_op jit(solution)/shard_map/ppermute | solution.py:372
  67.8 0.6 copy-done.12
  68.4 0.7 copy-done.13
  69.0 3.3 %shard_map.105 = (bf16[1,256,128]{2,1,0:T(8,128)(2,1)}, bf16[1,256,128]{2,1,0:T(8,128)(2,1)}, bf16[1,256,1024]{2,1,0:T(8,128)(2,1)}, bf16[1,256,1024]{2,1,0:T(8,128)(2,1)}) custom-call(s32[5]{0:T(128)} %pad_add_fusion.info, bf16[288,256]{1,0:T(8,128)(2,1)} %copy-done.1, bf16[288,256]{1,0:T(8,128)(2,1)} %copy-done.2, bf16[288,256]{1,0:T(8,128)(2,1)} %copy-done.4, ...), custom_call_target="tpu_custom_call" | custom-call | tf_op jit(solution)/shard_map/pallas_call | solution.py:341
  (47 shorter events, 0.1 us)
Async XLA Ops:
  0.6 0.7 copy-start.22
  5.8 9.0 %collective-permute-start.3 = (bf16[256,128]{1,0:T(8,128)(2,1)}, bf16[256,128]{1,0:T(8,128)(2,1)S(1)}, u32[]{:S(2)}, u32[]{:S(2)}) collective-permute-start(bf16[256,128]{1,0:T(8,128)(2,1)} %get-tuple-element.32), channel_id=1, source_target_pairs={{0,7},{1,0},{2,1},{3,2},{4,3},{5,4},{6,5},{7,6},{8,15},{9,8},{10,9... | collective-permute-start | bytes 196616 | tf_op jit(solution)/shard_map/ppermute | solution.py:372
  10.3 5.7 %collective-permute-start.4 = (bf16[256,128]{1,0:T(8,128)(2,1)}, bf16[256,128]{1,0:T(8,128)(2,1)S(1)}, u32[]{:S(2)}, u32[]{:S(2)}) collective-permute-start(bf16[256,128]{1,0:T(8,128)(2,1)} %get-tuple-element.33), channel_id=1, source_target_pairs={{0,15},{1,8},{2,9},{3,10},{4,11},{5,12},{6,13},{7,14},{8,7},{9,0},... | collective-permute-start | bytes 196616 | tf_op jit(solution)/shard_map/ppermute | solution.py:372
  11.9 5.6 %collective-permute-start.5 = (bf16[256,128]{1,0:T(8,128)(2,1)}, bf16[256,128]{1,0:T(8,128)(2,1)S(1)}, u32[]{:S(2)}, u32[]{:S(2)}) collective-permute-start(bf16[256,128]{1,0:T(8,128)(2,1)} %get-tuple-element.34), channel_id=1, source_target_pairs={{0,23},{1,16},{2,17},{3,18},{4,19},{5,20},{6,21},{7,22},{8,31},{9,... | collective-permute-start | bytes 196616 | tf_op jit(solution)/shard_map/ppermute | solution.py:372
  13.1 16.2 %collective-permute-start = (bf16[288,256]{1,0:T(8,128)(2,1)}, bf16[288,256]{1,0:T(8,128)(2,1)S(1)}, u32[]{:S(2)}, u32[]{:S(2)}) collective-permute-start(bf16[288,256]{1,0:T(8,128)(2,1)} %get-tuple-element.29), channel_id=1, source_target_pairs={{0,8},{8,0},{16,24},{24,16},{1,9},{9,1},{17,25},{25,17},{2,10},{10... | collective-permute-start | bytes 442376 | tf_op jit(solution)/shard_map/ppermute | solution.py:364
  13.6 7.3 %collective-permute-start.6 = (bf16[256,128]{1,0:T(8,128)(2,1)}, bf16[256,128]{1,0:T(8,128)(2,1)S(1)}, u32[]{:S(2)}, u32[]{:S(2)}) collective-permute-start(bf16[256,128]{1,0:T(8,128)(2,1)} %get-tuple-element.35), channel_id=1, source_target_pairs={{0,31},{1,24},{2,25},{3,26},{4,27},{5,28},{6,29},{7,30},{8,23},{9,... | collective-permute-start | bytes 196616 | tf_op jit(solution)/shard_map/ppermute | solution.py:372
  14.7 18.5 %copy-start.15 = (bf16[256,128]{1,0:T(8,128)(2,1)}, bf16[256,128]{1,0:T(8,128)(2,1)S(1)}, u32[]{:S(2)}) copy-start(bf16[256,128]{1,0:T(8,128)(2,1)S(1)} %collective-permute-done.3.rest_4_) | copy-start | bytes 196612
  14.7 6.8 %collective-permute-start.14 = (bf16[256,128]{1,0:T(8,128)(2,1)}, bf16[256,128]{1,0:T(8,128)(2,1)S(1)}, u32[]{:S(2)}, u32[]{:S(2)}) collective-permute-start(bf16[256,128]{1,0:T(8,128)(2,1)} %get-tuple-element.44), channel_id=1, source_target_pairs={{0,7},{1,0},{2,1},{3,2},{4,3},{5,4},{6,5},{7,6},{8,15},{9,8},{10,9... | collective-permute-start | bytes 196616 | tf_op jit(solution)/shard_map/ppermute | solution.py:372
  16.0 17.2 %copy-start.16 = (bf16[256,128]{1,0:T(8,128)(2,1)}, bf16[256,128]{1,0:T(8,128)(2,1)S(1)}, u32[]{:S(2)}) copy-start(bf16[256,128]{1,0:T(8,128)(2,1)S(1)} %collective-permute-done.4.rest_5_) | copy-start | bytes 196612
  16.0 14.3 %collective-permute-start.1 = (bf16[288,256]{1,0:T(8,128)(2,1)}, bf16[288,256]{1,0:T(8,128)(2,1)S(1)}, u32[]{:S(2)}, u32[]{:S(2)}) collective-permute-start(bf16[288,256]{1,0:T(8,128)(2,1)} %get-tuple-element.30), channel_id=1, source_target_pairs={{0,16},{8,24},{16,0},{24,8},{1,17},{9,25},{17,1},{25,9},{2,18},{10... | collective-permute-start | bytes 442376 | tf_op jit(solution)/shard_map/ppermute | solution.py:364
  17.5 15.7 %copy-start.18 = (bf16[256,128]{1,0:T(8,128)(2,1)}, bf16[256,128]{1,0:T(8,128)(2,1)S(1)}, u32[]{:S(2)}) copy-start(bf16[256,128]{1,0:T(8,128)(2,1)S(1)} %collective-permute-done.5.rest_6_) | copy-start | bytes 196612
  17.5 14.0 %collective-permute-start.2 = (bf16[288,256]{1,0:T(8,128)(2,1)}, bf16[288,256]{1,0:T(8,128)(2,1)S(1)}, u32[]{:S(2)}, u32[]{:S(2)}) collective-permute-start(bf16[288,256]{1,0:T(8,128)(2,1)} %get-tuple-element.31), channel_id=1, source_target_pairs={{0,24},{8,16},{16,8},{24,0},{1,25},{9,17},{17,9},{25,1},{2,26},{10... | collective-permute-start | bytes 442376 | tf_op jit(solution)/shard_map/ppermute | solution.py:364
  20.9 12.4 %copy-start.20 = (bf16[256,128]{1,0:T(8,128)(2,1)}, bf16[256,128]{1,0:T(8,128)(2,1)S(1)}, u32[]{:S(2)}) copy-start(bf16[256,128]{1,0:T(8,128)(2,1)S(1)} %collective-permute-done.6.rest_7_) | copy-start | bytes 196612
  20.9 21.7 %collective-permute-start.11 = (bf16[288,256]{1,0:T(8,128)(2,1)}, bf16[288,256]{1,0:T(8,128)(2,1)S(1)}, u32[]{:S(2)}, u32[]{:S(2)}) collective-permute-start(bf16[288,256]{1,0:T(8,128)(2,1)} %get-tuple-element.41), channel_id=1, source_target_pairs={{0,8},{8,0},{16,24},{24,16},{1,9},{9,1},{17,25},{25,17},{2,10},{10... | collective-permute-start | bytes 442376 | tf_op jit(solution)/shard_map/ppermute | solution.py:364
  21.5 20.4 %copy-start.14 = (bf16[256,128]{1,0:T(8,128)(2,1)}, bf16[256,128]{1,0:T(8,128)(2,1)S(1)}, u32[]{:S(2)}) copy-start(bf16[256,128]{1,0:T(8,128)(2,1)S(1)} %collective-permute-done.14.rest_4_) | copy-start | bytes 196612
  21.5 7.2 %collective-permute-start.15 = (bf16[256,128]{1,0:T(8,128)(2,1)}, bf16[256,128]{1,0:T(8,128)(2,1)S(1)}, u32[]{:S(2)}, u32[]{:S(2)}) collective-permute-start(bf16[256,128]{1,0:T(8,128)(2,1)} %get-tuple-element.45), channel_id=1, source_target_pairs={{0,15},{1,8},{2,9},{3,10},{4,11},{5,12},{6,13},{7,14},{8,7},{9,0},... | collective-permute-start | bytes 196616 | tf_op jit(solution)/shard_map/ppermute | solution.py:372
  28.7 13.3 %copy-start.17 = (bf16[256,128]{1,0:T(8,128)(2,1)}, bf16[256,128]{1,0:T(8,128)(2,1)S(1)}, u32[]{:S(2)}) copy-start(bf16[256,128]{1,0:T(8,128)(2,1)S(1)} %collective-permute-done.15.rest_5_) | copy-start | bytes 196612
  28.7 13.3 %collective-permute-start.16 = (bf16[256,128]{1,0:T(8,128)(2,1)}, bf16[256,128]{1,0:T(8,128)(2,1)S(1)}, u32[]{:S(2)}, u32[]{:S(2)}) collective-permute-start(bf16[256,128]{1,0:T(8,128)(2,1)} %get-tuple-element.46), channel_id=1, source_target_pairs={{0,23},{1,16},{2,17},{3,18},{4,19},{5,20},{6,21},{7,22},{8,31},{9,... | collective-permute-start | bytes 196616 | tf_op jit(solution)/shard_map/ppermute | solution.py:372
  29.3 3.9 %copy-start.3 = (bf16[288,256]{1,0:T(8,128)(2,1)}, bf16[288,256]{1,0:T(8,128)(2,1)S(1)}, u32[]{:S(2)}) copy-start(bf16[288,256]{1,0:T(8,128)(2,1)S(1)} %collective-permute-done.rest_1_) | copy-start | bytes 442372
  29.3 12.7 %collective-permute-start.17 = (bf16[256,128]{1,0:T(8,128)(2,1)}, bf16[256,128]{1,0:T(8,128)(2,1)S(1)}, u32[]{:S(2)}, u32[]{:S(2)}) collective-permute-start(bf16[256,128]{1,0:T(8,128)(2,1)} %get-tuple-element.47), channel_id=1, source_target_pairs={{0,31},{1,24},{2,25},{3,26},{4,27},{5,28},{6,29},{7,30},{8,23},{9,... | collective-permute-start | bytes 196616 | tf_op jit(solution)/shard_map/ppermute | solution.py:372
  30.3 3.0 %copy-start.7 = (bf16[288,256]{1,0:T(8,128)(2,1)}, bf16[288,256]{1,0:T(8,128)(2,1)S(1)}, u32[]{:S(2)}) copy-start(bf16[288,256]{1,0:T(8,128)(2,1)S(1)} %collective-permute-done.1.rest_2_) | copy-start | bytes 442372
  30.3 13.1 %collective-permute-start.12 = (bf16[288,256]{1,0:T(8,128)(2,1)}, bf16[288,256]{1,0:T(8,128)(2,1)S(1)}, u32[]{:S(2)}, u32[]{:S(2)}) collective-permute-start(bf16[288,256]{1,0:T(8,128)(2,1)} %get-tuple-element.42), channel_id=1, source_target_pairs={{0,16},{8,24},{16,0},{24,8},{1,17},{9,25},{17,1},{25,9},{2,18},{10... | collective-permute-start | bytes 442376 | tf_op jit(solution)/shard_map/ppermute | solution.py:364
  31.5 1.7 %copy-start.9 = (bf16[288,256]{1,0:T(8,128)(2,1)}, bf16[288,256]{1,0:T(8,128)(2,1)S(1)}, u32[]{:S(2)}) copy-start(bf16[288,256]{1,0:T(8,128)(2,1)S(1)} %collective-permute-done.2.rest_3_) | copy-start | bytes 442372
  31.5 14.6 %collective-permute-start.13 = (bf16[288,256]{1,0:T(8,128)(2,1)}, bf16[288,256]{1,0:T(8,128)(2,1)S(1)}, u32[]{:S(2)}, u32[]{:S(2)}) collective-permute-start(bf16[288,256]{1,0:T(8,128)(2,1)} %get-tuple-element.43), channel_id=1, source_target_pairs={{0,24},{8,16},{16,8},{24,0},{1,25},{9,17},{17,9},{25,1},{2,26},{10... | collective-permute-start | bytes 442376 | tf_op jit(solution)/shard_map/ppermute | solution.py:364
  42.0 4.2 %copy-start.19 = (bf16[256,128]{1,0:T(8,128)(2,1)}, bf16[256,128]{1,0:T(8,128)(2,1)S(1)}, u32[]{:S(2)}) copy-start(bf16[256,128]{1,0:T(8,128)(2,1)S(1)} %collective-permute-done.16.rest_6_) | copy-start | bytes 196612
  42.0 13.8 %collective-permute-start.7 = (bf16[288,256]{1,0:T(8,128)(2,1)}, bf16[288,256]{1,0:T(8,128)(2,1)S(1)}, u32[]{:S(2)}, u32[]{:S(2)}) collective-permute-start(bf16[288,256]{1,0:T(8,128)(2,1)} %get-tuple-element.36), channel_id=1, source_target_pairs={{0,7},{1,0},{2,1},{3,2},{4,3},{5,4},{6,5},{7,6},{8,15},{9,8},{10,9... | collective-permute-start | bytes 442376 | tf_op jit(solution)/shard_map/ppermute | solution.py:372
  42.1 4.1 %copy-start.21 = (bf16[256,128]{1,0:T(8,128)(2,1)}, bf16[256,128]{1,0:T(8,128)(2,1)S(1)}, u32[]{:S(2)}) copy-start(bf16[256,128]{1,0:T(8,128)(2,1)S(1)} %collective-permute-done.17.rest_7_) | copy-start | bytes 196612
  42.1 16.1 %collective-permute-start.8 = (bf16[288,256]{1,0:T(8,128)(2,1)}, bf16[288,256]{1,0:T(8,128)(2,1)S(1)}, u32[]{:S(2)}, u32[]{:S(2)}) collective-permute-start(bf16[288,256]{1,0:T(8,128)(2,1)} %get-tuple-element.37), channel_id=1, source_target_pairs={{0,15},{1,8},{2,9},{3,10},{4,11},{5,12},{6,13},{7,14},{8,7},{9,0},... | collective-permute-start | bytes 442376 | tf_op jit(solution)/shard_map/ppermute | solution.py:372
  42.6 3.6 %copy-start = (bf16[288,256]{1,0:T(8,128)(2,1)}, bf16[288,256]{1,0:T(8,128)(2,1)S(1)}, u32[]{:S(2)}) copy-start(bf16[288,256]{1,0:T(8,128)(2,1)S(1)} %collective-permute-done.11.rest_1_) | copy-start | bytes 442372
  42.6 17.0 %collective-permute-start.9 = (bf16[288,256]{1,0:T(8,128)(2,1)}, bf16[288,256]{1,0:T(8,128)(2,1)S(1)}, u32[]{:S(2)}, u32[]{:S(2)}) collective-permute-start(bf16[288,256]{1,0:T(8,128)(2,1)} %get-tuple-element.38), channel_id=1, source_target_pairs={{0,23},{1,16},{2,17},{3,18},{4,19},{5,20},{6,21},{7,22},{8,31},{9,... | collective-permute-start | bytes 442376 | tf_op jit(solution)/shard_map/ppermute | solution.py:372
  43.4 2.7 %copy-start.6 = (bf16[288,256]{1,0:T(8,128)(2,1)}, bf16[288,256]{1,0:T(8,128)(2,1)S(1)}, u32[]{:S(2)}) copy-start(bf16[288,256]{1,0:T(8,128)(2,1)S(1)} %collective-permute-done.12.rest_2_) | copy-start | bytes 442372
  43.4 17.3 %collective-permute-start.10 = (bf16[288,256]{1,0:T(8,128)(2,1)}, bf16[288,256]{1,0:T(8,128)(2,1)S(1)}, u32[]{:S(2)}, u32[]{:S(2)}) collective-permute-start(bf16[288,256]{1,0:T(8,128)(2,1)} %get-tuple-element.39), channel_id=1, source_target_pairs={{0,31},{1,24},{2,25},{3,26},{4,27},{5,28},{6,29},{7,30},{8,23},{9,... | collective-permute-start | bytes 442376 | tf_op jit(solution)/shard_map/ppermute | solution.py:372
  46.1 0.7 copy-start.8
  55.4 5.4 %collective-permute-start.18 = (bf16[288,256]{1,0:T(8,128)(2,1)}, bf16[288,256]{1,0:T(8,128)(2,1)S(1)}, u32[]{:S(2)}, u32[]{:S(2)}) collective-permute-start(bf16[288,256]{1,0:T(8,128)(2,1)} %get-tuple-element.48), channel_id=1, source_target_pairs={{0,7},{1,0},{2,1},{3,2},{4,3},{5,4},{6,5},{7,6},{8,15},{9,8},{10,9... | collective-permute-start | bytes 442376 | tf_op jit(solution)/shard_map/ppermute | solution.py:372
  55.8 11.9 %copy-start.1 = (bf16[288,256]{1,0:T(8,128)(2,1)}, bf16[288,256]{1,0:T(8,128)(2,1)S(1)}, u32[]{:S(2)}) copy-start(bf16[288,256]{1,0:T(8,128)(2,1)S(1)} %collective-permute-done.7.rest_0_) | copy-start | bytes 442372
  55.8 6.4 %collective-permute-start.19 = (bf16[288,256]{1,0:T(8,128)(2,1)}, bf16[288,256]{1,0:T(8,128)(2,1)S(1)}, u32[]{:S(2)}, u32[]{:S(2)}) collective-permute-start(bf16[288,256]{1,0:T(8,128)(2,1)} %get-tuple-element.49), channel_id=1, source_target_pairs={{0,15},{1,8},{2,9},{3,10},{4,11},{5,12},{6,13},{7,14},{8,7},{9,0},... | collective-permute-start | bytes 442376 | tf_op jit(solution)/shard_map/ppermute | solution.py:372
  58.2 9.5 %copy-start.2 = (bf16[288,256]{1,0:T(8,128)(2,1)}, bf16[288,256]{1,0:T(8,128)(2,1)S(1)}, u32[]{:S(2)}) copy-start(bf16[288,256]{1,0:T(8,128)(2,1)S(1)} %collective-permute-done.8.rest_1_) | copy-start | bytes 442372
  58.2 9.5 %collective-permute-start.20 = (bf16[288,256]{1,0:T(8,128)(2,1)}, bf16[288,256]{1,0:T(8,128)(2,1)S(1)}, u32[]{:S(2)}, u32[]{:S(2)}) collective-permute-start(bf16[288,256]{1,0:T(8,128)(2,1)} %get-tuple-element.50), channel_id=1, source_target_pairs={{0,23},{1,16},{2,17},{3,18},{4,19},{5,20},{6,21},{7,22},{8,31},{9,... | collective-permute-start | bytes 442376 | tf_op jit(solution)/shard_map/ppermute | solution.py:372
  59.6 8.2 %copy-start.4 = (bf16[288,256]{1,0:T(8,128)(2,1)}, bf16[288,256]{1,0:T(8,128)(2,1)S(1)}, u32[]{:S(2)}) copy-start(bf16[288,256]{1,0:T(8,128)(2,1)S(1)} %collective-permute-done.9.rest_2_) | copy-start | bytes 442372
  59.6 8.2 %collective-permute-start.21 = (bf16[288,256]{1,0:T(8,128)(2,1)}, bf16[288,256]{1,0:T(8,128)(2,1)S(1)}, u32[]{:S(2)}, u32[]{:S(2)}) collective-permute-start(bf16[288,256]{1,0:T(8,128)(2,1)} %get-tuple-element.51), channel_id=1, source_target_pairs={{0,31},{1,24},{2,25},{3,26},{4,27},{5,28},{6,29},{7,30},{8,23},{9,... | collective-permute-start | bytes 442376 | tf_op jit(solution)/shard_map/ppermute | solution.py:372
  60.8 7.0 %copy-start.5 = (bf16[288,256]{1,0:T(8,128)(2,1)}, bf16[288,256]{1,0:T(8,128)(2,1)S(1)}, u32[]{:S(2)}) copy-start(bf16[288,256]{1,0:T(8,128)(2,1)S(1)} %collective-permute-done.10.rest_3_) | copy-start | bytes 442372
  60.8 7.0 %copy-start.10 = (bf16[288,256]{1,0:T(8,128)(2,1)}, bf16[288,256]{1,0:T(8,128)(2,1)S(1)}, u32[]{:S(2)}) copy-start(bf16[288,256]{1,0:T(8,128)(2,1)S(1)} %collective-permute-done.18.rest_4_) | copy-start | bytes 442372
  62.2 5.6 %copy-start.11 = (bf16[288,256]{1,0:T(8,128)(2,1)}, bf16[288,256]{1,0:T(8,128)(2,1)S(1)}, u32[]{:S(2)}) copy-start(bf16[288,256]{1,0:T(8,128)(2,1)S(1)} %collective-permute-done.19.rest_5_) | copy-start | bytes 442372
  67.7 0.7 copy-start.12
  68.4 0.7 copy-start.13
where the time goes:
time: 73 us; the launch traced here: 72.5 us
  starting transfers between devices  28.9 us (40%)
  Pallas kernels  24.5 us (34%)
  waiting for transfers between devices  14.9 us (20%)
  local copies, waits for them, and re-layouts  2.61 us (4%)
  between operations  1.02 us (1%)
    ppermute x16, starting transfers between devices, across_back(): return lax.ppermute(value, ('ctx', 'pipe'), pairs)  21.9 us
    pallas_call x2, Pallas kernels, attend(): pl.pallas_call(functools.partial(attend_kernel, count, phase), out_shape=...  17.3 us
    ppermute x16, waiting for transfers between devices, across_back(): return lax.ppermute(value, ('ctx', 'pipe'), pairs)  14.9 us
    ppermute x6, starting transfers between devices, across(): return lax.ppermute(value, 'ctx', [(c, c ^ partner) for c in range(count)])  7.02 us
    pallas_call x1, Pallas kernels, pack(): pl.pallas_call(functools.partial(pack_kernel, count), out_shape=[jax.Shap...  3.89 us
    pallas_call x1, Pallas kernels, unpack(): pl.pallas_call(functools.partial(unpack_kernel, count), out_shape=[jax.Sh...  3.32 us
    unnamed x46, local copies, waits for them, and re-layouts  2.61 us
  transfers between devices with their start and end apart: 22, of which 4 were waited for; matrix products, arithmetic and copies ran while one was open for 0% of the time, Pallas kernels for 24%

commit v1 on v0

v1 whole, which is shorter than its diff:
```python
import functools

import jax
import jax.numpy as jnp
from jax import lax
from jax.experimental import pallas as pl
from jax.experimental.pallas import tpu as pltpu
from jax.sharding import PartitionSpec as P

HEADS = 8
F = 16
DV = 128
CONV = 3
TOK = 256
ROWS = TOK + 2 * F
BF16 = jnp.bfloat16
F32 = jnp.float32
UNROLLED = 4
HBM = pl.BlockSpec(memory_space=pltpu.HBM)

ANY = pl.BlockSpec(memory_space=pl.ANY)
SMEM = pl.BlockSpec(memory_space=pltpu.SMEM)
VMEM = pl.BlockSpec(memory_space=pltpu.VMEM)


def params(count):
    return pltpu.CompilerParams(vmem_limit_bytes=(14 if count <= UNROLLED else 44) * 1024 * 1024)


PACK_PARAMS = pltpu.CompilerParams(vmem_limit_bytes=125 * 512 * 1024)


def first_head(place, count):
    return (place * HEADS) // count


def lanes_of(head, width):
    return pl.ds(pl.multiple_of(head * width, width), width)


def phases_of(count):
    return max(1, HEADS // count)


def senders_of(count):
    return range(0, count, max(1, count // HEADS))


def pack_kernel(count, phase, q_ref, k_ref, v_ref, gate_ref, *rest):
    me = lax.axis_index("ctx")
    packed = rest[-4 - count : -4]
    rows, turned, sem, sem_rows = rest[-4:]
    copies = []
    for partner, out in enumerate(packed):
        lanes = lanes_of(first_head(me ^ partner, count) + phase, DV)
        copies.append((v_ref.at[0, :, lanes], out.at[0:TOK, 0:DV]))
        copies.append((gate_ref.at[0, :, lanes], out.at[0:TOK, DV : 2 * DV]))
    copies = [pltpu.make_async_copy(a, b, sem.at[n]) for n, (a, b) in enumerate(copies)]
    loads = [
        pltpu.make_async_copy(ref.at[0], rows.at[side], sem_rows.at[side])
        for side, ref in enumerate((q_ref, k_ref))
    ]
    for copy in loads + copies:
        copy.start()
    for side, copy in enumerate(loads):
        copy.wait()
        turned[side] = rows[side].astype(F32).T.astype(BF16)
    for partner, out in enumerate(packed):
        head = first_head(me ^ partner, count) + phase
        for side in range(2):
            mine = turned[side, lanes_of(head, F)]
            out[TOK + side * F : TOK + (side + 1) * F] = mine
    if phase > 0:
        grad_ref = rest[0]
        for partner, out in enumerate(packed):
            pack_grad(count, phase, me ^ partner, grad_ref, out)
    for copy in copies:
        copy.wait()


def pack_grad(count, phase, place, grad_ref, out):
    mine = grad_ref[0, :, lanes_of(first_head(place, count) + phase, DV)]
    half = TOK // 2
    base = 0 if phase == 0 else ROWS
    out[base : base + half, 0:DV] = mine[0:half]
    out[base : base + half, DV : 2 * DV] = mine[half:TOK]


def pack(count, phase, q_in, k_in, v_in, gate_in, *others):
    rows = ROWS if phase == 0 else ROWS + TOK // 2
    return pl.pallas_call(
        functools.partial(pack_kernel, count, phase),
        out_shape=[jax.ShapeDtypeStruct((rows, 2 * DV), BF16)] * count,
        in_specs=[HBM] * 4 + [VMEM] * min(1, len(others)) + [ANY] * max(0, len(others) - 1),
        out_specs=[VMEM] * count,
        scratch_shapes=[
            pltpu.VMEM((2, TOK, HEADS * F), BF16),
            pltpu.VMEM((2, HEADS * F, TOK), BF16),
            pltpu.SemaphoreType.DMA((2 * count,)),
            pltpu.SemaphoreType.DMA((2,)),
        ],
        compiler_params=PACK_PARAMS if phase == 0 else params(count),
    )(q_in, k_in, v_in, gate_in, *others)


def pack_grads_kernel(count, grad_ref, *outs):
    me = lax.axis_index("ctx")
    for partner, out in enumerate(outs):
        pack_grad(count, 0, me ^ partner, grad_ref, out)


def pack_grads(count, grad):
    return pl.pallas_call(
        functools.partial(pack_grads_kernel, count),
        out_shape=[jax.ShapeDtypeStruct((TOK // 2, 2 * DV), BF16)] * count,
        in_specs=[VMEM],
        out_specs=[VMEM] * count,
        compiler_params=params(count),
    )(grad)


def nn(a, b):
    return lax.dot_general(a, b, (((1,), (0,)), ((), ())), preferred_element_type=F32)


def nt(a, b):
    return lax.dot_general(a, b, (((1,), (1,)), ((), ())), preferred_element_type=F32)


def halves(x):
    high = x.astype(BF16)
    return high, (x - high.astype(F32)).astype(BF16)


def iota(shape, dim):
    return lax.broadcasted_iota(jnp.int32, shape, dim)


def each(low, high, body):
    if isinstance(low, int) and isinstance(high, int) and high - low <= UNROLLED:
        for step in range(low, high):
            body(step)
    else:

        def one(step, carry):
            body(step)
            return carry

        lax.fori_loop(low, high, one, 0)


def attend_kernel(count, phase, bounds, taps_ref, *rest):
    senders = senders_of(count)
    packed, rest = rest[:count], rest[count:]
    grads, base = packed, ROWS
    if phase == 0:
        grads, base, rest = rest[:count], 0, rest[count:]
    outs = rest[: len(senders)]
    (block, grad, gates, mixed_grads, high_s, low_s, base_s, num_s, dq_s, dk_s, dv_s,
    ) = rest[len(senders) :]
    me = lax.axis_index("ctx")
    for partner in range(count):
        block[me ^ partner] = packed[partner][0:ROWS]
        for half in range(2):
            grad[me ^ partner, half * TOK // 2 : (half + 1) * TOK // 2] = grads[partner][
                base : base + TOK // 2, half * DV : (half + 1) * DV
            ]
    head = first_head(me, count) + phase
    taps = taps_ref[0, :, pl.ds(pl.multiple_of(head * DV, DV), DV)].astype(F32)
    gates[0:8] = jnp.zeros((8, DV), F32)
    mixed_grads[:, count * TOK : count * TOK + 8] = jnp.zeros((CONV, 8, DV), F32)

    def spread(j):
        gates[pl.ds(8 + j * TOK, TOK)] = block[j, 0:TOK, DV : 2 * DV].astype(F32)

    each(0, count, spread)

    def opening(i):
        bound = bounds[0, i]
        return jnp.where(bound < TOK, i * TOK + bound, 0)

    def earlier(i):
        if isinstance(i, int):
            last = jnp.int32(0)
            for j in range(i):
                last = jnp.maximum(last, opening(j))
            return last
        return lax.fori_loop(0, i, lambda j, last: jnp.maximum(last, opening(j)), jnp.int32(0))

    def values(j, wide):
        return block[pl.ds(j, wide), 0:TOK, 0:DV].reshape(wide * TOK, DV)

    def keys(j, wide):
        parts = [block[j + step, TOK + F : TOK + 2 * F] for step in range(wide)]
        return parts[0] if wide == 1 else jnp.concatenate(parts, axis=1)

    def spans(i, body):
        if isinstance(i, int):
            if i > 0:
                body(0, i)
        else:
            each(0, i, lambda j: body(j, 1))

    def row_block(i):
        bound = bounds[0, i]
        before = earlier(i)
        row, col = iota((TOK, TOK), 0), iota((TOK, TOK), 1)
        same = (col <= row) & ((col >= bound) | (row < bound))
        query_t = block[i, TOK : TOK + F] * BF16(0.25)
        query = query_t.astype(F32).T.astype(BF16)

        def kernel_of(j, wide):
            base = 1.0 + nn(query, keys(j, wide))
            return base, 0.5 * base * base + 0.5

        def weigh(high, low, value):
            value = jnp.concatenate([value, jnp.ones_like(value)], axis=1)
            return nn(high, value) + nn(low, value)

        own_base, own_kern = kernel_of(i, 1)
        own_high, own_low = halves(jnp.where(same, own_kern, 0.0))
        own = weigh(own_high, own_low, values(i, 1))
        num_s[i] = jnp.zeros((TOK, 2 * DV), F32)
        room = (i * (i - 1)) // 2 * TOK if isinstance(i, int) else 0

        def forward(j, wide):
            width = wide * TOK
            base, kern = kernel_of(j, wide)
            high, low = halves(kern)
            lanes = pl.ds(room + j * TOK, width)
            base_s[:, lanes] = base
            high_s[:, lanes] = high
            low_s[:, lanes] = low
            value = values(j, wide)
            allowed = iota((width, DV), 0) + j * TOK >= before
            ones = jnp.where(allowed, 1.0, 0.0).astype(BF16)
            value = jnp.concatenate([value * ones, ones], axis=1)
            num_s[i] += nn(high, value) + nn(low, value)

        spans(i, forward)
        yield
        old = iota((TOK, 2 * DV), 0) < bound
        total = own + jnp.where(old, num_s[i], 0.0)
        num, den = total[:, 0:DV], total[:, DV:]

        position = iota((TOK, DV), 0) + i * TOK
        depth = position - jnp.where(iota((TOK, DV), 0) >= bound, opening(i), before)
        mixed = taps[0:1] * gates[pl.ds(8 + i * TOK, TOK)]
        for shift in range(1, CONV):
            moved = gates[pl.ds(8 - shift + i * TOK, TOK)]
            mixed += jnp.where(depth >= shift, taps[shift : shift + 1] * moved, 0.0)
        incoming = grad[i].astype(F32)
        gate = 1.0 / (1.0 + jnp.exp(-mixed))
        scale = 1.0 / den
        attended = num * scale
        d_num = incoming * mixed * gate * scale
        d_den = -jnp.sum(d_num * attended, axis=1, keepdims=True)
        mixed_grad = incoming * attended * gate * (1.0 + mixed * (1.0 - gate))
        mixed_grads[0, pl.ds(i * TOK, TOK)] = mixed_grad
        for shift in range(1, CONV):
            mixed_grads[shift, pl.ds(i * TOK, TOK)] = jnp.where(depth >= shift, mixed_grad, 0.0)

        d_pair = jnp.concatenate(halves(d_num), axis=1)
        d_pair_t = jnp.concatenate(halves(d_num.T), axis=0)

        def slopes(d_pair, d_den, base, value):
            return (nt(d_pair, jnp.concatenate([value, value], axis=1)) + d_den) * base

        slope = slopes(d_pair, d_den, own_base, values(i, 1))
        s_high, s_low = halves(jnp.where(same, slope, 0.0))
        key = keys(i, 1)
        lanes = pl.ds(i * TOK, TOK)
        dv_s[:, lanes] = nn(d_pair_t, own_high) + nn(d_pair_t, own_low)
        dk_s[:, lanes] = nn(query_t, s_high) + nn(query_t, s_low)
        dq_s[i] = nt(key, s_high) + nt(key, s_low)

        def backward(j, wide):
            width = wide * TOK
            lanes = pl.ds(j * TOK, width)
            lane_old = jnp.where(iota((2 * DV, TOK), 1) < bound, 1.0, 0.0).astype(BF16)
            row_old = jnp.where(old, 1.0, 0.0).astype(BF16)
            pair, pair_t = d_pair * row_old, d_pair_t * lane_old
            den = jnp.where(iota((TOK, 1), 0) < bound, d_den, 0.0)
            saved = pl.ds(room + j * TOK, width)
            s_high, s_low = halves(slopes(pair, den, base_s[:, saved], values(j, wide)))
            allowed = iota((1, width), 1) + j * TOK >= before
            keep = jnp.where(allowed, 1.0, 0.0)
            key = keys(j, wide) * keep.astype(BF16)
            dv_s[:, lanes] += keep * (nn(pair_t, high_s[:, saved]) + nn(pair_t, low_s[:, saved]))
            dk_s[:, lanes] += keep * (nn(query_t, s_high) + nn(query_t, s_low))
            dq_s[i] += nt(key, s_high) + nt(key, s_low)

        spans(i, backward)
        yield

    if count <= UNROLLED:
        rows = [row_block(i) for i in range(count)]
        for _ in range(2):
            for row in rows:
                next(row)
    else:
        each(0, count, lambda i: list(row_block(i)))

    for partner, out in zip(senders, outs):
        j = me ^ partner
        lanes = pl.ds(pl.multiple_of(j * TOK, TOK), TOK)
        total = dv_s[0:DV, lanes] + dv_s[DV : 2 * DV, lanes]
        out[0:TOK, 0:DV] = total.T.astype(BF16)
        back = taps[0:1] * mixed_grads[0, pl.ds(pl.multiple_of(j * TOK, TOK), TOK)]
        for shift in range(1, CONV):
            window = mixed_grads[shift, pl.ds(pl.multiple_of(j * TOK, TOK), TOK + 8)]
            back += taps[shift : shift + 1] * window[shift : shift + TOK]
        out[0:TOK, DV : 2 * DV] = back.astype(BF16)
        out[TOK : TOK + F] = (0.25 * dq_s[j]).astype(BF16)
        out[TOK + F : TOK + 2 * F] = dk_s[:, lanes].astype(BF16)


def attend(count, phase, bounds, taps, packed, grads):
    outs = len(senders_of(count))
    saved = (count * (count - 1) // 2 if count <= UNROLLED else count - 1) * TOK
    return pl.pallas_call(
        functools.partial(attend_kernel, count, phase),
        out_shape=[jax.ShapeDtypeStruct((ROWS, 2 * DV), BF16)] * outs,
        in_specs=[SMEM, VMEM] + [VMEM] * (len(packed) + len(grads)),
        out_specs=[VMEM] * outs,
        scratch_shapes=[
            pltpu.VMEM((count, ROWS, 2 * DV), BF16),
            pltpu.VMEM((count, TOK, DV), BF16),
            pltpu.VMEM((count * TOK + 8, DV), F32),
            pltpu.VMEM((CONV, count * TOK + 8, DV), F32),
            pltpu.VMEM((TOK, saved), BF16),
            pltpu.VMEM((TOK, saved), BF16),
            pltpu.VMEM((TOK, saved), F32),
            pltpu.VMEM((count, TOK, 2 * DV), F32),
            pltpu.VMEM((count, F, TOK), F32),
            pltpu.VMEM((F, count * TOK), F32),
            pltpu.VMEM((2 * DV, count * TOK), F32),
        ],
        compiler_params=params(count),
    )(bounds, taps, *packed, *grads)


def unpack_kernel(count, phase, *rest):
    senders = senders_of(count)
    many = len(senders)
    me = lax.axis_index("ctx")
    last = phase == phases_of(count) - 1
    arrived, rest = rest[:many], rest[many:]
    earlier = None
    if phase > 0:
        earlier, rest = rest[0], rest[3:]
    v_ref, gate_ref = rest[:2]
    sem = rest[-1]
    rows_ref = rest[-2] if last else rest[2]
    copies = []
    for n, partner in enumerate(senders):
        head = first_head(me ^ partner, count) + phase
        lanes = pl.ds(pl.multiple_of(head * DV, DV), DV)
        copies.append((arrived[n].at[0:TOK, 0:DV], v_ref.at[0, :, lanes]))
        copies.append((arrived[n].at[0:TOK, DV : 2 * DV], gate_ref.at[0, :, lanes]))
    copies = [pltpu.make_async_copy(a, b, sem.at[n]) for n, (a, b) in enumerate(copies)]
    for copy in copies:
        copy.start()
    if earlier is not None:
        rows_ref[...] = earlier[...]
    for n, partner in enumerate(senders):
        head = first_head(me ^ partner, count) + phase
        rows = pl.ds(pl.multiple_of(head * F, F), F)
        for side in range(2):
            rows_ref[side, rows] = arrived[n][TOK + side * F : TOK + (side + 1) * F]
    if last:
        for side, ref in enumerate(rest[2:4]):
            ref[0] = rows_ref[side].astype(F32).T.astype(BF16)
    for copy in copies:
        copy.wait()


def unpack(count, phase, arrived, begun):
    wide = jax.ShapeDtypeStruct((1, TOK, HEADS * DV), BF16)
    narrow = jax.ShapeDtypeStruct((1, TOK, HEADS * F), BF16)
    turned = (2, HEADS * F, TOK)
    last = phase == phases_of(count) - 1
    many = len(arrived)
    small = [narrow, narrow] if last else [jax.ShapeDtypeStruct(turned, BF16)]
    return pl.pallas_call(
        functools.partial(unpack_kernel, count, phase),
        out_shape=[wide, wide] + small,
        in_specs=[VMEM] * many + [VMEM, HBM, HBM][: len(begun)],
        out_specs=[HBM, HBM] + [VMEM] * len(small),
        input_output_aliases={many + 1: 0, many + 2: 1} if begun else {},
        scratch_shapes=([pltpu.VMEM(turned, BF16)] if last else [])
        + [pltpu.SemaphoreType.DMA((2 * many,))],
        compiler_params=params(count),
    )(*arrived, *begun)


def on_device(count, sections, q_in, k_in, v_in, gate_in, out_grad, conv_weight, bounds):
    phases, senders = phases_of(count), senders_of(count)

    def across(value, partner):
        if partner == 0:
            return value
        return lax.ppermute(value, "ctx", [(c, c ^ partner) for c in range(count)])

    def across_back(value, partner):
        pairs = [
            (c * sections + s, (c ^ partner) * sections + (s - 1) % sections)
            for c in range(count)
            for s in range(sections)
        ]
        return lax.ppermute(value, ("ctx", "pipe"), pairs)

    order = sorted(range(count), key=lambda partner: -bin(partner).count("1"))
    shift = [(s, (s - 1) % sections) for s in range(sections)]
    cotangent = lax.ppermute(out_grad, "pipe", shift)

    def spread(packed):
        moved = {partner: across(packed[partner], partner) for partner in order}
        return [moved[partner] for partner in range(count)]

    inputs = (q_in, k_in, v_in, gate_in)
    blocks = [spread(pack(count, 0, *inputs))]
    own_grads = pack_grads(count, cotangent)
    grads = spread(own_grads)
    for phase in range(1, phases):
        before = blocks[phase - 1][order[-2]], own_grads[0]
        blocks.append(spread(pack(count, phase, *inputs, cotangent, *before)))
    arrived = []
    for phase in range(phases):
        results = attend(count, phase, bounds, conv_weight, blocks[phase], grads)
        grads = []
        results = dict(zip(senders, results))
        moved = {p: across_back(results[p], p) for p in order if p in results}
        arrived.append([moved[partner] for partner in senders])
    begun = ()
    for phase in range(phases):
        out = unpack(count, phase, arrived[phase], begun)
        begun = (out[2], out[0], out[1])
    v_grad, gate_grad, q_grad, k_grad = out
    return q_grad, k_grad, v_grad, gate_grad


def solution(mesh):
    count, sections = mesh.shape["ctx"], mesh.shape["pipe"]
    split = P("pipe", "ctx", None)
    in_specs = (split,) * 5 + (P("pipe", None, None), P("pipe", None))
    return jax.shard_map(
        functools.partial(on_device, count, sections),
        mesh=mesh,
        in_specs=in_specs,
        out_specs=(split,) * 4,
        check_vma=False,
    )
```

time: 73 us -> 53.9 us (0.74)
  Pallas kernels: 24.5 us -> 16.4 us
  starting transfers between devices: 28.9 us -> 24.6 us
  waiting for transfers between devices: 14.9 us -> 11.9 us
  local copies, waits for them, and re-layouts: 2.61 us -> 0.03 us
    ppermute x16 -> x8, starting transfers between devices: 21.9 us -> 9.41 us  [across_back(): return lax.ppermute(value, ('ctx', 'pipe'), pairs)]
    ppermute x16 -> x8, waiting for transfers between devices: 14.9 us -> 5.33 us  [across_back(): return lax.ppermute(value, ('ctx', 'pipe'), pairs)]
    pallas_call x2, Pallas kernels: 17.3 us -> 11.1 us  [attend(): pl.pallas_call(functools.partial(attend_kernel, count, phase), out_shape=...]
    ppermute x6 -> x9, waiting for transfers between devices: 0.02 us -> 5.32 us  [across(): return lax.ppermute(value, 'ctx', [(c, c ^ partner) for c in range(count)])]
    ppermute x0 -> x1, starting transfers between devices: none -> 4.54 us  [on_device(): cotangent = lax.ppermute(out_grad, 'pipe', shift)]
    ppermute x6 -> x9, starting transfers between devices: 7.02 us -> 10.7 us  [across(): return lax.ppermute(value, 'ctx', [(c, c ^ partner) for c in range(count)])]
    unnamed x46 -> x14, local copies, waits for them, and re-layouts: 2.61 us -> 0.03 us
    pallas_call x2 -> x5, Pallas kernels: 7.21 us -> 5.35 us  [the longest x2 2.9 us: pack(): pl.pallas_call(functools.partial(pack_kernel, count, phase), out_shape=[j...]
  transfers between devices with their start and end apart: 22 -> 18, of which waited for: 4 -> 6; matrix products, arithmetic and copies ran while one was open for 0% -> 0% of each run, Pallas kernels for 24% -> 28%
where the time goes in v1:
time: 53.9 us; the launch traced here: 53.8 us
  starting transfers between devices  24.6 us (46%)
  Pallas kernels  16.4 us (30%)
  waiting for transfers between devices  11.9 us (22%)
  between operations  0.74 us (1%)
    pallas_call x2, Pallas kernels, attend(): pl.pallas_call(functools.partial(attend_kernel, count, phase), out_shape=...  11.1 us
    ppermute x9, starting transfers between devices, across(): return lax.ppermute(value, 'ctx', [(c, c ^ partner) for c in range(count)])  10.7 us
    ppermute x8, starting transfers between devices, across_back(): return lax.ppermute(value, ('ctx', 'pipe'), pairs)  9.41 us
    ppermute x8, waiting for transfers between devices, across_back(): return lax.ppermute(value, ('ctx', 'pipe'), pairs)  5.33 us
    ppermute x9, waiting for transfers between devices, across(): return lax.ppermute(value, 'ctx', [(c, c ^ partner) for c in range(count)])  5.32 us
    ppermute x1, starting transfers between devices, on_device(): cotangent = lax.ppermute(out_grad, 'pipe', shift)  4.54 us
    pallas_call x2, Pallas kernels, pack(): pl.pallas_call(functools.partial(pack_kernel, count, phase), out_shape=[j...  2.9 us
    pallas_call x2, Pallas kernels, unpack(): pl.pallas_call(functools.partial(unpack_kernel, count, phase), out_shape=...  2.38 us
  transfers between devices with their start and end apart: 18, of which 6 were waited for; matrix products, arithmetic and copies ran while one was open for 0% of the time, Pallas kernels for 28%

profile of v1, /device:TPU:0, one launch (start us, length us, event | category | flops | bytes accessed | tf_op | source)
XLA Modules:
  0.0 53.8 jit_solution(15240277735078819195)
XLA Ops:
  0.6 4.5 %collective-permute-start = (bf16[1,256,1024]{2,1,0:T(8,128)(2,1)}, bf16[1,256,1024]{2,1,0:T(8,128)(2,1)S(1)}, u32[]{:S(2)}, u32[]{:S(2)}) collective-permute-start(bf16[1,256,1024]{2,1,0:T(8,128)(2,1)} %param.11), channel_id=1, source_target_pairs={{0,7},{1,0},{2,1},{3,2},{4,3},{5,4},{6,5},{7,6},{8,15},{9,8},{10,9... | collective-permute-start | bytes 1572872 | tf_op jit(solution)/shard_map/ppermute | solution.py:415
  5.2 2.2 %shard_map.102 = (bf16[288,256]{1,0:T(8,128)(2,1)}, bf16[288,256]{1,0:T(8,128)(2,1)}, bf16[288,256]{1,0:T(8,128)(2,1)}, bf16[288,256]{1,0:T(8,128)(2,1)}) custom-call(bf16[1,256,128]{2,1,0:T(8,128)(2,1)} %q_ref.3, bf16[1,256,128]{2,1,0:T(8,128)(2,1)} %k_ref.3, bf16[1,256,1024]{2,1,0:T(8,128)(2,1)} %v_ref.3, bf16[1,256,1024]{2,1,0:T(8,128)(2,1)} %gate_ref.3), custom_call_target="tpu_custom_call" | custom-call | tf_op jit(solution)/shard_map/pallas_call | solution.py:91
  7.3 0.0 copy-start
  7.4 1.6 %collective-permute-start.1 = (bf16[288,256]{1,0:T(8,128)(2,1)}, bf16[288,256]{1,0:T(8,128)(2,1)S(1)}, u32[]{:S(2)}, u32[]{:S(2)}) collective-permute-start(bf16[288,256]{1,0:T(8,128)(2,1)} %get-tuple-element.31), channel_id=1, source_target_pairs={{0,16},{8,24},{16,0},{24,8},{1,17},{9,25},{17,1},{25,9},{2,18},{10... | collective-permute-start | bytes 442376 | tf_op jit(solution)/shard_map/ppermute | solution.py:403
  8.9 1.5 %collective-permute-start.9 = (bf16[288,256]{1,0:T(8,128)(2,1)}, bf16[288,256]{1,0:T(8,128)(2,1)S(1)}, u32[]{:S(2)}, u32[]{:S(2)}) collective-permute-start(bf16[288,256]{1,0:T(8,128)(2,1)} %get-tuple-element.42), channel_id=1, source_target_pairs={{0,8},{8,0},{16,24},{24,16},{1,9},{9,1},{17,25},{25,17},{2,10},{10... | collective-permute-start | bytes 442376 | tf_op jit(solution)/shard_map/ppermute | solution.py:403
  10.4 0.5 collective-permute-start.10
  10.9 1.3 %collective-permute-done.grad_ref.rest_0_ = bf16[1,256,1024]{2,1,0:T(8,128)(2,1)S(1)} collective-permute-done((bf16[1,256,1024]{2,1,0:T(8,128)(2,1)}, bf16[1,256,1024]{2,1,0:T(8,128)(2,1)S(1)}, u32[]{:S(2)}, u32[]{:S(2)}) %collective-permute-start) | collective-permute-done | bytes 524320 | tf_op jit(solution)/shard_map/ppermute | solution.py:415
  12.2 0.1 shard_map.103
  12.3 1.9 %collective-permute-done.1.rest_1_.rest_2_ = bf16[288,256]{1,0:T(8,128)(2,1)S(1)} collective-permute-done((bf16[288,256]{1,0:T(8,128)(2,1)}, bf16[288,256]{1,0:T(8,128)(2,1)S(1)}, u32[]{:S(2)}, u32[]{:S(2)}) %collective-permute-start.1) | collective-permute-done | bytes 147488 | tf_op jit(solution)/shard_map/ppermute | solution.py:403
  14.2 0.0 copy-done.1
  14.2 0.0 copy-done.3
  14.2 0.0 copy-start.4
  14.2 0.7 %shard_map.104 = (bf16[416,256]{1,0:T(8,128)(2,1)S(1)}, bf16[416,256]{1,0:T(8,128)(2,1)S(1)}, bf16[416,256]{1,0:T(8,128)(2,1)S(1)}, bf16[416,256]{1,0:T(8,128)(2,1)S(1)}) custom-call(bf16[1,256,128]{2,1,0:T(8,128)(2,1)S(1)} %copy-done.2, bf16[1,256,128]{2,1,0:T(8,128)(2,1)S(1)} %copy-done.3, bf16[1,256,1024]{2,1,0:T(8,128)(2,1)S(1)} %copy-done, ...), custom_call_target="tpu_custom_call" | custom-call | tf_op jit(solution)/shard_map/pallas_call | solution.py:91
  15.0 0.0 copy-start.5
  15.0 1.0 %collective-permute-start.2 = (bf16[416,256]{1,0:T(8,128)(2,1)S(1)}, bf16[416,256]{1,0:T(8,128)(2,1)S(1)}, u32[]{:S(2)}, u32[]{:S(2)}) collective-permute-start(bf16[416,256]{1,0:T(8,128)(2,1)S(1)} %get-tuple-element.34), channel_id=1, source_target_pairs={{0,8},{8,0},{16,24},{24,16},{1,9},{9,1},{17,25},{25,17},{2,10},{10... | collective-permute-start | bytes 638984 | tf_op jit(solution)/shard_map/ppermute | solution.py:403
  16.0 1.1 %collective-permute-start.11 = (bf16[128,256]{1,0:T(8,128)(2,1)S(1)}, bf16[128,256]{1,0:T(8,128)(2,1)S(1)}, u32[]{:S(2)}, u32[]{:S(2)}) collective-permute-start(bf16[128,256]{1,0:T(8,128)(2,1)S(1)} %get-tuple-element.44), channel_id=1, source_target_pairs={{0,8},{8,0},{16,24},{24,16},{1,9},{9,1},{17,25},{25,17},{2,10},{10... | collective-permute-start | bytes 196616 | tf_op jit(solution)/shard_map/ppermute | solution.py:403
  17.1 0.9 %collective-permute-start.12 = (bf16[128,256]{1,0:T(8,128)(2,1)S(1)}, bf16[128,256]{1,0:T(8,128)(2,1)S(1)}, u32[]{:S(2)}, u32[]{:S(2)}) collective-permute-start(bf16[128,256]{1,0:T(8,128)(2,1)S(1)} %get-tuple-element.45), channel_id=1, source_target_pairs={{0,16},{8,24},{16,0},{24,8},{1,17},{9,25},{17,1},{25,9},{2,18},{10... | collective-permute-start | bytes 196616 | tf_op jit(solution)/shard_map/ppermute | solution.py:403
  18.0 0.0 collective-permute-done.9.rest_1_
  18.0 1.4 %collective-permute-start.13 = (bf16[128,256]{1,0:T(8,128)(2,1)S(1)}, bf16[128,256]{1,0:T(8,128)(2,1)S(1)}, u32[]{:S(2)}, u32[]{:S(2)}) collective-permute-start(bf16[128,256]{1,0:T(8,128)(2,1)S(1)} %get-tuple-element.46), channel_id=1, source_target_pairs={{0,24},{8,16},{16,8},{24,0},{1,25},{9,17},{17,9},{25,1},{2,26},{10... | collective-permute-start | bytes 196616 | tf_op jit(solution)/shard_map/ppermute | solution.py:403
  19.5 0.0 collective-permute-done.10.rest_3_
  19.5 1.5 %collective-permute-start.3 = (bf16[416,256]{1,0:T(8,128)(2,1)S(1)}, bf16[416,256]{1,0:T(8,128)(2,1)S(1)}, u32[]{:S(2)}, u32[]{:S(2)}) collective-permute-start(bf16[416,256]{1,0:T(8,128)(2,1)S(1)} %get-tuple-element.35), channel_id=1, source_target_pairs={{0,16},{8,24},{16,0},{24,8},{1,17},{9,25},{17,1},{25,9},{2,18},{10... | collective-permute-start | bytes 638984 | tf_op jit(solution)/shard_map/ppermute | solution.py:403
  21.0 1.8 %collective-permute-done.11.rest_5_ = bf16[128,256]{1,0:T(8,128)(2,1)S(1)} collective-permute-done((bf16[128,256]{1,0:T(8,128)(2,1)S(1)}, bf16[128,256]{1,0:T(8,128)(2,1)S(1)}, u32[]{:S(2)}, u32[]{:S(2)}) %collective-permute-start.11) | collective-permute-done | bytes 65568 | tf_op jit(solution)/shard_map/ppermute | solution.py:403
  22.8 1.2 %collective-permute-start.4 = (bf16[416,256]{1,0:T(8,128)(2,1)S(1)}, bf16[416,256]{1,0:T(8,128)(2,1)S(1)}, u32[]{:S(2)}, u32[]{:S(2)}) collective-permute-start(bf16[416,256]{1,0:T(8,128)(2,1)S(1)} %get-tuple-element.36), channel_id=1, source_target_pairs={{0,24},{8,16},{16,8},{24,0},{1,25},{9,17},{17,9},{25,1},{2,26},{10... | collective-permute-start | bytes 638984 | tf_op jit(solution)/shard_map/ppermute | solution.py:403
  24.0 0.0 collective-permute-done.12.rest_6_
  24.0 1.5 %collective-permute-done.13.rest_7_ = bf16[128,256]{1,0:T(8,128)(2,1)S(1)} collective-permute-done((bf16[128,256]{1,0:T(8,128)(2,1)S(1)}, bf16[128,256]{1,0:T(8,128)(2,1)S(1)}, u32[]{:S(2)}, u32[]{:S(2)}) %collective-permute-start.13) | collective-permute-done | bytes 65568 | tf_op jit(solution)/shard_map/ppermute | solution.py:403
  25.5 5.5 %shard_map.106 = (bf16[288,256]{1,0:T(8,128)(2,1)S(1)}, bf16[288,256]{1,0:T(8,128)(2,1)S(1)}, bf16[288,256]{1,0:T(8,128)(2,1)S(1)}, bf16[288,256]{1,0:T(8,128)(2,1)S(1)}) custom-call(s32[1,4]{1,0:T(1,128)S(1)} %copy-done.6, bf16[1,3,1024]{2,1,0:T(4,128)(2,1)S(1)} %copy-done.5, bf16[288,256]{1,0:T(8,128)(2,1)S(1)} %copy-done.4, ...), custom_call_target="tpu_custom_call" | custom-call | tf_op jit(solution)/shard_map/pallas_call | solution.py:321
  31.1 2.0 %collective-permute-start.14 = (bf16[288,256]{1,0:T(8,128)(2,1)S(1)}, bf16[288,256]{1,0:T(8,128)(2,1)S(1)}, u32[]{:S(2)}, u32[]{:S(2)}) collective-permute-start(bf16[288,256]{1,0:T(8,128)(2,1)S(1)} %get-tuple-element.47), channel_id=1, source_target_pairs={{0,7},{1,0},{2,1},{3,2},{4,3},{5,4},{6,5},{7,6},{8,15},{9,8},{10,9... | collective-permute-start | bytes 442376 | tf_op jit(solution)/shard_map/ppermute | solution.py:411
  33.1 0.3 collective-permute-start.15
  33.3 0.0 collective-permute-done.2.rest_1_
  33.3 0.3 collective-permute-start.16
  33.7 0.0 collective-permute-done.3.rest_2_
  33.7 1.8 %collective-permute-start.17 = (bf16[288,256]{1,0:T(8,128)(2,1)S(1)}, bf16[288,256]{1,0:T(8,128)(2,1)S(1)}, u32[]{:S(2)}, u32[]{:S(2)}) collective-permute-start(bf16[288,256]{1,0:T(8,128)(2,1)S(1)} %get-tuple-element.50), channel_id=1, source_target_pairs={{0,31},{1,24},{2,25},{3,26},{4,27},{5,28},{6,29},{7,30},{8,23},{9,... | collective-permute-start | bytes 442376 | tf_op jit(solution)/shard_map/ppermute | solution.py:411
  35.5 0.0 collective-permute-done.4.rest_3_
  35.5 5.5 %shard_map.105 = (bf16[288,256]{1,0:T(8,128)(2,1)S(1)}, bf16[288,256]{1,0:T(8,128)(2,1)S(1)}, bf16[288,256]{1,0:T(8,128)(2,1)S(1)}, bf16[288,256]{1,0:T(8,128)(2,1)S(1)}) custom-call(s32[1,4]{1,0:T(1,128)S(1)} %copy-done.6, bf16[1,3,1024]{2,1,0:T(4,128)(2,1)S(1)} %copy-done.5, bf16[416,256]{1,0:T(8,128)(2,1)S(1)} %get-tuple-element.33.rest_0_, ...), custom_call_target="tpu_custom_call" | custom-call | tf_op jit(solution)/shard_map/pallas_call | solution.py:321
  41.0 0.3 collective-permute-start.5
  41.3 0.0 collective-permute-done.14.rest_0_
  41.3 0.8 %collective-permute-start.6 = (bf16[288,256]{1,0:T(8,128)(2,1)S(1)}, bf16[288,256]{1,0:T(8,128)(2,1)S(1)}, u32[]{:S(2)}, u32[]{:S(2)}) collective-permute-start(bf16[288,256]{1,0:T(8,128)(2,1)S(1)} %get-tuple-element.38), channel_id=1, source_target_pairs={{0,15},{1,8},{2,9},{3,10},{4,11},{5,12},{6,13},{7,14},{8,7},{9,0},... | collective-permute-start | bytes 442376 | tf_op jit(solution)/shard_map/ppermute | solution.py:411
  42.1 0.0 collective-permute-done.15.rest_1_
  42.1 0.9 %collective-permute-start.7 = (bf16[288,256]{1,0:T(8,128)(2,1)S(1)}, bf16[288,256]{1,0:T(8,128)(2,1)S(1)}, u32[]{:S(2)}, u32[]{:S(2)}) collective-permute-start(bf16[288,256]{1,0:T(8,128)(2,1)S(1)} %get-tuple-element.39), channel_id=1, source_target_pairs={{0,23},{1,16},{2,17},{3,18},{4,19},{5,20},{6,21},{7,22},{8,31},{9,... | collective-permute-start | bytes 442376 | tf_op jit(solution)/shard_map/ppermute | solution.py:411
  43.0 0.0 collective-permute-done.16.rest_2_
  43.0 3.1 %collective-permute-start.8 = (bf16[288,256]{1,0:T(8,128)(2,1)S(1)}, bf16[288,256]{1,0:T(8,128)(2,1)S(1)}, u32[]{:S(2)}, u32[]{:S(2)}) collective-permute-start(bf16[288,256]{1,0:T(8,128)(2,1)S(1)} %get-tuple-element.40), channel_id=1, source_target_pairs={{0,31},{1,24},{2,25},{3,26},{4,27},{5,28},{6,29},{7,30},{8,23},{9,... | collective-permute-start | bytes 442376 | tf_op jit(solution)/shard_map/ppermute | solution.py:411
  46.1 0.0 collective-permute-done.17.rest_3_
  46.1 0.8 %shard_map.107 = (bf16[1,256,1024]{2,1,0:T(8,128)(2,1)}, bf16[1,256,1024]{2,1,0:T(8,128)(2,1)}, bf16[2,128,256]{2,1,0:T(8,128)(2,1)S(1)}) custom-call(bf16[288,256]{1,0:T(8,128)(2,1)S(1)} %collective-permute-done.14.rest_0_, bf16[288,256]{1,0:T(8,128)(2,1)S(1)} %collective-permute-done.15.rest_1_, bf16[288,256]{1,0:T(8,128)(2,1)S(1)} %collective-permute-done.16.rest_2_, ...), custom_call_target="tpu_custom_call" | custom-call | tf_op jit(solution)/shard_map/pallas_call | solution.py:385
  46.9 0.0 collective-permute-done.5.rest_0_
  46.9 0.0 collective-permute-done.6.rest_1_
  46.9 0.2 collective-permute-done.7.rest_2_
  47.1 5.1 %collective-permute-done.8.rest_3_ = bf16[288,256]{1,0:T(8,128)(2,1)S(1)} collective-permute-done((bf16[288,256]{1,0:T(8,128)(2,1)S(1)}, bf16[288,256]{1,0:T(8,128)(2,1)S(1)}, u32[]{:S(2)}, u32[]{:S(2)}) %collective-permute-start.8) | collective-permute-done | bytes 147488 | tf_op jit(solution)/shard_map/ppermute | solution.py:411
  52.2 1.5 %shard_map.108 = (bf16[1,256,1024]{2,1,0:T(8,128)(2,1)}, bf16[1,256,1024]{2,1,0:T(8,128)(2,1)}, bf16[1,256,128]{2,1,0:T(8,128)(2,1)}, bf16[1,256,128]{2,1,0:T(8,128)(2,1)}) custom-call(bf16[288,256]{1,0:T(8,128)(2,1)S(1)} %collective-permute-done.5.rest_0_, ...), custom_call_target="tpu_custom_call", output_to_operand_aliasing={{0}: (5, {}), {1}: (6, {})} | custom-call | tf_op jit(solution)/shard_map/pallas_call | solution.py:385
  (9 shorter events, 0.0 us)
Async XLA Ops:
  0.6 11.6 %collective-permute-start = (bf16[1,256,1024]{2,1,0:T(8,128)(2,1)}, bf16[1,256,1024]{2,1,0:T(8,128)(2,1)S(1)}, u32[]{:S(2)}, u32[]{:S(2)}) collective-permute-start(bf16[1,256,1024]{2,1,0:T(8,128)(2,1)} %param.11), channel_id=1, source_target_pairs={{0,7},{1,0},{2,1},{3,2},{4,3},{5,4},{6,5},{7,6},{8,15},{9,8},{10,9... | collective-permute-start | bytes 1572872 | tf_op jit(solution)/shard_map/ppermute | solution.py:415
  5.2 9.0 %copy-start.1 = (bf16[1,256,1024]{2,1,0:T(8,128)(2,1)S(1)}, bf16[1,256,1024]{2,1,0:T(8,128)(2,1)}, u32[]{:S(2)}) copy-start(bf16[1,256,1024]{2,1,0:T(8,128)(2,1)} %gate_ref.3) | copy-start | bytes 1572868
  5.2 9.0 %copy-start.2 = (bf16[1,256,128]{2,1,0:T(8,128)(2,1)S(1)}, bf16[1,256,128]{2,1,0:T(8,128)(2,1)}, u32[]{:S(2)}) copy-start(bf16[1,256,128]{2,1,0:T(8,128)(2,1)} %q_ref.3) | copy-start | bytes 196612
  5.2 9.0 %copy-start.3 = (bf16[1,256,128]{2,1,0:T(8,128)(2,1)S(1)}, bf16[1,256,128]{2,1,0:T(8,128)(2,1)}, u32[]{:S(2)}) copy-start(bf16[1,256,128]{2,1,0:T(8,128)(2,1)} %k_ref.3) | copy-start | bytes 196612
  7.3 6.9 %copy-start = (bf16[1,256,1024]{2,1,0:T(8,128)(2,1)S(1)}, bf16[1,256,1024]{2,1,0:T(8,128)(2,1)}, u32[]{:S(2)}) copy-start(bf16[1,256,1024]{2,1,0:T(8,128)(2,1)} %v_ref.3) | copy-start | bytes 1572868
  7.4 6.8 %collective-permute-start.1 = (bf16[288,256]{1,0:T(8,128)(2,1)}, bf16[288,256]{1,0:T(8,128)(2,1)S(1)}, u32[]{:S(2)}, u32[]{:S(2)}) collective-permute-start(bf16[288,256]{1,0:T(8,128)(2,1)} %get-tuple-element.31), channel_id=1, source_target_pairs={{0,16},{8,24},{16,0},{24,8},{1,17},{9,25},{17,1},{25,9},{2,18},{10... | collective-permute-start | bytes 442376 | tf_op jit(solution)/shard_map/ppermute | solution.py:403
  8.9 9.1 %collective-permute-start.9 = (bf16[288,256]{1,0:T(8,128)(2,1)}, bf16[288,256]{1,0:T(8,128)(2,1)S(1)}, u32[]{:S(2)}, u32[]{:S(2)}) collective-permute-start(bf16[288,256]{1,0:T(8,128)(2,1)} %get-tuple-element.42), channel_id=1, source_target_pairs={{0,8},{8,0},{16,24},{24,16},{1,9},{9,1},{17,25},{25,17},{2,10},{10... | collective-permute-start | bytes 442376 | tf_op jit(solution)/shard_map/ppermute | solution.py:403
  10.4 9.0 %collective-permute-start.10 = (bf16[288,256]{1,0:T(8,128)(2,1)}, bf16[288,256]{1,0:T(8,128)(2,1)S(1)}, u32[]{:S(2)}, u32[]{:S(2)}) collective-permute-start(bf16[288,256]{1,0:T(8,128)(2,1)} %get-tuple-element.43), channel_id=1, source_target_pairs={{0,24},{8,16},{16,8},{24,0},{1,25},{9,17},{17,9},{25,1},{2,26},{10... | collective-permute-start | bytes 442376 | tf_op jit(solution)/shard_map/ppermute | solution.py:403
  14.2 11.3 %copy-start.4 = (bf16[288,256]{1,0:T(8,128)(2,1)S(1)}, bf16[288,256]{1,0:T(8,128)(2,1)}, u32[]{:S(2)}) copy-start(bf16[288,256]{1,0:T(8,128)(2,1)} %get-tuple-element.41.rest_0_) | copy-start | bytes 442372
  15.0 10.5 %copy-start.5 = (bf16[1,3,1024]{2,1,0:T(4,128)(2,1)S(1)}, bf16[1,3,1024]{2,1,0:T(4,128)(2,1)}, u32[]{:S(2)}) copy-start(bf16[1,3,1024]{2,1,0:T(4,128)(2,1)} %taps_ref.3) | copy-start | bytes 18436
  15.0 18.3 %collective-permute-start.2 = (bf16[416,256]{1,0:T(8,128)(2,1)S(1)}, bf16[416,256]{1,0:T(8,128)(2,1)S(1)}, u32[]{:S(2)}, u32[]{:S(2)}) collective-permute-start(bf16[416,256]{1,0:T(8,128)(2,1)S(1)} %get-tuple-element.34), channel_id=1, source_target_pairs={{0,8},{8,0},{16,24},{24,16},{1,9},{9,1},{17,25},{25,17},{2,10},{10... | collective-permute-start | bytes 638984 | tf_op jit(solution)/shard_map/ppermute | solution.py:403
  16.0 6.8 %collective-permute-start.11 = (bf16[128,256]{1,0:T(8,128)(2,1)S(1)}, bf16[128,256]{1,0:T(8,128)(2,1)S(1)}, u32[]{:S(2)}, u32[]{:S(2)}) collective-permute-start(bf16[128,256]{1,0:T(8,128)(2,1)S(1)} %get-tuple-element.44), channel_id=1, source_target_pairs={{0,8},{8,0},{16,24},{24,16},{1,9},{9,1},{17,25},{25,17},{2,10},{10... | collective-permute-start | bytes 196616 | tf_op jit(solution)/shard_map/ppermute | solution.py:403
  17.1 6.9 %collective-permute-start.12 = (bf16[128,256]{1,0:T(8,128)(2,1)S(1)}, bf16[128,256]{1,0:T(8,128)(2,1)S(1)}, u32[]{:S(2)}, u32[]{:S(2)}) collective-permute-start(bf16[128,256]{1,0:T(8,128)(2,1)S(1)} %get-tuple-element.45), channel_id=1, source_target_pairs={{0,16},{8,24},{16,0},{24,8},{1,17},{9,25},{17,1},{25,9},{2,18},{10... | collective-permute-start | bytes 196616 | tf_op jit(solution)/shard_map/ppermute | solution.py:403
  18.0 7.5 %collective-permute-start.13 = (bf16[128,256]{1,0:T(8,128)(2,1)S(1)}, bf16[128,256]{1,0:T(8,128)(2,1)S(1)}, u32[]{:S(2)}, u32[]{:S(2)}) collective-permute-start(bf16[128,256]{1,0:T(8,128)(2,1)S(1)} %get-tuple-element.46), channel_id=1, source_target_pairs={{0,24},{8,16},{16,8},{24,0},{1,25},{9,17},{17,9},{25,1},{2,26},{10... | collective-permute-start | bytes 196616 | tf_op jit(solution)/shard_map/ppermute | solution.py:403
  19.5 14.2 %collective-permute-start.3 = (bf16[416,256]{1,0:T(8,128)(2,1)S(1)}, bf16[416,256]{1,0:T(8,128)(2,1)S(1)}, u32[]{:S(2)}, u32[]{:S(2)}) collective-permute-start(bf16[416,256]{1,0:T(8,128)(2,1)S(1)} %get-tuple-element.35), channel_id=1, source_target_pairs={{0,16},{8,24},{16,0},{24,8},{1,17},{9,25},{17,1},{25,9},{2,18},{10... | collective-permute-start | bytes 638984 | tf_op jit(solution)/shard_map/ppermute | solution.py:403
  22.8 2.7 %copy-start.6 = (s32[1,4]{1,0:T(1,128)S(1)}, s32[1,4]{1,0:T(1,128)}, u32[]{:S(2)}) copy-start(s32[1,4]{1,0:T(1,128)} %bounds.3) | copy-start | bytes 52
  22.8 12.7 %collective-permute-start.4 = (bf16[416,256]{1,0:T(8,128)(2,1)S(1)}, bf16[416,256]{1,0:T(8,128)(2,1)S(1)}, u32[]{:S(2)}, u32[]{:S(2)}) collective-permute-start(bf16[416,256]{1,0:T(8,128)(2,1)S(1)} %get-tuple-element.36), channel_id=1, source_target_pairs={{0,24},{8,16},{16,8},{24,0},{1,25},{9,17},{17,9},{25,1},{2,26},{10... | collective-permute-start | bytes 638984 | tf_op jit(solution)/shard_map/ppermute | solution.py:403
  31.1 10.2 %collective-permute-start.14 = (bf16[288,256]{1,0:T(8,128)(2,1)S(1)}, bf16[288,256]{1,0:T(8,128)(2,1)S(1)}, u32[]{:S(2)}, u32[]{:S(2)}) collective-permute-start(bf16[288,256]{1,0:T(8,128)(2,1)S(1)} %get-tuple-element.47), channel_id=1, source_target_pairs={{0,7},{1,0},{2,1},{3,2},{4,3},{5,4},{6,5},{7,6},{8,15},{9,8},{10,9... | collective-permute-start | bytes 442376 | tf_op jit(solution)/shard_map/ppermute | solution.py:411
  33.1 9.1 %collective-permute-start.15 = (bf16[288,256]{1,0:T(8,128)(2,1)S(1)}, bf16[288,256]{1,0:T(8,128)(2,1)S(1)}, u32[]{:S(2)}, u32[]{:S(2)}) collective-permute-start(bf16[288,256]{1,0:T(8,128)(2,1)S(1)} %get-tuple-element.48), channel_id=1, source_target_pairs={{0,15},{1,8},{2,9},{3,10},{4,11},{5,12},{6,13},{7,14},{8,7},{9,0},... | collective-permute-start | bytes 442376 | tf_op jit(solution)/shard_map/ppermute | solution.py:411
  33.3 9.6 %collective-permute-start.16 = (bf16[288,256]{1,0:T(8,128)(2,1)S(1)}, bf16[288,256]{1,0:T(8,128)(2,1)S(1)}, u32[]{:S(2)}, u32[]{:S(2)}) collective-permute-start(bf16[288,256]{1,0:T(8,128)(2,1)S(1)} %get-tuple-element.49), channel_id=1, source_target_pairs={{0,23},{1,16},{2,17},{3,18},{4,19},{5,20},{6,21},{7,22},{8,31},{9,... | collective-permute-start | bytes 442376 | tf_op jit(solution)/shard_map/ppermute | solution.py:411
  33.7 12.4 %collective-permute-start.17 = (bf16[288,256]{1,0:T(8,128)(2,1)S(1)}, bf16[288,256]{1,0:T(8,128)(2,1)S(1)}, u32[]{:S(2)}, u32[]{:S(2)}) collective-permute-start(bf16[288,256]{1,0:T(8,128)(2,1)S(1)} %get-tuple-element.50), channel_id=1, source_target_pairs={{0,31},{1,24},{2,25},{3,26},{4,27},{5,28},{6,29},{7,30},{8,23},{9,... | collective-permute-start | bytes 442376 | tf_op jit(solution)/shard_map/ppermute | solution.py:411
  41.0 5.9 %collective-permute-start.5 = (bf16[288,256]{1,0:T(8,128)(2,1)S(1)}, bf16[288,256]{1,0:T(8,128)(2,1)S(1)}, u32[]{:S(2)}, u32[]{:S(2)}) collective-permute-start(bf16[288,256]{1,0:T(8,128)(2,1)S(1)} %get-tuple-element.37), channel_id=1, source_target_pairs={{0,7},{1,0},{2,1},{3,2},{4,3},{5,4},{6,5},{7,6},{8,15},{9,8},{10,9... | collective-permute-start | bytes 442376 | tf_op jit(solution)/shard_map/ppermute | solution.py:411
  41.3 5.6 %collective-permute-start.6 = (bf16[288,256]{1,0:T(8,128)(2,1)S(1)}, bf16[288,256]{1,0:T(8,128)(2,1)S(1)}, u32[]{:S(2)}, u32[]{:S(2)}) collective-permute-start(bf16[288,256]{1,0:T(8,128)(2,1)S(1)} %get-tuple-element.38), channel_id=1, source_target_pairs={{0,15},{1,8},{2,9},{3,10},{4,11},{5,12},{6,13},{7,14},{8,7},{9,0},... | collective-permute-start | bytes 442376 | tf_op jit(solution)/shard_map/ppermute | solution.py:411
  42.1 5.0 %collective-permute-start.7 = (bf16[288,256]{1,0:T(8,128)(2,1)S(1)}, bf16[288,256]{1,0:T(8,128)(2,1)S(1)}, u32[]{:S(2)}, u32[]{:S(2)}) collective-permute-start(bf16[288,256]{1,0:T(8,128)(2,1)S(1)} %get-tuple-element.39), channel_id=1, source_target_pairs={{0,23},{1,16},{2,17},{3,18},{4,19},{5,20},{6,21},{7,22},{8,31},{9,... | collective-permute-start | bytes 442376 | tf_op jit(solution)/shard_map/ppermute | solution.py:411
  43.0 9.3 %collective-permute-start.8 = (bf16[288,256]{1,0:T(8,128)(2,1)S(1)}, bf16[288,256]{1,0:T(8,128)(2,1)S(1)}, u32[]{:S(2)}, u32[]{:S(2)}) collective-permute-start(bf16[288,256]{1,0:T(8,128)(2,1)S(1)} %get-tuple-element.40), channel_id=1, source_target_pairs={{0,31},{1,24},{2,25},{3,26},{4,27},{5,28},{6,29},{7,30},{8,23},{9,... | collective-permute-start | bytes 442376 | tf_op jit(solution)/shard_map/ppermute | solution.py:411

commit v2 on v1

--- a/solution.py
+++ b/solution.py
@@ -32,6 +32,10 @@
 
 def first_head(place, count):
     return (place * HEADS) // count
+
+
+def cost(micros):
+    return pl.CostEstimate(flops=int(1e9 * micros), bytes_accessed=int(3e6 * micros), transcendentals=0)
 
 
 def lanes_of(head, width):
@@ -90,6 +94,7 @@
     rows = ROWS if phase == 0 else ROWS + TOK // 2
     return pl.pallas_call(
         functools.partial(pack_kernel, count, phase),
+        cost_estimate=cost(2),
         out_shape=[jax.ShapeDtypeStruct((rows, 2 * DV), BF16)] * count,
         in_specs=[HBM] * 4 + [VMEM] * min(1, len(others)) + [ANY] * max(0, len(others) - 1),
         out_specs=[VMEM] * count,
@@ -104,19 +109,21 @@
 
 
 def pack_grads_kernel(count, grad_ref, *outs):
+    outs = outs[-count:]
     me = lax.axis_index("ctx")
     for partner, out in enumerate(outs):
         pack_grad(count, 0, me ^ partner, grad_ref, out)
 
 
-def pack_grads(count, grad):
+def pack_grads(count, grad, *before):
     return pl.pallas_call(
         functools.partial(pack_grads_kernel, count),
+        cost_estimate=cost(0.5),
         out_shape=[jax.ShapeDtypeStruct((TOK // 2, 2 * DV), BF16)] * count,
-        in_specs=[VMEM],
+        in_specs=[VMEM] + [ANY] * len(before),
         out_specs=[VMEM] * count,
         compiler_params=params(count),
-    )(grad)
+    )(grad, *before)
 
 
 def nn(a, b):
@@ -320,6 +327,7 @@
     saved = (count * (count - 1) // 2 if count <= UNROLLED else count - 1) * TOK
     return pl.pallas_call(
         functools.partial(attend_kernel, count, phase),
+        cost_estimate=cost(5),
         out_shape=[jax.ShapeDtypeStruct((ROWS, 2 * DV), BF16)] * outs,
         in_specs=[SMEM, VMEM] + [VMEM] * (len(packed) + len(grads)),
         out_specs=[VMEM] * outs,
@@ -384,6 +392,7 @@
     small = [narrow, narrow] if last else [jax.ShapeDtypeStruct(turned, BF16)]
     return pl.pallas_call(
         functools.partial(unpack_kernel, count, phase),
+        cost_estimate=cost(1),
         out_shape=[wide, wide] + small,
         in_specs=[VMEM] * many + [VMEM, HBM, HBM][: len(begun)],
         out_specs=[HBM, HBM] + [VMEM] * len(small),
@@ -423,7 +432,7 @@
     own_grads = pack_grads(count, cotangent)
     grads = spread(own_grads)
     for phase in range(1, phases):
-        before = blocks[phase - 1][order[-2]], own_grads[0]
+        before = [own_grads[0]]
         blocks.append(spread(pack(count, phase, *inputs, cotangent, *before)))
     arrived = []
     for phase in range(phases):

time: 53.9 us -> 50.3 us (0.933)
  the two profiles are of different devices: /device:TPU:0 before, /device:TPU:1 now
where the time goes in v2:
time: 50.3 us; the launch traced here: 50.1 us
  starting transfers between devices  21.8 us (43%)
  Pallas kernels  16.4 us (33%)
  waiting for transfers between devices  11.2 us (22%)
  between operations  0.73 us (1%)
    ppermute x8, starting transfers between devices, across_back(): return lax.ppermute(value, ('ctx', 'pipe'), pairs)  12.2 us
    pallas_call x2, Pallas kernels, attend(): pl.pallas_call(functools.partial(attend_kernel, count, phase), cost_estim...  11.1 us
    ppermute x9, starting transfers between devices, across(): return lax.ppermute(value, 'ctx', [(c, c ^ partner) for c in range(count)])  9.51 us
    ppermute x8, waiting for transfers between devices, across_back(): return lax.ppermute(value, ('ctx', 'pipe'), pairs)  6.75 us
    ppermute x1, waiting for transfers between devices, on_device(): cotangent = lax.ppermute(out_grad, 'pipe', shift)  3.55 us
    pallas_call x2, Pallas kernels, pack(): pl.pallas_call(functools.partial(pack_kernel, count, phase), cost_estimat...  2.83 us
    pallas_call x2, Pallas kernels, unpack(): pl.pallas_call(functools.partial(unpack_kernel, count, phase), cost_estim...  2.38 us
  transfers between devices with their start and end apart: 18, of which 5 were waited for; matrix products, arithmetic and copies ran while one was open for 0% of the time, Pallas kernels for 30%

profile of v2, /device:TPU:1, one launch (start us, length us, event | category | flops | bytes accessed | tf_op | source)
XLA Modules:
  0.0 50.1 jit_solution(10296671909143822110)
XLA Ops:
  0.6 0.1 collective-permute-start
  0.7 2.1 %shard_map.105 = (bf16[288,256]{1,0:T(8,128)(2,1)}, bf16[288,256]{1,0:T(8,128)(2,1)}, bf16[288,256]{1,0:T(8,128)(2,1)}, bf16[288,256]{1,0:T(8,128)(2,1)}) custom-call(bf16[1,256,128]{2,1,0:T(8,128)(2,1)} %q_ref.3, bf16[1,256,128]{2,1,0:T(8,128)(2,1)} %k_ref.3, bf16[1,256,1024]{2,1,0:T(8,128)(2,1)} %v_ref.3, bf16[1,256,1024]{2,1,0:T(8,128)(2,1)} %gate_ref.3), custom_call_target="tpu_custom_call" | custom-call | flops 2000000000 | bytes 6000000 | tf_op jit(solution)/shard_map/pallas_call | solution.py:95
  2.8 2.7 %collective-permute-start.8 = (bf16[288,256]{1,0:T(8,128)(2,1)}, bf16[288,256]{1,0:T(8,128)(2,1)S(1)}, u32[]{:S(2)}, u32[]{:S(2)}) collective-permute-start(bf16[288,256]{1,0:T(8,128)(2,1)} %get-tuple-element.41), channel_id=1, source_target_pairs={{0,8},{8,0},{16,24},{24,16},{1,9},{9,1},{17,25},{25,17},{2,10},{10... | collective-permute-start | bytes 442376 | tf_op jit(solution)/shard_map/ppermute | solution.py:412
  5.6 1.2 %collective-permute-start.9 = (bf16[288,256]{1,0:T(8,128)(2,1)}, bf16[288,256]{1,0:T(8,128)(2,1)S(1)}, u32[]{:S(2)}, u32[]{:S(2)}) collective-permute-start(bf16[288,256]{1,0:T(8,128)(2,1)} %get-tuple-element.42), channel_id=1, source_target_pairs={{0,16},{8,24},{16,0},{24,8},{1,17},{9,25},{17,1},{25,9},{2,18},{10... | collective-permute-start | bytes 442376 | tf_op jit(solution)/shard_map/ppermute | solution.py:412
  6.8 0.1 collective-permute-start.10
  6.9 3.5 %collective-permute-done.grad_ref.rest_0_ = bf16[1,256,1024]{2,1,0:T(8,128)(2,1)S(1)} collective-permute-done((bf16[1,256,1024]{2,1,0:T(8,128)(2,1)}, bf16[1,256,1024]{2,1,0:T(8,128)(2,1)S(1)}, u32[]{:S(2)}, u32[]{:S(2)}) %collective-permute-start) | collective-permute-done | bytes 524320 | tf_op jit(solution)/shard_map/ppermute | solution.py:424
  10.4 0.1 shard_map.102
  10.5 1.3 %collective-permute-start.11 = (bf16[128,256]{1,0:T(8,128)(2,1)S(1)}, bf16[128,256]{1,0:T(8,128)(2,1)S(1)}, u32[]{:S(2)}, u32[]{:S(2)}) collective-permute-start(bf16[128,256]{1,0:T(8,128)(2,1)S(1)} %get-tuple-element.44), channel_id=1, source_target_pairs={{0,8},{8,0},{16,24},{24,16},{1,9},{9,1},{17,25},{25,17},{2,10},{10... | collective-permute-start | bytes 196616 | tf_op jit(solution)/shard_map/ppermute | solution.py:412
  11.8 1.2 %collective-permute-start.12 = (bf16[128,256]{1,0:T(8,128)(2,1)S(1)}, bf16[128,256]{1,0:T(8,128)(2,1)S(1)}, u32[]{:S(2)}, u32[]{:S(2)}) collective-permute-start(bf16[128,256]{1,0:T(8,128)(2,1)S(1)} %get-tuple-element.45), channel_id=1, source_target_pairs={{0,16},{8,24},{16,0},{24,8},{1,17},{9,25},{17,1},{25,9},{2,18},{10... | collective-permute-start | bytes 196616 | tf_op jit(solution)/shard_map/ppermute | solution.py:412
  13.0 0.0 collective-permute-done.8.rest_1_
  13.0 0.2 collective-permute-start.13
  13.2 0.0 copy-done
  13.2 0.0 copy-done.1
  13.2 0.0 copy-done.2
  13.3 0.0 copy-start.4
  13.3 0.0 copy-start.6
  13.3 0.7 %shard_map.103 = (bf16[416,256]{1,0:T(8,128)(2,1)S(1)}, bf16[416,256]{1,0:T(8,128)(2,1)S(1)}, bf16[416,256]{1,0:T(8,128)(2,1)S(1)}, bf16[416,256]{1,0:T(8,128)(2,1)S(1)}) custom-call(bf16[1,256,128]{2,1,0:T(8,128)(2,1)S(1)} %copy-done.2, bf16[1,256,128]{2,1,0:T(8,128)(2,1)S(1)} %copy-done.3, bf16[1,256,1024]{2,1,0:T(8,128)(2,1)S(1)} %copy-done, ...), custom_call_target="tpu_custom_call" | custom-call | flops 2000000000 | bytes 6000000 | tf_op jit(solution)/shard_map/pallas_call | solution.py:95
  14.0 0.0 collective-permute-done.9.rest_2_
  14.0 1.3 %collective-permute-start.1 = (bf16[416,256]{1,0:T(8,128)(2,1)S(1)}, bf16[416,256]{1,0:T(8,128)(2,1)S(1)}, u32[]{:S(2)}, u32[]{:S(2)}) collective-permute-start(bf16[416,256]{1,0:T(8,128)(2,1)S(1)} %get-tuple-element.33), channel_id=1, source_target_pairs={{0,8},{8,0},{16,24},{24,16},{1,9},{9,1},{17,25},{25,17},{2,10},{10... | collective-permute-start | bytes 638984 | tf_op jit(solution)/shard_map/ppermute | solution.py:412
  15.3 0.0 collective-permute-done.10.rest_3_
  15.3 1.2 %collective-permute-start.2 = (bf16[416,256]{1,0:T(8,128)(2,1)S(1)}, bf16[416,256]{1,0:T(8,128)(2,1)S(1)}, u32[]{:S(2)}, u32[]{:S(2)}) collective-permute-start(bf16[416,256]{1,0:T(8,128)(2,1)S(1)} %get-tuple-element.34), channel_id=1, source_target_pairs={{0,16},{8,24},{16,0},{24,8},{1,17},{9,25},{17,1},{25,9},{2,18},{10... | collective-permute-start | bytes 638984 | tf_op jit(solution)/shard_map/ppermute | solution.py:412
  16.6 0.0 collective-permute-done.11.rest_5_
  16.6 0.2 collective-permute-start.3
  16.8 0.0 collective-permute-done.12.rest_6_
  16.8 0.9 %collective-permute-done.13.rest_7_ = bf16[128,256]{1,0:T(8,128)(2,1)S(1)} collective-permute-done((bf16[128,256]{1,0:T(8,128)(2,1)S(1)}, bf16[128,256]{1,0:T(8,128)(2,1)S(1)}, u32[]{:S(2)}, u32[]{:S(2)}) %collective-permute-start.13) | collective-permute-done | bytes 65568 | tf_op jit(solution)/shard_map/ppermute | solution.py:412
  17.7 5.5 %shard_map.106 = (bf16[288,256]{1,0:T(8,128)(2,1)S(1)}, bf16[288,256]{1,0:T(8,128)(2,1)S(1)}, bf16[288,256]{1,0:T(8,128)(2,1)S(1)}, bf16[288,256]{1,0:T(8,128)(2,1)S(1)}) custom-call(s32[1,4]{1,0:T(1,128)S(1)} %copy-done.5, bf16[1,3,1024]{2,1,0:T(4,128)(2,1)S(1)} %copy-done.4, bf16[288,256]{1,0:T(8,128)(2,1)S(1)} %copy-done.6, ...), custom_call_target="tpu_custom_call" | custom-call | flops 5000000000 | bytes 15000000 | tf_op jit(solution)/shard_map/pallas_call | solution.py:328
  23.2 3.8 %collective-permute-start.14 = (bf16[288,256]{1,0:T(8,128)(2,1)S(1)}, bf16[288,256]{1,0:T(8,128)(2,1)S(1)}, u32[]{:S(2)}, u32[]{:S(2)}) collective-permute-start(bf16[288,256]{1,0:T(8,128)(2,1)S(1)} %get-tuple-element.47), channel_id=1, source_target_pairs={{0,7},{1,0},{2,1},{3,2},{4,3},{5,4},{6,5},{7,6},{8,15},{9,8},{10,9... | collective-permute-start | bytes 442376 | tf_op jit(solution)/shard_map/ppermute | solution.py:420
  27.0 1.8 %collective-permute-start.15 = (bf16[288,256]{1,0:T(8,128)(2,1)S(1)}, bf16[288,256]{1,0:T(8,128)(2,1)S(1)}, u32[]{:S(2)}, u32[]{:S(2)}) collective-permute-start(bf16[288,256]{1,0:T(8,128)(2,1)S(1)} %get-tuple-element.48), channel_id=1, source_target_pairs={{0,15},{1,8},{2,9},{3,10},{4,11},{5,12},{6,13},{7,14},{8,7},{9,0},... | collective-permute-start | bytes 442376 | tf_op jit(solution)/shard_map/ppermute | solution.py:420
  28.9 0.0 collective-permute-done.1.rest_1_
  28.9 1.0 %collective-permute-start.16 = (bf16[288,256]{1,0:T(8,128)(2,1)S(1)}, bf16[288,256]{1,0:T(8,128)(2,1)S(1)}, u32[]{:S(2)}, u32[]{:S(2)}) collective-permute-start(bf16[288,256]{1,0:T(8,128)(2,1)S(1)} %get-tuple-element.49), channel_id=1, source_target_pairs={{0,23},{1,16},{2,17},{3,18},{4,19},{5,20},{6,21},{7,22},{8,31},{9,... | collective-permute-start | bytes 442376 | tf_op jit(solution)/shard_map/ppermute | solution.py:420
  29.9 0.0 collective-permute-done.2.rest_2_
  29.9 0.3 collective-permute-start.17
  30.2 0.0 collective-permute-done.3.rest_3_
  30.2 5.5 %shard_map.104 = (bf16[288,256]{1,0:T(8,128)(2,1)S(1)}, bf16[288,256]{1,0:T(8,128)(2,1)S(1)}, bf16[288,256]{1,0:T(8,128)(2,1)S(1)}, bf16[288,256]{1,0:T(8,128)(2,1)S(1)}) custom-call(s32[1,4]{1,0:T(1,128)S(1)} %copy-done.5, bf16[1,3,1024]{2,1,0:T(4,128)(2,1)S(1)} %copy-done.4, bf16[416,256]{1,0:T(8,128)(2,1)S(1)} %get-tuple-element.32.rest_0_, ...), custom_call_target="tpu_custom_call" | custom-call | flops 5000000000 | bytes 15000000 | tf_op jit(solution)/shard_map/pallas_call | solution.py:328
  35.8 3.1 %collective-permute-start.4 = (bf16[288,256]{1,0:T(8,128)(2,1)S(1)}, bf16[288,256]{1,0:T(8,128)(2,1)S(1)}, u32[]{:S(2)}, u32[]{:S(2)}) collective-permute-start(bf16[288,256]{1,0:T(8,128)(2,1)S(1)} %get-tuple-element.36), channel_id=1, source_target_pairs={{0,7},{1,0},{2,1},{3,2},{4,3},{5,4},{6,5},{7,6},{8,15},{9,8},{10,9... | collective-permute-start | bytes 442376 | tf_op jit(solution)/shard_map/ppermute | solution.py:420
  38.9 0.0 collective-permute-done.14.rest_0_
  38.9 0.5 %collective-permute-start.5 = (bf16[288,256]{1,0:T(8,128)(2,1)S(1)}, bf16[288,256]{1,0:T(8,128)(2,1)S(1)}, u32[]{:S(2)}, u32[]{:S(2)}) collective-permute-start(bf16[288,256]{1,0:T(8,128)(2,1)S(1)} %get-tuple-element.37), channel_id=1, source_target_pairs={{0,15},{1,8},{2,9},{3,10},{4,11},{5,12},{6,13},{7,14},{8,7},{9,0},... | collective-permute-start | bytes 442376 | tf_op jit(solution)/shard_map/ppermute | solution.py:420
  39.4 0.0 collective-permute-done.15.rest_1_
  39.4 0.5 %collective-permute-start.6 = (bf16[288,256]{1,0:T(8,128)(2,1)S(1)}, bf16[288,256]{1,0:T(8,128)(2,1)S(1)}, u32[]{:S(2)}, u32[]{:S(2)}) collective-permute-start(bf16[288,256]{1,0:T(8,128)(2,1)S(1)} %get-tuple-element.38), channel_id=1, source_target_pairs={{0,23},{1,16},{2,17},{3,18},{4,19},{5,20},{6,21},{7,22},{8,31},{9,... | collective-permute-start | bytes 442376 | tf_op jit(solution)/shard_map/ppermute | solution.py:420
  40.0 0.0 collective-permute-done.16.rest_2_
  40.0 1.0 %collective-permute-start.7 = (bf16[288,256]{1,0:T(8,128)(2,1)S(1)}, bf16[288,256]{1,0:T(8,128)(2,1)S(1)}, u32[]{:S(2)}, u32[]{:S(2)}) collective-permute-start(bf16[288,256]{1,0:T(8,128)(2,1)S(1)} %get-tuple-element.39), channel_id=1, source_target_pairs={{0,31},{1,24},{2,25},{3,26},{4,27},{5,28},{6,29},{7,30},{8,23},{9,... | collective-permute-start | bytes 442376 | tf_op jit(solution)/shard_map/ppermute | solution.py:420
  40.9 0.0 collective-permute-done.17.rest_3_
  41.0 0.8 %shard_map.107 = (bf16[1,256,1024]{2,1,0:T(8,128)(2,1)}, bf16[1,256,1024]{2,1,0:T(8,128)(2,1)}, bf16[2,128,256]{2,1,0:T(8,128)(2,1)S(1)}) custom-call(bf16[288,256]{1,0:T(8,128)(2,1)S(1)} %collective-permute-done.14.rest_0_, bf16[288,256]{1,0:T(8,128)(2,1)S(1)} %collective-permute-done.15.rest_1_, bf16[288,256]{1,0:T(8,128)(2,1)S(1)} %collective-permute-done.16.rest_2_, ...), custom_call_target="tpu_custom_call" | custom-call | flops 1000000000 | bytes 3000000 | tf_op jit(solution)/shard_map/pallas_call | solution.py:393
  41.8 0.0 collective-permute-done.4.rest_0_
  41.8 2.7 %collective-permute-done.5.rest_1_ = bf16[288,256]{1,0:T(8,128)(2,1)S(1)} collective-permute-done((bf16[288,256]{1,0:T(8,128)(2,1)S(1)}, bf16[288,256]{1,0:T(8,128)(2,1)S(1)}, u32[]{:S(2)}, u32[]{:S(2)}) %collective-permute-start.5) | collective-permute-done | bytes 147488 | tf_op jit(solution)/shard_map/ppermute | solution.py:420
  44.5 0.5 %collective-permute-done.6.rest_2_ = bf16[288,256]{1,0:T(8,128)(2,1)S(1)} collective-permute-done((bf16[288,256]{1,0:T(8,128)(2,1)S(1)}, bf16[288,256]{1,0:T(8,128)(2,1)S(1)}, u32[]{:S(2)}, u32[]{:S(2)}) %collective-permute-start.6) | collective-permute-done | bytes 147488 | tf_op jit(solution)/shard_map/ppermute | solution.py:420
  45.0 3.5 %collective-permute-done.7.rest_3_ = bf16[288,256]{1,0:T(8,128)(2,1)S(1)} collective-permute-done((bf16[288,256]{1,0:T(8,128)(2,1)S(1)}, bf16[288,256]{1,0:T(8,128)(2,1)S(1)}, u32[]{:S(2)}, u32[]{:S(2)}) %collective-permute-start.7) | collective-permute-done | bytes 147488 | tf_op jit(solution)/shard_map/ppermute | solution.py:420
  48.6 1.5 %shard_map.108 = (bf16[1,256,1024]{2,1,0:T(8,128)(2,1)}, bf16[1,256,1024]{2,1,0:T(8,128)(2,1)}, bf16[1,256,128]{2,1,0:T(8,128)(2,1)}, bf16[1,256,128]{2,1,0:T(8,128)(2,1)}) custom-call(bf16[288,256]{1,0:T(8,128)(2,1)S(1)} %collective-permute-done.4.rest_0_, ...), custom_call_target="tpu_custom_call", output_to_operand_aliasing={{0}: (5, {}), {1}: (6, {})} | custom-call | flops 1000000000 | bytes 3000000 | tf_op jit(solution)/shard_map/pallas_call | solution.py:393
  (9 shorter events, 0.0 us)
Async XLA Ops:
  0.6 9.8 %collective-permute-start = (bf16[1,256,1024]{2,1,0:T(8,128)(2,1)}, bf16[1,256,1024]{2,1,0:T(8,128)(2,1)S(1)}, u32[]{:S(2)}, u32[]{:S(2)}) collective-permute-start(bf16[1,256,1024]{2,1,0:T(8,128)(2,1)} %param.11), channel_id=1, source_target_pairs={{0,7},{1,0},{2,1},{3,2},{4,3},{5,4},{6,5},{7,6},{8,15},{9,8},{10,9... | collective-permute-start | bytes 1572872 | tf_op jit(solution)/shard_map/ppermute | solution.py:424
  2.8 10.2 %collective-permute-start.8 = (bf16[288,256]{1,0:T(8,128)(2,1)}, bf16[288,256]{1,0:T(8,128)(2,1)S(1)}, u32[]{:S(2)}, u32[]{:S(2)}) collective-permute-start(bf16[288,256]{1,0:T(8,128)(2,1)} %get-tuple-element.41), channel_id=1, source_target_pairs={{0,8},{8,0},{16,24},{24,16},{1,9},{9,1},{17,25},{25,17},{2,10},{10... | collective-permute-start | bytes 442376 | tf_op jit(solution)/shard_map/ppermute | solution.py:412
  5.6 8.5 %collective-permute-start.9 = (bf16[288,256]{1,0:T(8,128)(2,1)}, bf16[288,256]{1,0:T(8,128)(2,1)S(1)}, u32[]{:S(2)}, u32[]{:S(2)}) collective-permute-start(bf16[288,256]{1,0:T(8,128)(2,1)} %get-tuple-element.42), channel_id=1, source_target_pairs={{0,16},{8,24},{16,0},{24,8},{1,17},{9,25},{17,1},{25,9},{2,18},{10... | collective-permute-start | bytes 442376 | tf_op jit(solution)/shard_map/ppermute | solution.py:412
  6.8 6.4 %copy-start = (bf16[1,256,1024]{2,1,0:T(8,128)(2,1)S(1)}, bf16[1,256,1024]{2,1,0:T(8,128)(2,1)}, u32[]{:S(2)}) copy-start(bf16[1,256,1024]{2,1,0:T(8,128)(2,1)} %v_ref.3) | copy-start | bytes 1572868
  6.8 6.4 %copy-start.1 = (bf16[1,256,1024]{2,1,0:T(8,128)(2,1)S(1)}, bf16[1,256,1024]{2,1,0:T(8,128)(2,1)}, u32[]{:S(2)}) copy-start(bf16[1,256,1024]{2,1,0:T(8,128)(2,1)} %gate_ref.3) | copy-start | bytes 1572868
  6.8 6.4 %copy-start.2 = (bf16[1,256,128]{2,1,0:T(8,128)(2,1)S(1)}, bf16[1,256,128]{2,1,0:T(8,128)(2,1)}, u32[]{:S(2)}) copy-start(bf16[1,256,128]{2,1,0:T(8,128)(2,1)} %q_ref.3) | copy-start | bytes 196612
  6.8 6.4 %copy-start.3 = (bf16[1,256,128]{2,1,0:T(8,128)(2,1)S(1)}, bf16[1,256,128]{2,1,0:T(8,128)(2,1)}, u32[]{:S(2)}) copy-start(bf16[1,256,128]{2,1,0:T(8,128)(2,1)} %k_ref.3) | copy-start | bytes 196612
  6.8 8.5 %collective-permute-start.10 = (bf16[288,256]{1,0:T(8,128)(2,1)}, bf16[288,256]{1,0:T(8,128)(2,1)S(1)}, u32[]{:S(2)}, u32[]{:S(2)}) collective-permute-start(bf16[288,256]{1,0:T(8,128)(2,1)} %get-tuple-element.43), channel_id=1, source_target_pairs={{0,24},{8,16},{16,8},{24,0},{1,25},{9,17},{17,9},{25,1},{2,26},{10... | collective-permute-start | bytes 442376 | tf_op jit(solution)/shard_map/ppermute | solution.py:412
  10.5 6.0 %collective-permute-start.11 = (bf16[128,256]{1,0:T(8,128)(2,1)S(1)}, bf16[128,256]{1,0:T(8,128)(2,1)S(1)}, u32[]{:S(2)}, u32[]{:S(2)}) collective-permute-start(bf16[128,256]{1,0:T(8,128)(2,1)S(1)} %get-tuple-element.44), channel_id=1, source_target_pairs={{0,8},{8,0},{16,24},{24,16},{1,9},{9,1},{17,25},{25,17},{2,10},{10... | collective-permute-start | bytes 196616 | tf_op jit(solution)/shard_map/ppermute | solution.py:412
  11.8 5.0 %collective-permute-start.12 = (bf16[128,256]{1,0:T(8,128)(2,1)S(1)}, bf16[128,256]{1,0:T(8,128)(2,1)S(1)}, u32[]{:S(2)}, u32[]{:S(2)}) collective-permute-start(bf16[128,256]{1,0:T(8,128)(2,1)S(1)} %get-tuple-element.45), channel_id=1, source_target_pairs={{0,16},{8,24},{16,0},{24,8},{1,17},{9,25},{17,1},{25,9},{2,18},{10... | collective-permute-start | bytes 196616 | tf_op jit(solution)/shard_map/ppermute | solution.py:412
  13.0 4.6 %collective-permute-start.13 = (bf16[128,256]{1,0:T(8,128)(2,1)S(1)}, bf16[128,256]{1,0:T(8,128)(2,1)S(1)}, u32[]{:S(2)}, u32[]{:S(2)}) collective-permute-start(bf16[128,256]{1,0:T(8,128)(2,1)S(1)} %get-tuple-element.46), channel_id=1, source_target_pairs={{0,24},{8,16},{16,8},{24,0},{1,25},{9,17},{17,9},{25,1},{2,26},{10... | collective-permute-start | bytes 196616 | tf_op jit(solution)/shard_map/ppermute | solution.py:412
  13.3 4.4 %copy-start.4 = (bf16[1,3,1024]{2,1,0:T(4,128)(2,1)S(1)}, bf16[1,3,1024]{2,1,0:T(4,128)(2,1)}, u32[]{:S(2)}) copy-start(bf16[1,3,1024]{2,1,0:T(4,128)(2,1)} %taps_ref.3) | copy-start | bytes 18436
  13.3 4.4 %copy-start.6 = (bf16[288,256]{1,0:T(8,128)(2,1)S(1)}, bf16[288,256]{1,0:T(8,128)(2,1)}, u32[]{:S(2)}) copy-start(bf16[288,256]{1,0:T(8,128)(2,1)} %get-tuple-element.40.rest_0_) | copy-start | bytes 442372
  14.0 14.8 %collective-permute-start.1 = (bf16[416,256]{1,0:T(8,128)(2,1)S(1)}, bf16[416,256]{1,0:T(8,128)(2,1)S(1)}, u32[]{:S(2)}, u32[]{:S(2)}) collective-permute-start(bf16[416,256]{1,0:T(8,128)(2,1)S(1)} %get-tuple-element.33), channel_id=1, source_target_pairs={{0,8},{8,0},{16,24},{24,16},{1,9},{9,1},{17,25},{25,17},{2,10},{10... | collective-permute-start | bytes 638984 | tf_op jit(solution)/shard_map/ppermute | solution.py:412
  15.3 14.6 %collective-permute-start.2 = (bf16[416,256]{1,0:T(8,128)(2,1)S(1)}, bf16[416,256]{1,0:T(8,128)(2,1)S(1)}, u32[]{:S(2)}, u32[]{:S(2)}) collective-permute-start(bf16[416,256]{1,0:T(8,128)(2,1)S(1)} %get-tuple-element.34), channel_id=1, source_target_pairs={{0,16},{8,24},{16,0},{24,8},{1,17},{9,25},{17,1},{25,9},{2,18},{10... | collective-permute-start | bytes 638984 | tf_op jit(solution)/shard_map/ppermute | solution.py:412
  16.6 1.1 %copy-start.5 = (s32[1,4]{1,0:T(1,128)S(1)}, s32[1,4]{1,0:T(1,128)}, u32[]{:S(2)}) copy-start(s32[1,4]{1,0:T(1,128)} %bounds.3) | copy-start | bytes 52
  16.6 13.7 %collective-permute-start.3 = (bf16[416,256]{1,0:T(8,128)(2,1)S(1)}, bf16[416,256]{1,0:T(8,128)(2,1)S(1)}, u32[]{:S(2)}, u32[]{:S(2)}) collective-permute-start(bf16[416,256]{1,0:T(8,128)(2,1)S(1)} %get-tuple-element.35), channel_id=1, source_target_pairs={{0,24},{8,16},{16,8},{24,0},{1,25},{9,17},{17,9},{25,1},{2,26},{10... | collective-permute-start | bytes 638984 | tf_op jit(solution)/shard_map/ppermute | solution.py:412
  23.2 15.7 %collective-permute-start.14 = (bf16[288,256]{1,0:T(8,128)(2,1)S(1)}, bf16[288,256]{1,0:T(8,128)(2,1)S(1)}, u32[]{:S(2)}, u32[]{:S(2)}) collective-permute-start(bf16[288,256]{1,0:T(8,128)(2,1)S(1)} %get-tuple-element.47), channel_id=1, source_target_pairs={{0,7},{1,0},{2,1},{3,2},{4,3},{5,4},{6,5},{7,6},{8,15},{9,8},{10,9... | collective-permute-start | bytes 442376 | tf_op jit(solution)/shard_map/ppermute | solution.py:420
  27.0 12.4 %collective-permute-start.15 = (bf16[288,256]{1,0:T(8,128)(2,1)S(1)}, bf16[288,256]{1,0:T(8,128)(2,1)S(1)}, u32[]{:S(2)}, u32[]{:S(2)}) collective-permute-start(bf16[288,256]{1,0:T(8,128)(2,1)S(1)} %get-tuple-element.48), channel_id=1, source_target_pairs={{0,15},{1,8},{2,9},{3,10},{4,11},{5,12},{6,13},{7,14},{8,7},{9,0},... | collective-permute-start | bytes 442376 | tf_op jit(solution)/shard_map/ppermute | solution.py:420
  28.9 11.1 %collective-permute-start.16 = (bf16[288,256]{1,0:T(8,128)(2,1)S(1)}, bf16[288,256]{1,0:T(8,128)(2,1)S(1)}, u32[]{:S(2)}, u32[]{:S(2)}) collective-permute-start(bf16[288,256]{1,0:T(8,128)(2,1)S(1)} %get-tuple-element.49), channel_id=1, source_target_pairs={{0,23},{1,16},{2,17},{3,18},{4,19},{5,20},{6,21},{7,22},{8,31},{9,... | collective-permute-start | bytes 442376 | tf_op jit(solution)/shard_map/ppermute | solution.py:420
  29.9 11.0 %collective-permute-start.17 = (bf16[288,256]{1,0:T(8,128)(2,1)S(1)}, bf16[288,256]{1,0:T(8,128)(2,1)S(1)}, u32[]{:S(2)}, u32[]{:S(2)}) collective-permute-start(bf16[288,256]{1,0:T(8,128)(2,1)S(1)} %get-tuple-element.50), channel_id=1, source_target_pairs={{0,31},{1,24},{2,25},{3,26},{4,27},{5,28},{6,29},{7,30},{8,23},{9,... | collective-permute-start | bytes 442376 | tf_op jit(solution)/shard_map/ppermute | solution.py:420
  35.8 6.0 %collective-permute-start.4 = (bf16[288,256]{1,0:T(8,128)(2,1)S(1)}, bf16[288,256]{1,0:T(8,128)(2,1)S(1)}, u32[]{:S(2)}, u32[]{:S(2)}) collective-permute-start(bf16[288,256]{1,0:T(8,128)(2,1)S(1)} %get-tuple-element.36), channel_id=1, source_target_pairs={{0,7},{1,0},{2,1},{3,2},{4,3},{5,4},{6,5},{7,6},{8,15},{9,8},{10,9... | collective-permute-start | bytes 442376 | tf_op jit(solution)/shard_map/ppermute | solution.py:420
  38.9 5.6 %collective-permute-start.5 = (bf16[288,256]{1,0:T(8,128)(2,1)S(1)}, bf16[288,256]{1,0:T(8,128)(2,1)S(1)}, u32[]{:S(2)}, u32[]{:S(2)}) collective-permute-start(bf16[288,256]{1,0:T(8,128)(2,1)S(1)} %get-tuple-element.37), channel_id=1, source_target_pairs={{0,15},{1,8},{2,9},{3,10},{4,11},{5,12},{6,13},{7,14},{8,7},{9,0},... | collective-permute-start | bytes 442376 | tf_op jit(solution)/shard_map/ppermute | solution.py:420
  39.4 5.6 %collective-permute-start.6 = (bf16[288,256]{1,0:T(8,128)(2,1)S(1)}, bf16[288,256]{1,0:T(8,128)(2,1)S(1)}, u32[]{:S(2)}, u32[]{:S(2)}) collective-permute-start(bf16[288,256]{1,0:T(8,128)(2,1)S(1)} %get-tuple-element.38), channel_id=1, source_target_pairs={{0,23},{1,16},{2,17},{3,18},{4,19},{5,20},{6,21},{7,22},{8,31},{9,... | collective-permute-start | bytes 442376 | tf_op jit(solution)/shard_map/ppermute | solution.py:420
  40.0 8.6 %collective-permute-start.7 = (bf16[288,256]{1,0:T(8,128)(2,1)S(1)}, bf16[288,256]{1,0:T(8,128)(2,1)S(1)}, u32[]{:S(2)}, u32[]{:S(2)}) collective-permute-start(bf16[288,256]{1,0:T(8,128)(2,1)S(1)} %get-tuple-element.39), channel_id=1, source_target_pairs={{0,31},{1,24},{2,25},{3,26},{4,27},{5,28},{6,29},{7,30},{8,23},{9,... | collective-permute-start | bytes 442376 | tf_op jit(solution)/shard_map/ppermute | solution.py:420

commit v3 on v2

--- a/solution.py
+++ b/solution.py
@@ -47,7 +47,7 @@
 
 
 def senders_of(count):
-    return range(0, count, max(1, count // HEADS))
+    return [p for p in (sorted(range(count), key=lambda p: -bin(p).count('1'))) if p % max(1, count // HEADS) == 0]
 
 
 def pack_kernel(count, phase, q_ref, k_ref, v_ref, gate_ref, *rest):
@@ -158,10 +158,10 @@
 
 def attend_kernel(count, phase, bounds, taps_ref, *rest):
     senders = senders_of(count)
-    packed, rest = rest[:count], rest[count:]
+    packed, rest = dict(zip((sorted(range(count), key=lambda p: -bin(p).count('1'))), rest)), rest[count:]
     grads, base = packed, ROWS
     if phase == 0:
-        grads, base, rest = rest[:count], 0, rest[count:]
+        grads, base, rest = dict(zip((sorted(range(count), key=lambda p: -bin(p).count('1'))), rest)), 0, rest[count:]
     outs = rest[: len(senders)]
     (block, grad, gates, mixed_grads, high_s, low_s, base_s, num_s, dq_s, dk_s, dv_s,
     ) = rest[len(senders) :]
@@ -203,8 +203,8 @@
 
     def spans(i, body):
         if isinstance(i, int):
-            if i > 0:
-                body(0, i)
+            for j in range(i):
+                body(j, 1)
         else:
             each(0, i, lambda j: body(j, 1))
 
@@ -215,10 +215,11 @@
         same = (col <= row) & ((col >= bound) | (row < bound))
         query_t = block[i, TOK : TOK + F] * BF16(0.25)
         query = query_t.astype(F32).T.astype(BF16)
+        query_t = query_t * BF16(2)
 
         def kernel_of(j, wide):
             base = 1.0 + nn(query, keys(j, wide))
-            return base, 0.5 * base * base + 0.5
+            return base, base * base + 1.0
 
         def weigh(high, low, value):
             value = jnp.concatenate([value, jnp.ones_like(value)], axis=1)
@@ -318,7 +319,7 @@
             window = mixed_grads[shift, pl.ds(pl.multiple_of(j * TOK, TOK), TOK + 8)]
             back += taps[shift : shift + 1] * window[shift : shift + TOK]
         out[0:TOK, DV : 2 * DV] = back.astype(BF16)
-        out[TOK : TOK + F] = (0.25 * dq_s[j]).astype(BF16)
+        out[TOK : TOK + F] = (0.5 * dq_s[j]).astype(BF16)
         out[TOK + F : TOK + 2 * F] = dk_s[:, lanes].astype(BF16)
 
 
@@ -345,7 +346,7 @@
             pltpu.VMEM((2 * DV, count * TOK), F32),
         ],
         compiler_params=params(count),
-    )(bounds, taps, *packed, *grads)
+    )(bounds, taps, *[packed[p] for p in (sorted(range(count), key=lambda p: -bin(p).count('1')))], *[grads[p] for p in (sorted(range(count), key=lambda p: -bin(p).count('1'))) if grads])
 
 
 def unpack_kernel(count, phase, *rest):

time: 50.3 us -> 48.1 us (0.956)
  the two profiles are of different devices: /device:TPU:1 before, /device:TPU:0 now
where the time goes in v3:
time: 48.1 us; the launch traced here: 47.9 us
  starting transfers between devices  24.9 us (52%)
  Pallas kernels  15.5 us (32%)
  waiting for transfers between devices  6.74 us (14%)
  between operations  0.73 us (2%)
    ppermute x9, starting transfers between devices, across(): return lax.ppermute(value, 'ctx', [(c, c ^ partner) for c in range(count)])  10.7 us
    pallas_call x2, Pallas kernels, attend(): pl.pallas_call(functools.partial(attend_kernel, count, phase), cost_estim...  10.2 us
    ppermute x8, starting transfers between devices, across_back(): return lax.ppermute(value, ('ctx', 'pipe'), pairs)  9.63 us
    ppermute x1, starting transfers between devices, on_device(): cotangent = lax.ppermute(out_grad, 'pipe', shift)  4.54 us
    ppermute x8, waiting for transfers between devices, across_back(): return lax.ppermute(value, ('ctx', 'pipe'), pairs)  3.23 us
    pallas_call x2, Pallas kernels, pack(): pl.pallas_call(functools.partial(pack_kernel, count, phase), cost_estimat...  2.83 us
    pallas_call x2, Pallas kernels, unpack(): pl.pallas_call(functools.partial(unpack_kernel, count, phase), cost_estim...  2.38 us
    ppermute x9, waiting for transfers between devices, across(): return lax.ppermute(value, 'ctx', [(c, c ^ partner) for c in range(count)])  2.22 us
  transfers between devices with their start and end apart: 18, of which 5 were waited for; matrix products, arithmetic and copies ran while one was open for 0% of the time, Pallas kernels for 29%

profile of v3, /device:TPU:0, one launch (start us, length us, event | category | flops | bytes accessed | tf_op | source)
XLA Modules:
  0.0 47.9 jit_solution(1986137281038993682)
XLA Ops:
  0.6 4.5 %collective-permute-start = (bf16[1,256,1024]{2,1,0:T(8,128)(2,1)}, bf16[1,256,1024]{2,1,0:T(8,128)(2,1)S(1)}, u32[]{:S(2)}, u32[]{:S(2)}) collective-permute-start(bf16[1,256,1024]{2,1,0:T(8,128)(2,1)} %param.11), channel_id=1, source_target_pairs={{0,7},{1,0},{2,1},{3,2},{4,3},{5,4},{6,5},{7,6},{8,15},{9,8},{10,9... | collective-permute-start | bytes 1572872 | tf_op jit(solution)/shard_map/ppermute | solution.py:425
  5.2 2.1 %shard_map.105 = (bf16[288,256]{1,0:T(8,128)(2,1)}, bf16[288,256]{1,0:T(8,128)(2,1)}, bf16[288,256]{1,0:T(8,128)(2,1)}, bf16[288,256]{1,0:T(8,128)(2,1)}) custom-call(bf16[1,256,128]{2,1,0:T(8,128)(2,1)} %q_ref.3, bf16[1,256,128]{2,1,0:T(8,128)(2,1)} %k_ref.3, bf16[1,256,1024]{2,1,0:T(8,128)(2,1)} %v_ref.3, bf16[1,256,1024]{2,1,0:T(8,128)(2,1)} %gate_ref.3), custom_call_target="tpu_custom_call" | custom-call | flops 2000000000 | bytes 6000000 | tf_op jit(solution)/shard_map/pallas_call | solution.py:95
  7.3 2.5 %collective-permute-start.8 = (bf16[288,256]{1,0:T(8,128)(2,1)}, bf16[288,256]{1,0:T(8,128)(2,1)S(1)}, u32[]{:S(2)}, u32[]{:S(2)}) collective-permute-start(bf16[288,256]{1,0:T(8,128)(2,1)} %get-tuple-element.40), channel_id=1, source_target_pairs={{0,24},{8,16},{16,8},{24,0},{1,25},{9,17},{17,9},{25,1},{2,26},{10... | collective-permute-start | bytes 442376 | tf_op jit(solution)/shard_map/ppermute | solution.py:413
  9.8 0.5 %collective-permute-start.9 = (bf16[288,256]{1,0:T(8,128)(2,1)}, bf16[288,256]{1,0:T(8,128)(2,1)S(1)}, u32[]{:S(2)}, u32[]{:S(2)}) collective-permute-start(bf16[288,256]{1,0:T(8,128)(2,1)} %get-tuple-element.41), channel_id=1, source_target_pairs={{0,8},{8,0},{16,24},{24,16},{1,9},{9,1},{17,25},{25,17},{2,10},{10... | collective-permute-start | bytes 442376 | tf_op jit(solution)/shard_map/ppermute | solution.py:413
  10.3 0.6 %collective-permute-start.10 = (bf16[288,256]{1,0:T(8,128)(2,1)}, bf16[288,256]{1,0:T(8,128)(2,1)S(1)}, u32[]{:S(2)}, u32[]{:S(2)}) collective-permute-start(bf16[288,256]{1,0:T(8,128)(2,1)} %get-tuple-element.42), channel_id=1, source_target_pairs={{0,16},{8,24},{16,0},{24,8},{1,17},{9,25},{17,1},{25,9},{2,18},{10... | collective-permute-start | bytes 442376 | tf_op jit(solution)/shard_map/ppermute | solution.py:413
  10.9 1.3 %collective-permute-done.grad_ref.rest_0_ = bf16[1,256,1024]{2,1,0:T(8,128)(2,1)S(1)} collective-permute-done((bf16[1,256,1024]{2,1,0:T(8,128)(2,1)}, bf16[1,256,1024]{2,1,0:T(8,128)(2,1)S(1)}, u32[]{:S(2)}, u32[]{:S(2)}) %collective-permute-start) | collective-permute-done | bytes 524320 | tf_op jit(solution)/shard_map/ppermute | solution.py:425
  12.2 0.1 shard_map.102
  12.3 2.5 %collective-permute-start.11 = (bf16[128,256]{1,0:T(8,128)(2,1)S(1)}, bf16[128,256]{1,0:T(8,128)(2,1)S(1)}, u32[]{:S(2)}, u32[]{:S(2)}) collective-permute-start(bf16[128,256]{1,0:T(8,128)(2,1)S(1)} %get-tuple-element.44), channel_id=1, source_target_pairs={{0,24},{8,16},{16,8},{24,0},{1,25},{9,17},{17,9},{25,1},{2,26},{10... | collective-permute-start | bytes 196616 | tf_op jit(solution)/shard_map/ppermute | solution.py:413
  14.8 0.5 %collective-permute-start.12 = (bf16[128,256]{1,0:T(8,128)(2,1)S(1)}, bf16[128,256]{1,0:T(8,128)(2,1)S(1)}, u32[]{:S(2)}, u32[]{:S(2)}) collective-permute-start(bf16[128,256]{1,0:T(8,128)(2,1)S(1)} %get-tuple-element.45), channel_id=1, source_target_pairs={{0,8},{8,0},{16,24},{24,16},{1,9},{9,1},{17,25},{25,17},{2,10},{10... | collective-permute-start | bytes 196616 | tf_op jit(solution)/shard_map/ppermute | solution.py:413
  15.3 0.0 collective-permute-done.8.rest_0_
  15.3 0.5 %collective-permute-start.13 = (bf16[128,256]{1,0:T(8,128)(2,1)S(1)}, bf16[128,256]{1,0:T(8,128)(2,1)S(1)}, u32[]{:S(2)}, u32[]{:S(2)}) collective-permute-start(bf16[128,256]{1,0:T(8,128)(2,1)S(1)} %get-tuple-element.46), channel_id=1, source_target_pairs={{0,16},{8,24},{16,0},{24,8},{1,17},{9,25},{17,1},{25,9},{2,18},{10... | collective-permute-start | bytes 196616 | tf_op jit(solution)/shard_map/ppermute | solution.py:413
  15.8 0.0 copy-done
  15.8 0.0 copy-done.2
  15.8 0.0 copy-start.4
  15.8 0.0 copy-start.6
  15.9 0.7 %shard_map.103 = (bf16[416,256]{1,0:T(8,128)(2,1)S(1)}, bf16[416,256]{1,0:T(8,128)(2,1)S(1)}, bf16[416,256]{1,0:T(8,128)(2,1)S(1)}, bf16[416,256]{1,0:T(8,128)(2,1)S(1)}) custom-call(bf16[1,256,128]{2,1,0:T(8,128)(2,1)S(1)} %copy-done.2, bf16[1,256,128]{2,1,0:T(8,128)(2,1)S(1)} %copy-done.3, bf16[1,256,1024]{2,1,0:T(8,128)(2,1)S(1)} %copy-done, ...), custom_call_target="tpu_custom_call" | custom-call | flops 2000000000 | bytes 6000000 | tf_op jit(solution)/shard_map/pallas_call | solution.py:95
  16.6 0.0 collective-permute-done.9.rest_1_
  16.6 2.5 %collective-permute-start.1 = (bf16[416,256]{1,0:T(8,128)(2,1)S(1)}, bf16[416,256]{1,0:T(8,128)(2,1)S(1)}, u32[]{:S(2)}, u32[]{:S(2)}) collective-permute-start(bf16[416,256]{1,0:T(8,128)(2,1)S(1)} %get-tuple-element.32), channel_id=1, source_target_pairs={{0,24},{8,16},{16,8},{24,0},{1,25},{9,17},{17,9},{25,1},{2,26},{10... | collective-permute-start | bytes 638984 | tf_op jit(solution)/shard_map/ppermute | solution.py:413
  19.1 0.0 collective-permute-done.10.rest_2_
  19.1 0.5 %collective-permute-start.2 = (bf16[416,256]{1,0:T(8,128)(2,1)S(1)}, bf16[416,256]{1,0:T(8,128)(2,1)S(1)}, u32[]{:S(2)}, u32[]{:S(2)}) collective-permute-start(bf16[416,256]{1,0:T(8,128)(2,1)S(1)} %get-tuple-element.33), channel_id=1, source_target_pairs={{0,8},{8,0},{16,24},{24,16},{1,9},{9,1},{17,25},{25,17},{2,10},{10... | collective-permute-start | bytes 638984 | tf_op jit(solution)/shard_map/ppermute | solution.py:413
  19.7 0.0 collective-permute-done.11.rest_4_
  19.7 0.5 %collective-permute-start.3 = (bf16[416,256]{1,0:T(8,128)(2,1)S(1)}, bf16[416,256]{1,0:T(8,128)(2,1)S(1)}, u32[]{:S(2)}, u32[]{:S(2)}) collective-permute-start(bf16[416,256]{1,0:T(8,128)(2,1)S(1)} %get-tuple-element.34), channel_id=1, source_target_pairs={{0,16},{8,24},{16,0},{24,8},{1,17},{9,25},{17,1},{25,9},{2,18},{10... | collective-permute-start | bytes 638984 | tf_op jit(solution)/shard_map/ppermute | solution.py:413
  20.2 0.0 collective-permute-done.12.rest_5_
  20.2 2.0 %collective-permute-done.13.rest_6_ = bf16[128,256]{1,0:T(8,128)(2,1)S(1)} collective-permute-done((bf16[128,256]{1,0:T(8,128)(2,1)S(1)}, bf16[128,256]{1,0:T(8,128)(2,1)S(1)}, u32[]{:S(2)}, u32[]{:S(2)}) %collective-permute-start.13) | collective-permute-done | bytes 65568 | tf_op jit(solution)/shard_map/ppermute | solution.py:413
  22.2 0.0 copy-done.4
  22.2 5.1 %shard_map.106 = (bf16[288,256]{1,0:T(8,128)(2,1)S(1)}, bf16[288,256]{1,0:T(8,128)(2,1)S(1)}, bf16[288,256]{1,0:T(8,128)(2,1)S(1)}, bf16[288,256]{1,0:T(8,128)(2,1)S(1)}) custom-call(s32[1,4]{1,0:T(1,128)S(1)} %copy-done.5, bf16[1,3,1024]{2,1,0:T(4,128)(2,1)S(1)} %copy-done.4, bf16[288,256]{1,0:T(8,128)(2,1)S(1)} %collective-permute-done.8.rest_0_, ...), custom_call_target="tpu_custom_call" | custom-call | flops 5000000000 | bytes 15000000 | tf_op jit(solution)/shard_map/pallas_call | solution.py:329
  27.4 1.8 %collective-permute-start.14 = (bf16[288,256]{1,0:T(8,128)(2,1)S(1)}, bf16[288,256]{1,0:T(8,128)(2,1)S(1)}, u32[]{:S(2)}, u32[]{:S(2)}) collective-permute-start(bf16[288,256]{1,0:T(8,128)(2,1)S(1)} %get-tuple-element.47), channel_id=1, source_target_pairs={{0,31},{1,24},{2,25},{3,26},{4,27},{5,28},{6,29},{7,30},{8,23},{9,... | collective-permute-start | bytes 442376 | tf_op jit(solution)/shard_map/ppermute | solution.py:421
  29.2 0.0 collective-permute-start.15
  29.2 0.0 collective-permute-done.1.rest_0_
  29.2 0.1 collective-permute-start.16
  29.4 0.2 collective-permute-done.2.rest_1_
  29.5 1.3 %collective-permute-start.17 = (bf16[288,256]{1,0:T(8,128)(2,1)S(1)}, bf16[288,256]{1,0:T(8,128)(2,1)S(1)}, u32[]{:S(2)}, u32[]{:S(2)}) collective-permute-start(bf16[288,256]{1,0:T(8,128)(2,1)S(1)} %get-tuple-element.50), channel_id=1, source_target_pairs={{0,7},{1,0},{2,1},{3,2},{4,3},{5,4},{6,5},{7,6},{8,15},{9,8},{10,9... | collective-permute-start | bytes 442376 | tf_op jit(solution)/shard_map/ppermute | solution.py:421
  30.8 0.0 collective-permute-done.3.rest_2_
  30.8 5.1 %shard_map.104 = (bf16[288,256]{1,0:T(8,128)(2,1)S(1)}, bf16[288,256]{1,0:T(8,128)(2,1)S(1)}, bf16[288,256]{1,0:T(8,128)(2,1)S(1)}, bf16[288,256]{1,0:T(8,128)(2,1)S(1)}) custom-call(s32[1,4]{1,0:T(1,128)S(1)} %copy-done.5, bf16[1,3,1024]{2,1,0:T(4,128)(2,1)S(1)} %copy-done.4, bf16[416,256]{1,0:T(8,128)(2,1)S(1)} %collective-permute-done.1.rest_0_, ...), custom_call_target="tpu_custom_call" | custom-call | flops 5000000000 | bytes 15000000 | tf_op jit(solution)/shard_map/pallas_call | solution.py:329
  36.0 2.1 %collective-permute-start.4 = (bf16[288,256]{1,0:T(8,128)(2,1)S(1)}, bf16[288,256]{1,0:T(8,128)(2,1)S(1)}, u32[]{:S(2)}, u32[]{:S(2)}) collective-permute-start(bf16[288,256]{1,0:T(8,128)(2,1)S(1)} %get-tuple-element.36), channel_id=1, source_target_pairs={{0,31},{1,24},{2,25},{3,26},{4,27},{5,28},{6,29},{7,30},{8,23},{9,... | collective-permute-start | bytes 442376 | tf_op jit(solution)/shard_map/ppermute | solution.py:421
  38.0 0.0 collective-permute-done.14.rest_0_
  38.0 0.3 collective-permute-start.5
  38.4 0.0 collective-permute-done.15.rest_1_
  38.4 1.0 %collective-permute-start.6 = (bf16[288,256]{1,0:T(8,128)(2,1)S(1)}, bf16[288,256]{1,0:T(8,128)(2,1)S(1)}, u32[]{:S(2)}, u32[]{:S(2)}) collective-permute-start(bf16[288,256]{1,0:T(8,128)(2,1)S(1)} %get-tuple-element.38), channel_id=1, source_target_pairs={{0,23},{1,16},{2,17},{3,18},{4,19},{5,20},{6,21},{7,22},{8,31},{9,... | collective-permute-start | bytes 442376 | tf_op jit(solution)/shard_map/ppermute | solution.py:421
  39.4 0.0 collective-permute-done.16.rest_2_
  39.4 2.9 %collective-permute-start.7 = (bf16[288,256]{1,0:T(8,128)(2,1)S(1)}, bf16[288,256]{1,0:T(8,128)(2,1)S(1)}, u32[]{:S(2)}, u32[]{:S(2)}) collective-permute-start(bf16[288,256]{1,0:T(8,128)(2,1)S(1)} %get-tuple-element.39), channel_id=1, source_target_pairs={{0,7},{1,0},{2,1},{3,2},{4,3},{5,4},{6,5},{7,6},{8,15},{9,8},{10,9... | collective-permute-start | bytes 442376 | tf_op jit(solution)/shard_map/ppermute | solution.py:421
  42.3 0.0 collective-permute-done.17.rest_3_
  42.3 0.8 %shard_map.107 = (bf16[1,256,1024]{2,1,0:T(8,128)(2,1)}, bf16[1,256,1024]{2,1,0:T(8,128)(2,1)}, bf16[2,128,256]{2,1,0:T(8,128)(2,1)S(1)}) custom-call(bf16[288,256]{1,0:T(8,128)(2,1)S(1)} %collective-permute-done.14.rest_0_, bf16[288,256]{1,0:T(8,128)(2,1)S(1)} %collective-permute-done.15.rest_1_, bf16[288,256]{1,0:T(8,128)(2,1)S(1)} %collective-permute-done.16.rest_2_, ...), custom_call_target="tpu_custom_call" | custom-call | flops 1000000000 | bytes 3000000 | tf_op jit(solution)/shard_map/pallas_call | solution.py:394
  43.2 1.9 %collective-permute-done.4.rest_0_ = bf16[288,256]{1,0:T(8,128)(2,1)S(1)} collective-permute-done((bf16[288,256]{1,0:T(8,128)(2,1)S(1)}, bf16[288,256]{1,0:T(8,128)(2,1)S(1)}, u32[]{:S(2)}, u32[]{:S(2)}) %collective-permute-start.4) | collective-permute-done | bytes 147488 | tf_op jit(solution)/shard_map/ppermute | solution.py:421
  45.1 1.3 %collective-permute-done.5.rest_1_ = bf16[288,256]{1,0:T(8,128)(2,1)S(1)} collective-permute-done((bf16[288,256]{1,0:T(8,128)(2,1)S(1)}, bf16[288,256]{1,0:T(8,128)(2,1)S(1)}, u32[]{:S(2)}, u32[]{:S(2)}) %collective-permute-start.5) | collective-permute-done | bytes 147488 | tf_op jit(solution)/shard_map/ppermute | solution.py:421
  46.4 0.0 collective-permute-done.6.rest_2_
  46.4 0.0 collective-permute-done.7.rest_3_
  46.4 1.5 %shard_map.108 = (bf16[1,256,1024]{2,1,0:T(8,128)(2,1)}, bf16[1,256,1024]{2,1,0:T(8,128)(2,1)}, bf16[1,256,128]{2,1,0:T(8,128)(2,1)}, bf16[1,256,128]{2,1,0:T(8,128)(2,1)}) custom-call(bf16[288,256]{1,0:T(8,128)(2,1)S(1)} %collective-permute-done.4.rest_0_, ...), custom_call_target="tpu_custom_call", output_to_operand_aliasing={{0}: (5, {}), {1}: (6, {})} | custom-call | flops 1000000000 | bytes 3000000 | tf_op jit(solution)/shard_map/pallas_call | solution.py:394
  (9 shorter events, 0.0 us)
Async XLA Ops:
  0.6 11.6 %collective-permute-start = (bf16[1,256,1024]{2,1,0:T(8,128)(2,1)}, bf16[1,256,1024]{2,1,0:T(8,128)(2,1)S(1)}, u32[]{:S(2)}, u32[]{:S(2)}) collective-permute-start(bf16[1,256,1024]{2,1,0:T(8,128)(2,1)} %param.11), channel_id=1, source_target_pairs={{0,7},{1,0},{2,1},{3,2},{4,3},{5,4},{6,5},{7,6},{8,15},{9,8},{10,9... | collective-permute-start | bytes 1572872 | tf_op jit(solution)/shard_map/ppermute | solution.py:425
  7.3 8.0 %collective-permute-start.8 = (bf16[288,256]{1,0:T(8,128)(2,1)}, bf16[288,256]{1,0:T(8,128)(2,1)S(1)}, u32[]{:S(2)}, u32[]{:S(2)}) collective-permute-start(bf16[288,256]{1,0:T(8,128)(2,1)} %get-tuple-element.40), channel_id=1, source_target_pairs={{0,24},{8,16},{16,8},{24,0},{1,25},{9,17},{17,9},{25,1},{2,26},{10... | collective-permute-start | bytes 442376 | tf_op jit(solution)/shard_map/ppermute | solution.py:413
  9.8 6.8 %collective-permute-start.9 = (bf16[288,256]{1,0:T(8,128)(2,1)}, bf16[288,256]{1,0:T(8,128)(2,1)S(1)}, u32[]{:S(2)}, u32[]{:S(2)}) collective-permute-start(bf16[288,256]{1,0:T(8,128)(2,1)} %get-tuple-element.41), channel_id=1, source_target_pairs={{0,8},{8,0},{16,24},{24,16},{1,9},{9,1},{17,25},{25,17},{2,10},{10... | collective-permute-start | bytes 442376 | tf_op jit(solution)/shard_map/ppermute | solution.py:413
  10.3 5.5 %copy-start = (bf16[1,256,1024]{2,1,0:T(8,128)(2,1)S(1)}, bf16[1,256,1024]{2,1,0:T(8,128)(2,1)}, u32[]{:S(2)}) copy-start(bf16[1,256,1024]{2,1,0:T(8,128)(2,1)} %v_ref.3) | copy-start | bytes 1572868
  10.3 5.5 %copy-start.1 = (bf16[1,256,1024]{2,1,0:T(8,128)(2,1)S(1)}, bf16[1,256,1024]{2,1,0:T(8,128)(2,1)}, u32[]{:S(2)}) copy-start(bf16[1,256,1024]{2,1,0:T(8,128)(2,1)} %gate_ref.3) | copy-start | bytes 1572868
  10.3 5.5 %copy-start.2 = (bf16[1,256,128]{2,1,0:T(8,128)(2,1)S(1)}, bf16[1,256,128]{2,1,0:T(8,128)(2,1)}, u32[]{:S(2)}) copy-start(bf16[1,256,128]{2,1,0:T(8,128)(2,1)} %q_ref.3) | copy-start | bytes 196612
  10.3 5.5 %copy-start.3 = (bf16[1,256,128]{2,1,0:T(8,128)(2,1)S(1)}, bf16[1,256,128]{2,1,0:T(8,128)(2,1)}, u32[]{:S(2)}) copy-start(bf16[1,256,128]{2,1,0:T(8,128)(2,1)} %k_ref.3) | copy-start | bytes 196612
  10.3 8.8 %collective-permute-start.10 = (bf16[288,256]{1,0:T(8,128)(2,1)}, bf16[288,256]{1,0:T(8,128)(2,1)S(1)}, u32[]{:S(2)}, u32[]{:S(2)}) collective-permute-start(bf16[288,256]{1,0:T(8,128)(2,1)} %get-tuple-element.42), channel_id=1, source_target_pairs={{0,16},{8,24},{16,0},{24,8},{1,17},{9,25},{17,1},{25,9},{2,18},{10... | collective-permute-start | bytes 442376 | tf_op jit(solution)/shard_map/ppermute | solution.py:413
  12.3 7.4 %collective-permute-start.11 = (bf16[128,256]{1,0:T(8,128)(2,1)S(1)}, bf16[128,256]{1,0:T(8,128)(2,1)S(1)}, u32[]{:S(2)}, u32[]{:S(2)}) collective-permute-start(bf16[128,256]{1,0:T(8,128)(2,1)S(1)} %get-tuple-element.44), channel_id=1, source_target_pairs={{0,24},{8,16},{16,8},{24,0},{1,25},{9,17},{17,9},{25,1},{2,26},{10... | collective-permute-start | bytes 196616 | tf_op jit(solution)/shard_map/ppermute | solution.py:413
  14.8 5.4 %collective-permute-start.12 = (bf16[128,256]{1,0:T(8,128)(2,1)S(1)}, bf16[128,256]{1,0:T(8,128)(2,1)S(1)}, u32[]{:S(2)}, u32[]{:S(2)}) collective-permute-start(bf16[128,256]{1,0:T(8,128)(2,1)S(1)} %get-tuple-element.45), channel_id=1, source_target_pairs={{0,8},{8,0},{16,24},{24,16},{1,9},{9,1},{17,25},{25,17},{2,10},{10... | collective-permute-start | bytes 196616 | tf_op jit(solution)/shard_map/ppermute | solution.py:413
  15.3 6.9 %collective-permute-start.13 = (bf16[128,256]{1,0:T(8,128)(2,1)S(1)}, bf16[128,256]{1,0:T(8,128)(2,1)S(1)}, u32[]{:S(2)}, u32[]{:S(2)}) collective-permute-start(bf16[128,256]{1,0:T(8,128)(2,1)S(1)} %get-tuple-element.46), channel_id=1, source_target_pairs={{0,16},{8,24},{16,0},{24,8},{1,17},{9,25},{17,1},{25,9},{2,18},{10... | collective-permute-start | bytes 196616 | tf_op jit(solution)/shard_map/ppermute | solution.py:413
  15.8 6.4 %copy-start.4 = (bf16[1,3,1024]{2,1,0:T(4,128)(2,1)S(1)}, bf16[1,3,1024]{2,1,0:T(4,128)(2,1)}, u32[]{:S(2)}) copy-start(bf16[1,3,1024]{2,1,0:T(4,128)(2,1)} %taps_ref.3) | copy-start | bytes 18436
  15.8 6.4 %copy-start.6 = (bf16[288,256]{1,0:T(8,128)(2,1)S(1)}, bf16[288,256]{1,0:T(8,128)(2,1)}, u32[]{:S(2)}) copy-start(bf16[288,256]{1,0:T(8,128)(2,1)} %get-tuple-element.43.rest_3_) | copy-start | bytes 442372
  16.6 12.6 %collective-permute-start.1 = (bf16[416,256]{1,0:T(8,128)(2,1)S(1)}, bf16[416,256]{1,0:T(8,128)(2,1)S(1)}, u32[]{:S(2)}, u32[]{:S(2)}) collective-permute-start(bf16[416,256]{1,0:T(8,128)(2,1)S(1)} %get-tuple-element.32), channel_id=1, source_target_pairs={{0,24},{8,16},{16,8},{24,0},{1,25},{9,17},{17,9},{25,1},{2,26},{10... | collective-permute-start | bytes 638984 | tf_op jit(solution)/shard_map/ppermute | solution.py:413
  19.1 10.4 %collective-permute-start.2 = (bf16[416,256]{1,0:T(8,128)(2,1)S(1)}, bf16[416,256]{1,0:T(8,128)(2,1)S(1)}, u32[]{:S(2)}, u32[]{:S(2)}) collective-permute-start(bf16[416,256]{1,0:T(8,128)(2,1)S(1)} %get-tuple-element.33), channel_id=1, source_target_pairs={{0,8},{8,0},{16,24},{24,16},{1,9},{9,1},{17,25},{25,17},{2,10},{10... | collective-permute-start | bytes 638984 | tf_op jit(solution)/shard_map/ppermute | solution.py:413
  19.7 2.6 %copy-start.5 = (s32[1,4]{1,0:T(1,128)S(1)}, s32[1,4]{1,0:T(1,128)}, u32[]{:S(2)}) copy-start(s32[1,4]{1,0:T(1,128)} %bounds.3) | copy-start | bytes 52
  19.7 11.2 %collective-permute-start.3 = (bf16[416,256]{1,0:T(8,128)(2,1)S(1)}, bf16[416,256]{1,0:T(8,128)(2,1)S(1)}, u32[]{:S(2)}, u32[]{:S(2)}) collective-permute-start(bf16[416,256]{1,0:T(8,128)(2,1)S(1)} %get-tuple-element.34), channel_id=1, source_target_pairs={{0,16},{8,24},{16,0},{24,8},{1,17},{9,25},{17,1},{25,9},{2,18},{10... | collective-permute-start | bytes 638984 | tf_op jit(solution)/shard_map/ppermute | solution.py:413
  27.4 10.7 %collective-permute-start.14 = (bf16[288,256]{1,0:T(8,128)(2,1)S(1)}, bf16[288,256]{1,0:T(8,128)(2,1)S(1)}, u32[]{:S(2)}, u32[]{:S(2)}) collective-permute-start(bf16[288,256]{1,0:T(8,128)(2,1)S(1)} %get-tuple-element.47), channel_id=1, source_target_pairs={{0,31},{1,24},{2,25},{3,26},{4,27},{5,28},{6,29},{7,30},{8,23},{9,... | collective-permute-start | bytes 442376 | tf_op jit(solution)/shard_map/ppermute | solution.py:421
  29.2 9.2 %collective-permute-start.15 = (bf16[288,256]{1,0:T(8,128)(2,1)S(1)}, bf16[288,256]{1,0:T(8,128)(2,1)S(1)}, u32[]{:S(2)}, u32[]{:S(2)}) collective-permute-start(bf16[288,256]{1,0:T(8,128)(2,1)S(1)} %get-tuple-element.48), channel_id=1, source_target_pairs={{0,15},{1,8},{2,9},{3,10},{4,11},{5,12},{6,13},{7,14},{8,7},{9,0},... | collective-permute-start | bytes 442376 | tf_op jit(solution)/shard_map/ppermute | solution.py:421
  29.2 10.2 %collective-permute-start.16 = (bf16[288,256]{1,0:T(8,128)(2,1)S(1)}, bf16[288,256]{1,0:T(8,128)(2,1)S(1)}, u32[]{:S(2)}, u32[]{:S(2)}) collective-permute-start(bf16[288,256]{1,0:T(8,128)(2,1)S(1)} %get-tuple-element.49), channel_id=1, source_target_pairs={{0,23},{1,16},{2,17},{3,18},{4,19},{5,20},{6,21},{7,22},{8,31},{9,... | collective-permute-start | bytes 442376 | tf_op jit(solution)/shard_map/ppermute | solution.py:421
  29.5 12.8 %collective-permute-start.17 = (bf16[288,256]{1,0:T(8,128)(2,1)S(1)}, bf16[288,256]{1,0:T(8,128)(2,1)S(1)}, u32[]{:S(2)}, u32[]{:S(2)}) collective-permute-start(bf16[288,256]{1,0:T(8,128)(2,1)S(1)} %get-tuple-element.50), channel_id=1, source_target_pairs={{0,7},{1,0},{2,1},{3,2},{4,3},{5,4},{6,5},{7,6},{8,15},{9,8},{10,9... | collective-permute-start | bytes 442376 | tf_op jit(solution)/shard_map/ppermute | solution.py:421
  36.0 9.1 %collective-permute-start.4 = (bf16[288,256]{1,0:T(8,128)(2,1)S(1)}, bf16[288,256]{1,0:T(8,128)(2,1)S(1)}, u32[]{:S(2)}, u32[]{:S(2)}) collective-permute-start(bf16[288,256]{1,0:T(8,128)(2,1)S(1)} %get-tuple-element.36), channel_id=1, source_target_pairs={{0,31},{1,24},{2,25},{3,26},{4,27},{5,28},{6,29},{7,30},{8,23},{9,... | collective-permute-start | bytes 442376 | tf_op jit(solution)/shard_map/ppermute | solution.py:421
  38.0 8.3 %collective-permute-start.5 = (bf16[288,256]{1,0:T(8,128)(2,1)S(1)}, bf16[288,256]{1,0:T(8,128)(2,1)S(1)}, u32[]{:S(2)}, u32[]{:S(2)}) collective-permute-start(bf16[288,256]{1,0:T(8,128)(2,1)S(1)} %get-tuple-element.37), channel_id=1, source_target_pairs={{0,15},{1,8},{2,9},{3,10},{4,11},{5,12},{6,13},{7,14},{8,7},{9,0},... | collective-permute-start | bytes 442376 | tf_op jit(solution)/shard_map/ppermute | solution.py:421
  38.4 8.0 %collective-permute-start.6 = (bf16[288,256]{1,0:T(8,128)(2,1)S(1)}, bf16[288,256]{1,0:T(8,128)(2,1)S(1)}, u32[]{:S(2)}, u32[]{:S(2)}) collective-permute-start(bf16[288,256]{1,0:T(8,128)(2,1)S(1)} %get-tuple-element.38), channel_id=1, source_target_pairs={{0,23},{1,16},{2,17},{3,18},{4,19},{5,20},{6,21},{7,22},{8,31},{9,... | collective-permute-start | bytes 442376 | tf_op jit(solution)/shard_map/ppermute | solution.py:421
  39.4 7.0 %collective-permute-start.7 = (bf16[288,256]{1,0:T(8,128)(2,1)S(1)}, bf16[288,256]{1,0:T(8,128)(2,1)S(1)}, u32[]{:S(2)}, u32[]{:S(2)}) collective-permute-start(bf16[288,256]{1,0:T(8,128)(2,1)S(1)} %get-tuple-element.39), channel_id=1, source_target_pairs={{0,7},{1,0},{2,1},{3,2},{4,3},{5,4},{6,5},{7,6},{8,15},{9,8},{10,9... | collective-permute-start | bytes 442376 | tf_op jit(solution)/shard_map/ppermute | solution.py:421

commit v4 on v3

--- a/solution.py
+++ b/solution.py
@@ -46,8 +46,12 @@
     return max(1, HEADS // count)
 
 
+def far_first(count):
+    return sorted(range(count), key=lambda partner: -bin(partner).count("1"))
+
+
 def senders_of(count):
-    return [p for p in (sorted(range(count), key=lambda p: -bin(p).count('1'))) if p % max(1, count // HEADS) == 0]
+    return [p for p in far_first(count) if p % max(1, count // HEADS) == 0]
 
 
 def pack_kernel(count, phase, q_ref, k_ref, v_ref, gate_ref, *rest):
@@ -158,10 +162,10 @@
 
 def attend_kernel(count, phase, bounds, taps_ref, *rest):
     senders = senders_of(count)
-    packed, rest = dict(zip((sorted(range(count), key=lambda p: -bin(p).count('1'))), rest)), rest[count:]
+    packed, rest = dict(zip(far_first(count), rest)), rest[count:]
     grads, base = packed, ROWS
     if phase == 0:
-        grads, base, rest = dict(zip((sorted(range(count), key=lambda p: -bin(p).count('1'))), rest)), 0, rest[count:]
+        grads, base, rest = dict(zip(far_first(count), rest)), 0, rest[count:]
     outs = rest[: len(senders)]
     (block, grad, gates, mixed_grads, high_s, low_s, base_s, num_s, dq_s, dk_s, dv_s,
     ) = rest[len(senders) :]
@@ -324,6 +328,9 @@
 
 
 def attend(count, phase, bounds, taps, packed, grads):
+    def in_order(blocks):
+        return [blocks[partner] for partner in far_first(count)] if blocks else []
+
     outs = len(senders_of(count))
     saved = (count * (count - 1) // 2 if count <= UNROLLED else count - 1) * TOK
     return pl.pallas_call(
@@ -346,7 +353,7 @@
             pltpu.VMEM((2 * DV, count * TOK), F32),
         ],
         compiler_params=params(count),
-    )(bounds, taps, *[packed[p] for p in (sorted(range(count), key=lambda p: -bin(p).count('1')))], *[grads[p] for p in (sorted(range(count), key=lambda p: -bin(p).count('1'))) if grads])
+    )(bounds, taps, *in_order(packed), *in_order(grads))
 
 
 def unpack_kernel(count, phase, *rest):
@@ -359,8 +366,10 @@
     if phase > 0:
         earlier, rest = rest[0], rest[3:]
     v_ref, gate_ref = rest[:2]
-    sem = rest[-1]
-    rows_ref = rest[-2] if last else rest[2]
+    if last:
+        rows_ref, flat_ref, sem_flat, sem = rest[4:]
+    else:
+        rows_ref, sem = rest[2:]
     copies = []
     for n, partner in enumerate(senders):
         head = first_head(me ^ partner, count) + phase
@@ -379,7 +388,9 @@
             rows_ref[side, rows] = arrived[n][TOK + side * F : TOK + (side + 1) * F]
     if last:
         for side, ref in enumerate(rest[2:4]):
-            ref[0] = rows_ref[side].astype(F32).T.astype(BF16)
+            flat_ref[side] = rows_ref[side].astype(F32).T.astype(BF16)
+            copies.append(pltpu.make_async_copy(flat_ref.at[side], ref.at[0], sem_flat.at[side]))
+            copies[-1].start()
     for copy in copies:
         copy.wait()
 
@@ -396,9 +407,17 @@
         cost_estimate=cost(1),
         out_shape=[wide, wide] + small,
         in_specs=[VMEM] * many + [VMEM, HBM, HBM][: len(begun)],
-        out_specs=[HBM, HBM] + [VMEM] * len(small),
+        out_specs=[HBM] * 4 if last else [HBM, HBM, VMEM],
         input_output_aliases={many + 1: 0, many + 2: 1} if begun else {},
-        scratch_shapes=([pltpu.VMEM(turned, BF16)] if last else [])
+        scratch_shapes=(
+            [
+                pltpu.VMEM(turned, BF16),
+                pltpu.VMEM((2, TOK, HEADS * F), BF16),
+                pltpu.SemaphoreType.DMA((2,)),
+            ]
+            if last
+            else []
+        )
         + [pltpu.SemaphoreType.DMA((2 * many,))],
         compiler_params=params(count),
     )(*arrived, *begun)
@@ -420,7 +439,7 @@
         ]
         return lax.ppermute(value, ("ctx", "pipe"), pairs)
 
-    order = sorted(range(count), key=lambda partner: -bin(partner).count("1"))
+    order = far_first(count)
     shift = [(s, (s - 1) % sections) for s in range(sections)]
     cotangent = lax.ppermute(out_grad, "pipe", shift)
 

time: 48.1 us -> 47.5 us (0.988)
  Pallas kernels: 15.5 us -> 14.9 us
    pallas_call x2, Pallas kernels: 2.38 us -> 1.79 us  [unpack(): pl.pallas_call(functools.partial(unpack_kernel, count, phase), cost_estim...]
  transfers between devices with their start and end apart: 18 -> 18, of which waited for: 5 -> 5; matrix products, arithmetic and copies ran while one was open for 0% -> 0% of each run, Pallas kernels for 29% -> 30%
where the time goes in v4:
time: 47.5 us; the launch traced here: 47.3 us
  starting transfers between devices  24.9 us (52%)
  Pallas kernels  14.9 us (31%)
  waiting for transfers between devices  6.74 us (14%)
  between operations  0.73 us (2%)
    ppermute x9, starting transfers between devices, across(): return lax.ppermute(value, 'ctx', [(c, c ^ partner) for c in range(count)])  10.7 us
    pallas_call x2, Pallas kernels, attend(): pl.pallas_call(functools.partial(attend_kernel, count, phase), cost_estim...  10.2 us
    ppermute x8, starting transfers between devices, across_back(): return lax.ppermute(value, ('ctx', 'pipe'), pairs)  9.63 us
    ppermute x1, starting transfers between devices, on_device(): cotangent = lax.ppermute(out_grad, 'pipe', shift)  4.54 us
    ppermute x8, waiting for transfers between devices, across_back(): return lax.ppermute(value, ('ctx', 'pipe'), pairs)  3.23 us
    pallas_call x2, Pallas kernels, pack(): pl.pallas_call(functools.partial(pack_kernel, count, phase), cost_estimat...  2.83 us
    ppermute x9, waiting for transfers between devices, across(): return lax.ppermute(value, 'ctx', [(c, c ^ partner) for c in range(count)])  2.22 us
    pallas_call x2, Pallas kernels, unpack(): pl.pallas_call(functools.partial(unpack_kernel, count, phase), cost_estim...  1.79 us
  transfers between devices with their start and end apart: 18, of which 5 were waited for; matrix products, arithmetic and copies ran while one was open for 0% of the time, Pallas kernels for 30%

profile of v4, /device:TPU:0, one launch (start us, length us, event | category | flops | bytes accessed | tf_op | source)
XLA Modules:
  0.0 47.3 jit_solution(13170535086049853543)
XLA Ops:
  0.6 4.5 %collective-permute-start = (bf16[1,256,1024]{2,1,0:T(8,128)(2,1)}, bf16[1,256,1024]{2,1,0:T(8,128)(2,1)S(1)}, u32[]{:S(2)}, u32[]{:S(2)}) collective-permute-start(bf16[1,256,1024]{2,1,0:T(8,128)(2,1)} %param.11), channel_id=1, source_target_pairs={{0,7},{1,0},{2,1},{3,2},{4,3},{5,4},{6,5},{7,6},{8,15},{9,8},{10,9... | collective-permute-start | bytes 1572872 | tf_op jit(solution)/shard_map/ppermute | solution.py:444
  5.2 2.1 %shard_map.105 = (bf16[288,256]{1,0:T(8,128)(2,1)}, bf16[288,256]{1,0:T(8,128)(2,1)}, bf16[288,256]{1,0:T(8,128)(2,1)}, bf16[288,256]{1,0:T(8,128)(2,1)}) custom-call(bf16[1,256,128]{2,1,0:T(8,128)(2,1)} %q_ref.3, bf16[1,256,128]{2,1,0:T(8,128)(2,1)} %k_ref.3, bf16[1,256,1024]{2,1,0:T(8,128)(2,1)} %v_ref.3, bf16[1,256,1024]{2,1,0:T(8,128)(2,1)} %gate_ref.3), custom_call_target="tpu_custom_call" | custom-call | flops 2000000000 | bytes 6000000 | tf_op jit(solution)/shard_map/pallas_call | solution.py:99
  7.3 2.5 %collective-permute-start.8 = (bf16[288,256]{1,0:T(8,128)(2,1)}, bf16[288,256]{1,0:T(8,128)(2,1)S(1)}, u32[]{:S(2)}, u32[]{:S(2)}) collective-permute-start(bf16[288,256]{1,0:T(8,128)(2,1)} %get-tuple-element.40), channel_id=1, source_target_pairs={{0,24},{8,16},{16,8},{24,0},{1,25},{9,17},{17,9},{25,1},{2,26},{10... | collective-permute-start | bytes 442376 | tf_op jit(solution)/shard_map/ppermute | solution.py:432
  9.8 0.5 %collective-permute-start.9 = (bf16[288,256]{1,0:T(8,128)(2,1)}, bf16[288,256]{1,0:T(8,128)(2,1)S(1)}, u32[]{:S(2)}, u32[]{:S(2)}) collective-permute-start(bf16[288,256]{1,0:T(8,128)(2,1)} %get-tuple-element.41), channel_id=1, source_target_pairs={{0,8},{8,0},{16,24},{24,16},{1,9},{9,1},{17,25},{25,17},{2,10},{10... | collective-permute-start | bytes 442376 | tf_op jit(solution)/shard_map/ppermute | solution.py:432
  10.3 0.6 %collective-permute-start.10 = (bf16[288,256]{1,0:T(8,128)(2,1)}, bf16[288,256]{1,0:T(8,128)(2,1)S(1)}, u32[]{:S(2)}, u32[]{:S(2)}) collective-permute-start(bf16[288,256]{1,0:T(8,128)(2,1)} %get-tuple-element.42), channel_id=1, source_target_pairs={{0,16},{8,24},{16,0},{24,8},{1,17},{9,25},{17,1},{25,9},{2,18},{10... | collective-permute-start | bytes 442376 | tf_op jit(solution)/shard_map/ppermute | solution.py:432
  10.9 1.3 %collective-permute-done.grad_ref.rest_0_ = bf16[1,256,1024]{2,1,0:T(8,128)(2,1)S(1)} collective-permute-done((bf16[1,256,1024]{2,1,0:T(8,128)(2,1)}, bf16[1,256,1024]{2,1,0:T(8,128)(2,1)S(1)}, u32[]{:S(2)}, u32[]{:S(2)}) %collective-permute-start) | collective-permute-done | bytes 524320 | tf_op jit(solution)/shard_map/ppermute | solution.py:444
  12.2 0.1 shard_map.102
  12.3 2.5 %collective-permute-start.11 = (bf16[128,256]{1,0:T(8,128)(2,1)S(1)}, bf16[128,256]{1,0:T(8,128)(2,1)S(1)}, u32[]{:S(2)}, u32[]{:S(2)}) collective-permute-start(bf16[128,256]{1,0:T(8,128)(2,1)S(1)} %get-tuple-element.44), channel_id=1, source_target_pairs={{0,24},{8,16},{16,8},{24,0},{1,25},{9,17},{17,9},{25,1},{2,26},{10... | collective-permute-start | bytes 196616 | tf_op jit(solution)/shard_map/ppermute | solution.py:432
  14.8 0.5 %collective-permute-start.12 = (bf16[128,256]{1,0:T(8,128)(2,1)S(1)}, bf16[128,256]{1,0:T(8,128)(2,1)S(1)}, u32[]{:S(2)}, u32[]{:S(2)}) collective-permute-start(bf16[128,256]{1,0:T(8,128)(2,1)S(1)} %get-tuple-element.45), channel_id=1, source_target_pairs={{0,8},{8,0},{16,24},{24,16},{1,9},{9,1},{17,25},{25,17},{2,10},{10... | collective-permute-start | bytes 196616 | tf_op jit(solution)/shard_map/ppermute | solution.py:432
  15.3 0.0 collective-permute-done.8.rest_0_
  15.3 0.5 %collective-permute-start.13 = (bf16[128,256]{1,0:T(8,128)(2,1)S(1)}, bf16[128,256]{1,0:T(8,128)(2,1)S(1)}, u32[]{:S(2)}, u32[]{:S(2)}) collective-permute-start(bf16[128,256]{1,0:T(8,128)(2,1)S(1)} %get-tuple-element.46), channel_id=1, source_target_pairs={{0,16},{8,24},{16,0},{24,8},{1,17},{9,25},{17,1},{25,9},{2,18},{10... | collective-permute-start | bytes 196616 | tf_op jit(solution)/shard_map/ppermute | solution.py:432
  15.8 0.0 copy-done
  15.8 0.0 copy-done.2
  15.8 0.0 copy-start.4
  15.8 0.0 copy-start.6
  15.9 0.7 %shard_map.103 = (bf16[416,256]{1,0:T(8,128)(2,1)S(1)}, bf16[416,256]{1,0:T(8,128)(2,1)S(1)}, bf16[416,256]{1,0:T(8,128)(2,1)S(1)}, bf16[416,256]{1,0:T(8,128)(2,1)S(1)}) custom-call(bf16[1,256,128]{2,1,0:T(8,128)(2,1)S(1)} %copy-done.2, bf16[1,256,128]{2,1,0:T(8,128)(2,1)S(1)} %copy-done.3, bf16[1,256,1024]{2,1,0:T(8,128)(2,1)S(1)} %copy-done, ...), custom_call_target="tpu_custom_call" | custom-call | flops 2000000000 | bytes 6000000 | tf_op jit(solution)/shard_map/pallas_call | solution.py:99
  16.6 0.0 collective-permute-done.9.rest_1_
  16.6 2.5 %collective-permute-start.1 = (bf16[416,256]{1,0:T(8,128)(2,1)S(1)}, bf16[416,256]{1,0:T(8,128)(2,1)S(1)}, u32[]{:S(2)}, u32[]{:S(2)}) collective-permute-start(bf16[416,256]{1,0:T(8,128)(2,1)S(1)} %get-tuple-element.32), channel_id=1, source_target_pairs={{0,24},{8,16},{16,8},{24,0},{1,25},{9,17},{17,9},{25,1},{2,26},{10... | collective-permute-start | bytes 638984 | tf_op jit(solution)/shard_map/ppermute | solution.py:432
  19.1 0.0 collective-permute-done.10.rest_2_
  19.1 0.5 %collective-permute-start.2 = (bf16[416,256]{1,0:T(8,128)(2,1)S(1)}, bf16[416,256]{1,0:T(8,128)(2,1)S(1)}, u32[]{:S(2)}, u32[]{:S(2)}) collective-permute-start(bf16[416,256]{1,0:T(8,128)(2,1)S(1)} %get-tuple-element.33), channel_id=1, source_target_pairs={{0,8},{8,0},{16,24},{24,16},{1,9},{9,1},{17,25},{25,17},{2,10},{10... | collective-permute-start | bytes 638984 | tf_op jit(solution)/shard_map/ppermute | solution.py:432
  19.7 0.0 collective-permute-done.11.rest_4_
  19.7 0.5 %collective-permute-start.3 = (bf16[416,256]{1,0:T(8,128)(2,1)S(1)}, bf16[416,256]{1,0:T(8,128)(2,1)S(1)}, u32[]{:S(2)}, u32[]{:S(2)}) collective-permute-start(bf16[416,256]{1,0:T(8,128)(2,1)S(1)} %get-tuple-element.34), channel_id=1, source_target_pairs={{0,16},{8,24},{16,0},{24,8},{1,17},{9,25},{17,1},{25,9},{2,18},{10... | collective-permute-start | bytes 638984 | tf_op jit(solution)/shard_map/ppermute | solution.py:432
  20.2 0.0 collective-permute-done.12.rest_5_
  20.2 2.0 %collective-permute-done.13.rest_6_ = bf16[128,256]{1,0:T(8,128)(2,1)S(1)} collective-permute-done((bf16[128,256]{1,0:T(8,128)(2,1)S(1)}, bf16[128,256]{1,0:T(8,128)(2,1)S(1)}, u32[]{:S(2)}, u32[]{:S(2)}) %collective-permute-start.13) | collective-permute-done | bytes 65568 | tf_op jit(solution)/shard_map/ppermute | solution.py:432
  22.2 0.0 copy-done.4
  22.2 5.1 %shard_map.106 = (bf16[288,256]{1,0:T(8,128)(2,1)S(1)}, bf16[288,256]{1,0:T(8,128)(2,1)S(1)}, bf16[288,256]{1,0:T(8,128)(2,1)S(1)}, bf16[288,256]{1,0:T(8,128)(2,1)S(1)}) custom-call(s32[1,4]{1,0:T(1,128)S(1)} %copy-done.5, bf16[1,3,1024]{2,1,0:T(4,128)(2,1)S(1)} %copy-done.4, bf16[288,256]{1,0:T(8,128)(2,1)S(1)} %collective-permute-done.8.rest_0_, ...), custom_call_target="tpu_custom_call" | custom-call | flops 5000000000 | bytes 15000000 | tf_op jit(solution)/shard_map/pallas_call | solution.py:336
  27.4 1.8 %collective-permute-start.14 = (bf16[288,256]{1,0:T(8,128)(2,1)S(1)}, bf16[288,256]{1,0:T(8,128)(2,1)S(1)}, u32[]{:S(2)}, u32[]{:S(2)}) collective-permute-start(bf16[288,256]{1,0:T(8,128)(2,1)S(1)} %get-tuple-element.47), channel_id=1, source_target_pairs={{0,31},{1,24},{2,25},{3,26},{4,27},{5,28},{6,29},{7,30},{8,23},{9,... | collective-permute-start | bytes 442376 | tf_op jit(solution)/shard_map/ppermute | solution.py:440
  29.2 0.0 collective-permute-start.15
  29.2 0.0 collective-permute-done.1.rest_0_
  29.2 0.1 collective-permute-start.16
  29.4 0.2 collective-permute-done.2.rest_1_
  29.5 1.3 %collective-permute-start.17 = (bf16[288,256]{1,0:T(8,128)(2,1)S(1)}, bf16[288,256]{1,0:T(8,128)(2,1)S(1)}, u32[]{:S(2)}, u32[]{:S(2)}) collective-permute-start(bf16[288,256]{1,0:T(8,128)(2,1)S(1)} %get-tuple-element.50), channel_id=1, source_target_pairs={{0,7},{1,0},{2,1},{3,2},{4,3},{5,4},{6,5},{7,6},{8,15},{9,8},{10,9... | collective-permute-start | bytes 442376 | tf_op jit(solution)/shard_map/ppermute | solution.py:440
  30.8 0.0 collective-permute-done.3.rest_2_
  30.8 5.1 %shard_map.104 = (bf16[288,256]{1,0:T(8,128)(2,1)S(1)}, bf16[288,256]{1,0:T(8,128)(2,1)S(1)}, bf16[288,256]{1,0:T(8,128)(2,1)S(1)}, bf16[288,256]{1,0:T(8,128)(2,1)S(1)}) custom-call(s32[1,4]{1,0:T(1,128)S(1)} %copy-done.5, bf16[1,3,1024]{2,1,0:T(4,128)(2,1)S(1)} %copy-done.4, bf16[416,256]{1,0:T(8,128)(2,1)S(1)} %collective-permute-done.1.rest_0_, ...), custom_call_target="tpu_custom_call" | custom-call | flops 5000000000 | bytes 15000000 | tf_op jit(solution)/shard_map/pallas_call | solution.py:336
  36.0 2.1 %collective-permute-start.4 = (bf16[288,256]{1,0:T(8,128)(2,1)S(1)}, bf16[288,256]{1,0:T(8,128)(2,1)S(1)}, u32[]{:S(2)}, u32[]{:S(2)}) collective-permute-start(bf16[288,256]{1,0:T(8,128)(2,1)S(1)} %get-tuple-element.36), channel_id=1, source_target_pairs={{0,31},{1,24},{2,25},{3,26},{4,27},{5,28},{6,29},{7,30},{8,23},{9,... | collective-permute-start | bytes 442376 | tf_op jit(solution)/shard_map/ppermute | solution.py:440
  38.0 0.0 collective-permute-done.14.rest_0_
  38.0 0.3 collective-permute-start.5
  38.4 0.0 collective-permute-done.15.rest_1_
  38.4 1.0 %collective-permute-start.6 = (bf16[288,256]{1,0:T(8,128)(2,1)S(1)}, bf16[288,256]{1,0:T(8,128)(2,1)S(1)}, u32[]{:S(2)}, u32[]{:S(2)}) collective-permute-start(bf16[288,256]{1,0:T(8,128)(2,1)S(1)} %get-tuple-element.38), channel_id=1, source_target_pairs={{0,23},{1,16},{2,17},{3,18},{4,19},{5,20},{6,21},{7,22},{8,31},{9,... | collective-permute-start | bytes 442376 | tf_op jit(solution)/shard_map/ppermute | solution.py:440
  39.4 0.0 collective-permute-done.16.rest_2_
  39.4 2.9 %collective-permute-start.7 = (bf16[288,256]{1,0:T(8,128)(2,1)S(1)}, bf16[288,256]{1,0:T(8,128)(2,1)S(1)}, u32[]{:S(2)}, u32[]{:S(2)}) collective-permute-start(bf16[288,256]{1,0:T(8,128)(2,1)S(1)} %get-tuple-element.39), channel_id=1, source_target_pairs={{0,7},{1,0},{2,1},{3,2},{4,3},{5,4},{6,5},{7,6},{8,15},{9,8},{10,9... | collective-permute-start | bytes 442376 | tf_op jit(solution)/shard_map/ppermute | solution.py:440
  42.3 0.0 collective-permute-done.17.rest_3_
  42.3 0.8 %shard_map.107 = (bf16[1,256,1024]{2,1,0:T(8,128)(2,1)}, bf16[1,256,1024]{2,1,0:T(8,128)(2,1)}, bf16[2,128,256]{2,1,0:T(8,128)(2,1)S(1)}) custom-call(bf16[288,256]{1,0:T(8,128)(2,1)S(1)} %collective-permute-done.14.rest_0_, bf16[288,256]{1,0:T(8,128)(2,1)S(1)} %collective-permute-done.15.rest_1_, bf16[288,256]{1,0:T(8,128)(2,1)S(1)} %collective-permute-done.16.rest_2_, ...), custom_call_target="tpu_custom_call" | custom-call | flops 1000000000 | bytes 3000000 | tf_op jit(solution)/shard_map/pallas_call | solution.py:405
  43.2 1.9 %collective-permute-done.4.rest_0_ = bf16[288,256]{1,0:T(8,128)(2,1)S(1)} collective-permute-done((bf16[288,256]{1,0:T(8,128)(2,1)S(1)}, bf16[288,256]{1,0:T(8,128)(2,1)S(1)}, u32[]{:S(2)}, u32[]{:S(2)}) %collective-permute-start.4) | collective-permute-done | bytes 147488 | tf_op jit(solution)/shard_map/ppermute | solution.py:440
  45.1 1.3 %collective-permute-done.5.rest_1_ = bf16[288,256]{1,0:T(8,128)(2,1)S(1)} collective-permute-done((bf16[288,256]{1,0:T(8,128)(2,1)S(1)}, bf16[288,256]{1,0:T(8,128)(2,1)S(1)}, u32[]{:S(2)}, u32[]{:S(2)}) %collective-permute-start.5) | collective-permute-done | bytes 147488 | tf_op jit(solution)/shard_map/ppermute | solution.py:440
  46.4 0.0 collective-permute-done.6.rest_2_
  46.4 0.0 collective-permute-done.7.rest_3_
  46.4 0.9 %shard_map.108 = (bf16[1,256,1024]{2,1,0:T(8,128)(2,1)}, bf16[1,256,1024]{2,1,0:T(8,128)(2,1)}, bf16[1,256,128]{2,1,0:T(8,128)(2,1)}, bf16[1,256,128]{2,1,0:T(8,128)(2,1)}) custom-call(bf16[288,256]{1,0:T(8,128)(2,1)S(1)} %collective-permute-done.4.rest_0_, ...), custom_call_target="tpu_custom_call", output_to_operand_aliasing={{0}: (5, {}), {1}: (6, {})} | custom-call | flops 1000000000 | bytes 3000000 | tf_op jit(solution)/shard_map/pallas_call | solution.py:405
  (9 shorter events, 0.0 us)
Async XLA Ops:
  0.6 11.6 %collective-permute-start = (bf16[1,256,1024]{2,1,0:T(8,128)(2,1)}, bf16[1,256,1024]{2,1,0:T(8,128)(2,1)S(1)}, u32[]{:S(2)}, u32[]{:S(2)}) collective-permute-start(bf16[1,256,1024]{2,1,0:T(8,128)(2,1)} %param.11), channel_id=1, source_target_pairs={{0,7},{1,0},{2,1},{3,2},{4,3},{5,4},{6,5},{7,6},{8,15},{9,8},{10,9... | collective-permute-start | bytes 1572872 | tf_op jit(solution)/shard_map/ppermute | solution.py:444
  7.3 8.0 %collective-permute-start.8 = (bf16[288,256]{1,0:T(8,128)(2,1)}, bf16[288,256]{1,0:T(8,128)(2,1)S(1)}, u32[]{:S(2)}, u32[]{:S(2)}) collective-permute-start(bf16[288,256]{1,0:T(8,128)(2,1)} %get-tuple-element.40), channel_id=1, source_target_pairs={{0,24},{8,16},{16,8},{24,0},{1,25},{9,17},{17,9},{25,1},{2,26},{10... | collective-permute-start | bytes 442376 | tf_op jit(solution)/shard_map/ppermute | solution.py:432
  9.8 6.8 %collective-permute-start.9 = (bf16[288,256]{1,0:T(8,128)(2,1)}, bf16[288,256]{1,0:T(8,128)(2,1)S(1)}, u32[]{:S(2)}, u32[]{:S(2)}) collective-permute-start(bf16[288,256]{1,0:T(8,128)(2,1)} %get-tuple-element.41), channel_id=1, source_target_pairs={{0,8},{8,0},{16,24},{24,16},{1,9},{9,1},{17,25},{25,17},{2,10},{10... | collective-permute-start | bytes 442376 | tf_op jit(solution)/shard_map/ppermute | solution.py:432
  10.3 5.5 %copy-start = (bf16[1,256,1024]{2,1,0:T(8,128)(2,1)S(1)}, bf16[1,256,1024]{2,1,0:T(8,128)(2,1)}, u32[]{:S(2)}) copy-start(bf16[1,256,1024]{2,1,0:T(8,128)(2,1)} %v_ref.3) | copy-start | bytes 1572868
  10.3 5.5 %copy-start.1 = (bf16[1,256,1024]{2,1,0:T(8,128)(2,1)S(1)}, bf16[1,256,1024]{2,1,0:T(8,128)(2,1)}, u32[]{:S(2)}) copy-start(bf16[1,256,1024]{2,1,0:T(8,128)(2,1)} %gate_ref.3) | copy-start | bytes 1572868
  10.3 5.5 %copy-start.2 = (bf16[1,256,128]{2,1,0:T(8,128)(2,1)S(1)}, bf16[1,256,128]{2,1,0:T(8,128)(2,1)}, u32[]{:S(2)}) copy-start(bf16[1,256,128]{2,1,0:T(8,128)(2,1)} %q_ref.3) | copy-start | bytes 196612
  10.3 5.5 %copy-start.3 = (bf16[1,256,128]{2,1,0:T(8,128)(2,1)S(1)}, bf16[1,256,128]{2,1,0:T(8,128)(2,1)}, u32[]{:S(2)}) copy-start(bf16[1,256,128]{2,1,0:T(8,128)(2,1)} %k_ref.3) | copy-start | bytes 196612
  10.3 8.8 %collective-permute-start.10 = (bf16[288,256]{1,0:T(8,128)(2,1)}, bf16[288,256]{1,0:T(8,128)(2,1)S(1)}, u32[]{:S(2)}, u32[]{:S(2)}) collective-permute-start(bf16[288,256]{1,0:T(8,128)(2,1)} %get-tuple-element.42), channel_id=1, source_target_pairs={{0,16},{8,24},{16,0},{24,8},{1,17},{9,25},{17,1},{25,9},{2,18},{10... | collective-permute-start | bytes 442376 | tf_op jit(solution)/shard_map/ppermute | solution.py:432
  12.3 7.4 %collective-permute-start.11 = (bf16[128,256]{1,0:T(8,128)(2,1)S(1)}, bf16[128,256]{1,0:T(8,128)(2,1)S(1)}, u32[]{:S(2)}, u32[]{:S(2)}) collective-permute-start(bf16[128,256]{1,0:T(8,128)(2,1)S(1)} %get-tuple-element.44), channel_id=1, source_target_pairs={{0,24},{8,16},{16,8},{24,0},{1,25},{9,17},{17,9},{25,1},{2,26},{10... | collective-permute-start | bytes 196616 | tf_op jit(solution)/shard_map/ppermute | solution.py:432
  14.8 5.4 %collective-permute-start.12 = (bf16[128,256]{1,0:T(8,128)(2,1)S(1)}, bf16[128,256]{1,0:T(8,128)(2,1)S(1)}, u32[]{:S(2)}, u32[]{:S(2)}) collective-permute-start(bf16[128,256]{1,0:T(8,128)(2,1)S(1)} %get-tuple-element.45), channel_id=1, source_target_pairs={{0,8},{8,0},{16,24},{24,16},{1,9},{9,1},{17,25},{25,17},{2,10},{10... | collective-permute-start | bytes 196616 | tf_op jit(solution)/shard_map/ppermute | solution.py:432
  15.3 6.9 %collective-permute-start.13 = (bf16[128,256]{1,0:T(8,128)(2,1)S(1)}, bf16[128,256]{1,0:T(8,128)(2,1)S(1)}, u32[]{:S(2)}, u32[]{:S(2)}) collective-permute-start(bf16[128,256]{1,0:T(8,128)(2,1)S(1)} %get-tuple-element.46), channel_id=1, source_target_pairs={{0,16},{8,24},{16,0},{24,8},{1,17},{9,25},{17,1},{25,9},{2,18},{10... | collective-permute-start | bytes 196616 | tf_op jit(solution)/shard_map/ppermute | solution.py:432
  15.8 6.4 %copy-start.4 = (bf16[1,3,1024]{2,1,0:T(4,128)(2,1)S(1)}, bf16[1,3,1024]{2,1,0:T(4,128)(2,1)}, u32[]{:S(2)}) copy-start(bf16[1,3,1024]{2,1,0:T(4,128)(2,1)} %taps_ref.3) | copy-start | bytes 18436
  15.8 6.4 %copy-start.6 = (bf16[288,256]{1,0:T(8,128)(2,1)S(1)}, bf16[288,256]{1,0:T(8,128)(2,1)}, u32[]{:S(2)}) copy-start(bf16[288,256]{1,0:T(8,128)(2,1)} %get-tuple-element.43.rest_3_) | copy-start | bytes 442372
  16.6 12.6 %collective-permute-start.1 = (bf16[416,256]{1,0:T(8,128)(2,1)S(1)}, bf16[416,256]{1,0:T(8,128)(2,1)S(1)}, u32[]{:S(2)}, u32[]{:S(2)}) collective-permute-start(bf16[416,256]{1,0:T(8,128)(2,1)S(1)} %get-tuple-element.32), channel_id=1, source_target_pairs={{0,24},{8,16},{16,8},{24,0},{1,25},{9,17},{17,9},{25,1},{2,26},{10... | collective-permute-start | bytes 638984 | tf_op jit(solution)/shard_map/ppermute | solution.py:432
  19.1 10.4 %collective-permute-start.2 = (bf16[416,256]{1,0:T(8,128)(2,1)S(1)}, bf16[416,256]{1,0:T(8,128)(2,1)S(1)}, u32[]{:S(2)}, u32[]{:S(2)}) collective-permute-start(bf16[416,256]{1,0:T(8,128)(2,1)S(1)} %get-tuple-element.33), channel_id=1, source_target_pairs={{0,8},{8,0},{16,24},{24,16},{1,9},{9,1},{17,25},{25,17},{2,10},{10... | collective-permute-start | bytes 638984 | tf_op jit(solution)/shard_map/ppermute | solution.py:432
  19.7 2.6 %copy-start.5 = (s32[1,4]{1,0:T(1,128)S(1)}, s32[1,4]{1,0:T(1,128)}, u32[]{:S(2)}) copy-start(s32[1,4]{1,0:T(1,128)} %bounds.3) | copy-start | bytes 52
  19.7 11.2 %collective-permute-start.3 = (bf16[416,256]{1,0:T(8,128)(2,1)S(1)}, bf16[416,256]{1,0:T(8,128)(2,1)S(1)}, u32[]{:S(2)}, u32[]{:S(2)}) collective-permute-start(bf16[416,256]{1,0:T(8,128)(2,1)S(1)} %get-tuple-element.34), channel_id=1, source_target_pairs={{0,16},{8,24},{16,0},{24,8},{1,17},{9,25},{17,1},{25,9},{2,18},{10... | collective-permute-start | bytes 638984 | tf_op jit(solution)/shard_map/ppermute | solution.py:432
  27.4 10.7 %collective-permute-start.14 = (bf16[288,256]{1,0:T(8,128)(2,1)S(1)}, bf16[288,256]{1,0:T(8,128)(2,1)S(1)}, u32[]{:S(2)}, u32[]{:S(2)}) collective-permute-start(bf16[288,256]{1,0:T(8,128)(2,1)S(1)} %get-tuple-element.47), channel_id=1, source_target_pairs={{0,31},{1,24},{2,25},{3,26},{4,27},{5,28},{6,29},{7,30},{8,23},{9,... | collective-permute-start | bytes 442376 | tf_op jit(solution)/shard_map/ppermute | solution.py:440
  29.2 9.2 %collective-permute-start.15 = (bf16[288,256]{1,0:T(8,128)(2,1)S(1)}, bf16[288,256]{1,0:T(8,128)(2,1)S(1)}, u32[]{:S(2)}, u32[]{:S(2)}) collective-permute-start(bf16[288,256]{1,0:T(8,128)(2,1)S(1)} %get-tuple-element.48), channel_id=1, source_target_pairs={{0,15},{1,8},{2,9},{3,10},{4,11},{5,12},{6,13},{7,14},{8,7},{9,0},... | collective-permute-start | bytes 442376 | tf_op jit(solution)/shard_map/ppermute | solution.py:440
  29.2 10.2 %collective-permute-start.16 = (bf16[288,256]{1,0:T(8,128)(2,1)S(1)}, bf16[288,256]{1,0:T(8,128)(2,1)S(1)}, u32[]{:S(2)}, u32[]{:S(2)}) collective-permute-start(bf16[288,256]{1,0:T(8,128)(2,1)S(1)} %get-tuple-element.49), channel_id=1, source_target_pairs={{0,23},{1,16},{2,17},{3,18},{4,19},{5,20},{6,21},{7,22},{8,31},{9,... | collective-permute-start | bytes 442376 | tf_op jit(solution)/shard_map/ppermute | solution.py:440
  29.5 12.8 %collective-permute-start.17 = (bf16[288,256]{1,0:T(8,128)(2,1)S(1)}, bf16[288,256]{1,0:T(8,128)(2,1)S(1)}, u32[]{:S(2)}, u32[]{:S(2)}) collective-permute-start(bf16[288,256]{1,0:T(8,128)(2,1)S(1)} %get-tuple-element.50), channel_id=1, source_target_pairs={{0,7},{1,0},{2,1},{3,2},{4,3},{5,4},{6,5},{7,6},{8,15},{9,8},{10,9... | collective-permute-start | bytes 442376 | tf_op jit(solution)/shard_map/ppermute | solution.py:440
  36.0 9.1 %collective-permute-start.4 = (bf16[288,256]{1,0:T(8,128)(2,1)S(1)}, bf16[288,256]{1,0:T(8,128)(2,1)S(1)}, u32[]{:S(2)}, u32[]{:S(2)}) collective-permute-start(bf16[288,256]{1,0:T(8,128)(2,1)S(1)} %get-tuple-element.36), channel_id=1, source_target_pairs={{0,31},{1,24},{2,25},{3,26},{4,27},{5,28},{6,29},{7,30},{8,23},{9,... | collective-permute-start | bytes 442376 | tf_op jit(solution)/shard_map/ppermute | solution.py:440
  38.0 8.3 %collective-permute-start.5 = (bf16[288,256]{1,0:T(8,128)(2,1)S(1)}, bf16[288,256]{1,0:T(8,128)(2,1)S(1)}, u32[]{:S(2)}, u32[]{:S(2)}) collective-permute-start(bf16[288,256]{1,0:T(8,128)(2,1)S(1)} %get-tuple-element.37), channel_id=1, source_target_pairs={{0,15},{1,8},{2,9},{3,10},{4,11},{5,12},{6,13},{7,14},{8,7},{9,0},... | collective-permute-start | bytes 442376 | tf_op jit(solution)/shard_map/ppermute | solution.py:440
  38.4 8.0 %collective-permute-start.6 = (bf16[288,256]{1,0:T(8,128)(2,1)S(1)}, bf16[288,256]{1,0:T(8,128)(2,1)S(1)}, u32[]{:S(2)}, u32[]{:S(2)}) collective-permute-start(bf16[288,256]{1,0:T(8,128)(2,1)S(1)} %get-tuple-element.38), channel_id=1, source_target_pairs={{0,23},{1,16},{2,17},{3,18},{4,19},{5,20},{6,21},{7,22},{8,31},{9,... | collective-permute-start | bytes 442376 | tf_op jit(solution)/shard_map/ppermute | solution.py:440
  39.4 7.0 %collective-permute-start.7 = (bf16[288,256]{1,0:T(8,128)(2,1)S(1)}, bf16[288,256]{1,0:T(8,128)(2,1)S(1)}, u32[]{:S(2)}, u32[]{:S(2)}) collective-permute-start(bf16[288,256]{1,0:T(8,128)(2,1)S(1)} %get-tuple-element.39), channel_id=1, source_target_pairs={{0,7},{1,0},{2,1},{3,2},{4,3},{5,4},{6,5},{7,6},{8,15},{9,8},{10,9... | collective-permute-start | bytes 442376 | tf_op jit(solution)/shard_map/ppermute | solution.py:440

commit v5 on v4

--- a/solution.py
+++ b/solution.py
@@ -50,8 +50,11 @@
     return sorted(range(count), key=lambda partner: -bin(partner).count("1"))
 
 
-def senders_of(count):
-    return [p for p in far_first(count) if p % max(1, count // HEADS) == 0]
+def senders_of(count, phase):
+    order = far_first(count)
+    if phase == phases_of(count) - 1:
+        order = order[:1] + order[-1:] + order[1:-1]
+    return [partner for partner in order if partner % max(1, count // HEADS) == 0]
 
 
 def pack_kernel(count, phase, q_ref, k_ref, v_ref, gate_ref, *rest):
@@ -161,7 +164,7 @@
 
 
 def attend_kernel(count, phase, bounds, taps_ref, *rest):
-    senders = senders_of(count)
+    senders = senders_of(count, phase)
     packed, rest = dict(zip(far_first(count), rest)), rest[count:]
     grads, base = packed, ROWS
     if phase == 0:
@@ -212,6 +215,19 @@
         else:
             each(0, i, lambda j: body(j, 1))
 
+    waiting = []
+
+    def finish_waiting():
+        while waiting:
+            waiting.pop(0)()
+
+    def ahead(first, second):
+        found = first()
+        finish_waiting()
+        waiting.append(lambda: second(found))
+        if count > UNROLLED:
+            finish_waiting()
+
     def row_block(i):
         bound = bounds[0, i]
         before = earlier(i)
@@ -229,30 +245,39 @@
             value = jnp.concatenate([value, jnp.ones_like(value)], axis=1)
             return nn(high, value) + nn(low, value)
 
-        own_base, own_kern = kernel_of(i, 1)
-        own_high, own_low = halves(jnp.where(same, own_kern, 0.0))
-        own = weigh(own_high, own_low, values(i, 1))
+        kept = {}
+
+        def own_forward(found):
+            kept["base"], kern = found
+            kept["high"], kept["low"] = halves(jnp.where(same, kern, 0.0))
+            kept["sum"] = weigh(kept["high"], kept["low"], values(i, 1))
+
+        ahead(lambda: kernel_of(i, 1), own_forward)
         num_s[i] = jnp.zeros((TOK, 2 * DV), F32)
         room = (i * (i - 1)) // 2 * TOK if isinstance(i, int) else 0
 
         def forward(j, wide):
             width = wide * TOK
-            base, kern = kernel_of(j, wide)
-            high, low = halves(kern)
-            lanes = pl.ds(room + j * TOK, width)
-            base_s[:, lanes] = base
-            high_s[:, lanes] = high
-            low_s[:, lanes] = low
-            value = values(j, wide)
-            allowed = iota((width, DV), 0) + j * TOK >= before
-            ones = jnp.where(allowed, 1.0, 0.0).astype(BF16)
-            value = jnp.concatenate([value * ones, ones], axis=1)
-            num_s[i] += nn(high, value) + nn(low, value)
+
+            def weigh_older(found):
+                base, kern = found
+                high, low = halves(kern)
+                lanes = pl.ds(room + j * TOK, width)
+                base_s[:, lanes] = base
+                high_s[:, lanes] = high
+                low_s[:, lanes] = low
+                value = values(j, wide)
+                allowed = iota((width, DV), 0) + j * TOK >= before
+                ones = jnp.where(allowed, 1.0, 0.0).astype(BF16)
+                value = jnp.concatenate([value * ones, ones], axis=1)
+                num_s[i] += nn(high, value) + nn(low, value)
+
+            ahead(lambda: kernel_of(j, wide), weigh_older)
 
         spans(i, forward)
         yield
         old = iota((TOK, 2 * DV), 0) < bound
-        total = own + jnp.where(old, num_s[i], 0.0)
+        total = kept["sum"] + jnp.where(old, num_s[i], 0.0)
         num, den = total[:, 0:DV], total[:, DV:]
 
         position = iota((TOK, DV), 0) + i * TOK
@@ -278,29 +303,43 @@
         def slopes(d_pair, d_den, base, value):
             return (nt(d_pair, jnp.concatenate([value, value], axis=1)) + d_den) * base
 
-        slope = slopes(d_pair, d_den, own_base, values(i, 1))
-        s_high, s_low = halves(jnp.where(same, slope, 0.0))
-        key = keys(i, 1)
-        lanes = pl.ds(i * TOK, TOK)
-        dv_s[:, lanes] = nn(d_pair_t, own_high) + nn(d_pair_t, own_low)
-        dk_s[:, lanes] = nn(query_t, s_high) + nn(query_t, s_low)
-        dq_s[i] = nt(key, s_high) + nt(key, s_low)
+        def own_slopes():
+            slope = slopes(d_pair, d_den, kept["base"], values(i, 1))
+            return halves(jnp.where(same, slope, 0.0))
+
+        def own_backward(found):
+            s_high, s_low = found
+            key = keys(i, 1)
+            lanes = pl.ds(i * TOK, TOK)
+            dv_s[:, lanes] = nn(d_pair_t, kept["high"]) + nn(d_pair_t, kept["low"])
+            dk_s[:, lanes] = nn(query_t, s_high) + nn(query_t, s_low)
+            dq_s[i] = nt(key, s_high) + nt(key, s_low)
+
+        ahead(own_slopes, own_backward)
 
         def backward(j, wide):
             width = wide * TOK
             lanes = pl.ds(j * TOK, width)
-            lane_old = jnp.where(iota((2 * DV, TOK), 1) < bound, 1.0, 0.0).astype(BF16)
-            row_old = jnp.where(old, 1.0, 0.0).astype(BF16)
-            pair, pair_t = d_pair * row_old, d_pair_t * lane_old
-            den = jnp.where(iota((TOK, 1), 0) < bound, d_den, 0.0)
             saved = pl.ds(room + j * TOK, width)
-            s_high, s_low = halves(slopes(pair, den, base_s[:, saved], values(j, wide)))
-            allowed = iota((1, width), 1) + j * TOK >= before
-            keep = jnp.where(allowed, 1.0, 0.0)
-            key = keys(j, wide) * keep.astype(BF16)
-            dv_s[:, lanes] += keep * (nn(pair_t, high_s[:, saved]) + nn(pair_t, low_s[:, saved]))
-            dk_s[:, lanes] += keep * (nn(query_t, s_high) + nn(query_t, s_low))
-            dq_s[i] += nt(key, s_high) + nt(key, s_low)
+
+            def older_slopes():
+                row_old = jnp.where(old, 1.0, 0.0).astype(BF16)
+                den = jnp.where(iota((TOK, 1), 0) < bound, d_den, 0.0)
+                return halves(slopes(d_pair * row_old, den, base_s[:, saved], values(j, wide)))
+
+            def older_backward(found):
+                s_high, s_low = found
+                lane_old = jnp.where(iota((2 * DV, TOK), 1) < bound, 1.0, 0.0).astype(BF16)
+                pair_t = d_pair_t * lane_old
+                keep = jnp.where(iota((1, width), 1) + j * TOK >= before, 1.0, 0.0)
+                key = keys(j, wide) * keep.astype(BF16)
+                dv_s[:, lanes] += keep * (
+                    nn(pair_t, high_s[:, saved]) + nn(pair_t, low_s[:, saved])
+                )
+                dk_s[:, lanes] += keep * (nn(query_t, s_high) + nn(query_t, s_low))
+                dq_s[i] += nt(key, s_high) + nt(key, s_low)
+
+            ahead(older_slopes, older_backward)
 
         spans(i, backward)
         yield
@@ -310,6 +349,7 @@
         for _ in range(2):
             for row in rows:
                 next(row)
+            finish_waiting()
     else:
         each(0, count, lambda i: list(row_block(i)))
 
@@ -331,7 +371,7 @@
     def in_order(blocks):
         return [blocks[partner] for partner in far_first(count)] if blocks else []
 
-    outs = len(senders_of(count))
+    outs = len(senders_of(count, phase))
     saved = (count * (count - 1) // 2 if count <= UNROLLED else count - 1) * TOK
     return pl.pallas_call(
         functools.partial(attend_kernel, count, phase),
@@ -357,7 +397,7 @@
 
 
 def unpack_kernel(count, phase, *rest):
-    senders = senders_of(count)
+    senders = senders_of(count, phase)
     many = len(senders)
     me = lax.axis_index("ctx")
     last = phase == phases_of(count) - 1
@@ -424,7 +464,7 @@
 
 
 def on_device(count, sections, q_in, k_in, v_in, gate_in, out_grad, conv_weight, bounds):
-    phases, senders = phases_of(count), senders_of(count)
+    phases = phases_of(count)
 
     def across(value, partner):
         if partner == 0:
@@ -458,6 +498,7 @@
     for phase in range(phases):
         results = attend(count, phase, bounds, conv_weight, blocks[phase], grads)
         grads = []
+        senders = senders_of(count, phase)
         results = dict(zip(senders, results))
         moved = {p: across_back(results[p], p) for p in order if p in results}
         arrived.append([moved[partner] for partner in senders])

time: 47.5 us -> 47.4 us (level)
  transfers between devices with their start and end apart: 18 -> 18, of which waited for: 5 -> 5; matrix products, arithmetic and copies ran while one was open for 0% -> 0% of each run, Pallas kernels for 30% -> 29%
where the time goes in v5:
time: 47.4 us; the launch traced here: 47.3 us
  starting transfers between devices  24.8 us (52%)
  Pallas kernels  14.9 us (31%)
  waiting for transfers between devices  6.81 us (14%)
  between operations  0.73 us (2%)
    ppermute x9, starting transfers between devices, across(): return lax.ppermute(value, 'ctx', [(c, c ^ partner) for c in range(count)])  10.7 us
    pallas_call x2, Pallas kernels, attend(): pl.pallas_call(functools.partial(attend_kernel, count, phase), cost_estim...  10.2 us
    ppermute x8, starting transfers between devices, across_back(): return lax.ppermute(value, ('ctx', 'pipe'), pairs)  9.57 us
    ppermute x1, starting transfers between devices, on_device(): cotangent = lax.ppermute(out_grad, 'pipe', shift)  4.54 us
    ppermute x8, waiting for transfers between devices, across_back(): return lax.ppermute(value, ('ctx', 'pipe'), pairs)  3.24 us
    pallas_call x2, Pallas kernels, pack(): pl.pallas_call(functools.partial(pack_kernel, count, phase), cost_estimat...  2.83 us
    ppermute x9, waiting for transfers between devices, across(): return lax.ppermute(value, 'ctx', [(c, c ^ partner) for c in range(count)])  2.28 us
    pallas_call x2, Pallas kernels, unpack(): pl.pallas_call(functools.partial(unpack_kernel, count, phase), cost_estim...  1.79 us
  transfers between devices with their start and end apart: 18, of which 5 were waited for; matrix products, arithmetic and copies ran while one was open for 0% of the time, Pallas kernels for 29%

profile of v5, /device:TPU:0, one launch (start us, length us, event | category | flops | bytes accessed | tf_op | source)
XLA Modules:
  0.0 47.3 jit_solution(7938285192795841097)
XLA Ops:
  0.6 4.5 %collective-permute-start = (bf16[1,256,1024]{2,1,0:T(8,128)(2,1)}, bf16[1,256,1024]{2,1,0:T(8,128)(2,1)S(1)}, u32[]{:S(2)}, u32[]{:S(2)}) collective-permute-start(bf16[1,256,1024]{2,1,0:T(8,128)(2,1)} %param.11), channel_id=1, source_target_pairs={{0,7},{1,0},{2,1},{3,2},{4,3},{5,4},{6,5},{7,6},{8,15},{9,8},{10,9... | collective-permute-start | bytes 1572872 | tf_op jit(solution)/shard_map/ppermute | solution.py:484
  5.2 2.1 %shard_map.105 = (bf16[288,256]{1,0:T(8,128)(2,1)}, bf16[288,256]{1,0:T(8,128)(2,1)}, bf16[288,256]{1,0:T(8,128)(2,1)}, bf16[288,256]{1,0:T(8,128)(2,1)}) custom-call(bf16[1,256,128]{2,1,0:T(8,128)(2,1)} %q_ref.3, bf16[1,256,128]{2,1,0:T(8,128)(2,1)} %k_ref.3, bf16[1,256,1024]{2,1,0:T(8,128)(2,1)} %v_ref.3, bf16[1,256,1024]{2,1,0:T(8,128)(2,1)} %gate_ref.3), custom_call_target="tpu_custom_call" | custom-call | flops 2000000000 | bytes 6000000 | tf_op jit(solution)/shard_map/pallas_call | solution.py:102
  7.3 2.5 %collective-permute-start.8 = (bf16[288,256]{1,0:T(8,128)(2,1)}, bf16[288,256]{1,0:T(8,128)(2,1)S(1)}, u32[]{:S(2)}, u32[]{:S(2)}) collective-permute-start(bf16[288,256]{1,0:T(8,128)(2,1)} %get-tuple-element.40), channel_id=1, source_target_pairs={{0,24},{8,16},{16,8},{24,0},{1,25},{9,17},{17,9},{25,1},{2,26},{10... | collective-permute-start | bytes 442376 | tf_op jit(solution)/shard_map/ppermute | solution.py:472
  9.8 0.5 %collective-permute-start.9 = (bf16[288,256]{1,0:T(8,128)(2,1)}, bf16[288,256]{1,0:T(8,128)(2,1)S(1)}, u32[]{:S(2)}, u32[]{:S(2)}) collective-permute-start(bf16[288,256]{1,0:T(8,128)(2,1)} %get-tuple-element.41), channel_id=1, source_target_pairs={{0,8},{8,0},{16,24},{24,16},{1,9},{9,1},{17,25},{25,17},{2,10},{10... | collective-permute-start | bytes 442376 | tf_op jit(solution)/shard_map/ppermute | solution.py:472
  10.3 0.6 %collective-permute-start.10 = (bf16[288,256]{1,0:T(8,128)(2,1)}, bf16[288,256]{1,0:T(8,128)(2,1)S(1)}, u32[]{:S(2)}, u32[]{:S(2)}) collective-permute-start(bf16[288,256]{1,0:T(8,128)(2,1)} %get-tuple-element.42), channel_id=1, source_target_pairs={{0,16},{8,24},{16,0},{24,8},{1,17},{9,25},{17,1},{25,9},{2,18},{10... | collective-permute-start | bytes 442376 | tf_op jit(solution)/shard_map/ppermute | solution.py:472
  10.9 1.3 %collective-permute-done.grad_ref.rest_0_ = bf16[1,256,1024]{2,1,0:T(8,128)(2,1)S(1)} collective-permute-done((bf16[1,256,1024]{2,1,0:T(8,128)(2,1)}, bf16[1,256,1024]{2,1,0:T(8,128)(2,1)S(1)}, u32[]{:S(2)}, u32[]{:S(2)}) %collective-permute-start) | collective-permute-done | bytes 524320 | tf_op jit(solution)/shard_map/ppermute | solution.py:484
  12.2 0.1 shard_map.102
  12.3 2.5 %collective-permute-start.11 = (bf16[128,256]{1,0:T(8,128)(2,1)S(1)}, bf16[128,256]{1,0:T(8,128)(2,1)S(1)}, u32[]{:S(2)}, u32[]{:S(2)}) collective-permute-start(bf16[128,256]{1,0:T(8,128)(2,1)S(1)} %get-tuple-element.44), channel_id=1, source_target_pairs={{0,24},{8,16},{16,8},{24,0},{1,25},{9,17},{17,9},{25,1},{2,26},{10... | collective-permute-start | bytes 196616 | tf_op jit(solution)/shard_map/ppermute | solution.py:472
  14.8 0.5 %collective-permute-start.12 = (bf16[128,256]{1,0:T(8,128)(2,1)S(1)}, bf16[128,256]{1,0:T(8,128)(2,1)S(1)}, u32[]{:S(2)}, u32[]{:S(2)}) collective-permute-start(bf16[128,256]{1,0:T(8,128)(2,1)S(1)} %get-tuple-element.45), channel_id=1, source_target_pairs={{0,8},{8,0},{16,24},{24,16},{1,9},{9,1},{17,25},{25,17},{2,10},{10... | collective-permute-start | bytes 196616 | tf_op jit(solution)/shard_map/ppermute | solution.py:472
  15.3 0.0 collective-permute-done.8.rest_0_
  15.3 0.5 %collective-permute-start.13 = (bf16[128,256]{1,0:T(8,128)(2,1)S(1)}, bf16[128,256]{1,0:T(8,128)(2,1)S(1)}, u32[]{:S(2)}, u32[]{:S(2)}) collective-permute-start(bf16[128,256]{1,0:T(8,128)(2,1)S(1)} %get-tuple-element.46), channel_id=1, source_target_pairs={{0,16},{8,24},{16,0},{24,8},{1,17},{9,25},{17,1},{25,9},{2,18},{10... | collective-permute-start | bytes 196616 | tf_op jit(solution)/shard_map/ppermute | solution.py:472
  15.8 0.0 copy-done
  15.8 0.0 copy-done.1
  15.8 0.0 copy-done.2
  15.8 0.0 copy-start.4
  15.8 0.0 copy-start.6
  15.9 0.7 %shard_map.103 = (bf16[416,256]{1,0:T(8,128)(2,1)S(1)}, bf16[416,256]{1,0:T(8,128)(2,1)S(1)}, bf16[416,256]{1,0:T(8,128)(2,1)S(1)}, bf16[416,256]{1,0:T(8,128)(2,1)S(1)}) custom-call(bf16[1,256,128]{2,1,0:T(8,128)(2,1)S(1)} %copy-done.2, bf16[1,256,128]{2,1,0:T(8,128)(2,1)S(1)} %copy-done.3, bf16[1,256,1024]{2,1,0:T(8,128)(2,1)S(1)} %copy-done, ...), custom_call_target="tpu_custom_call" | custom-call | flops 2000000000 | bytes 6000000 | tf_op jit(solution)/shard_map/pallas_call | solution.py:102
  16.6 0.0 collective-permute-done.9.rest_1_
  16.6 2.5 %collective-permute-start.1 = (bf16[416,256]{1,0:T(8,128)(2,1)S(1)}, bf16[416,256]{1,0:T(8,128)(2,1)S(1)}, u32[]{:S(2)}, u32[]{:S(2)}) collective-permute-start(bf16[416,256]{1,0:T(8,128)(2,1)S(1)} %get-tuple-element.32), channel_id=1, source_target_pairs={{0,24},{8,16},{16,8},{24,0},{1,25},{9,17},{17,9},{25,1},{2,26},{10... | collective-permute-start | bytes 638984 | tf_op jit(solution)/shard_map/ppermute | solution.py:472
  19.1 0.0 collective-permute-done.10.rest_2_
  19.1 0.5 %collective-permute-start.2 = (bf16[416,256]{1,0:T(8,128)(2,1)S(1)}, bf16[416,256]{1,0:T(8,128)(2,1)S(1)}, u32[]{:S(2)}, u32[]{:S(2)}) collective-permute-start(bf16[416,256]{1,0:T(8,128)(2,1)S(1)} %get-tuple-element.33), channel_id=1, source_target_pairs={{0,8},{8,0},{16,24},{24,16},{1,9},{9,1},{17,25},{25,17},{2,10},{10... | collective-permute-start | bytes 638984 | tf_op jit(solution)/shard_map/ppermute | solution.py:472
  19.7 0.0 collective-permute-done.11.rest_4_
  19.7 0.5 %collective-permute-start.3 = (bf16[416,256]{1,0:T(8,128)(2,1)S(1)}, bf16[416,256]{1,0:T(8,128)(2,1)S(1)}, u32[]{:S(2)}, u32[]{:S(2)}) collective-permute-start(bf16[416,256]{1,0:T(8,128)(2,1)S(1)} %get-tuple-element.34), channel_id=1, source_target_pairs={{0,16},{8,24},{16,0},{24,8},{1,17},{9,25},{17,1},{25,9},{2,18},{10... | collective-permute-start | bytes 638984 | tf_op jit(solution)/shard_map/ppermute | solution.py:472
  20.2 0.0 collective-permute-done.12.rest_5_
  20.2 2.0 %collective-permute-done.13.rest_6_ = bf16[128,256]{1,0:T(8,128)(2,1)S(1)} collective-permute-done((bf16[128,256]{1,0:T(8,128)(2,1)S(1)}, bf16[128,256]{1,0:T(8,128)(2,1)S(1)}, u32[]{:S(2)}, u32[]{:S(2)}) %collective-permute-start.13) | collective-permute-done | bytes 65568 | tf_op jit(solution)/shard_map/ppermute | solution.py:472
  22.2 5.1 %shard_map.106 = (bf16[288,256]{1,0:T(8,128)(2,1)S(1)}, bf16[288,256]{1,0:T(8,128)(2,1)S(1)}, bf16[288,256]{1,0:T(8,128)(2,1)S(1)}, bf16[288,256]{1,0:T(8,128)(2,1)S(1)}) custom-call(s32[1,4]{1,0:T(1,128)S(1)} %copy-done.5, bf16[1,3,1024]{2,1,0:T(4,128)(2,1)S(1)} %copy-done.4, bf16[288,256]{1,0:T(8,128)(2,1)S(1)} %collective-permute-done.8.rest_0_, ...), custom_call_target="tpu_custom_call" | custom-call | flops 5000000000 | bytes 15000000 | tf_op jit(solution)/shard_map/pallas_call | solution.py:376
  27.3 1.8 %collective-permute-start.14 = (bf16[288,256]{1,0:T(8,128)(2,1)S(1)}, bf16[288,256]{1,0:T(8,128)(2,1)S(1)}, u32[]{:S(2)}, u32[]{:S(2)}) collective-permute-start(bf16[288,256]{1,0:T(8,128)(2,1)S(1)} %get-tuple-element.47), channel_id=1, source_target_pairs={{0,31},{1,24},{2,25},{3,26},{4,27},{5,28},{6,29},{7,30},{8,23},{9,... | collective-permute-start | bytes 442376 | tf_op jit(solution)/shard_map/ppermute | solution.py:480
  29.1 0.0 collective-permute-start.15
  29.1 0.0 collective-permute-done.1.rest_0_
  29.1 0.1 collective-permute-start.16
  29.3 0.2 collective-permute-done.2.rest_1_
  29.5 1.3 %collective-permute-start.17 = (bf16[288,256]{1,0:T(8,128)(2,1)S(1)}, bf16[288,256]{1,0:T(8,128)(2,1)S(1)}, u32[]{:S(2)}, u32[]{:S(2)}) collective-permute-start(bf16[288,256]{1,0:T(8,128)(2,1)S(1)} %get-tuple-element.50), channel_id=1, source_target_pairs={{0,7},{1,0},{2,1},{3,2},{4,3},{5,4},{6,5},{7,6},{8,15},{9,8},{10,9... | collective-permute-start | bytes 442376 | tf_op jit(solution)/shard_map/ppermute | solution.py:480
  30.8 0.0 collective-permute-done.3.rest_2_
  30.8 5.1 %shard_map.104 = (bf16[288,256]{1,0:T(8,128)(2,1)S(1)}, bf16[288,256]{1,0:T(8,128)(2,1)S(1)}, bf16[288,256]{1,0:T(8,128)(2,1)S(1)}, bf16[288,256]{1,0:T(8,128)(2,1)S(1)}) custom-call(s32[1,4]{1,0:T(1,128)S(1)} %copy-done.5, bf16[1,3,1024]{2,1,0:T(4,128)(2,1)S(1)} %copy-done.4, bf16[416,256]{1,0:T(8,128)(2,1)S(1)} %collective-permute-done.1.rest_0_, ...), custom_call_target="tpu_custom_call" | custom-call | flops 5000000000 | bytes 15000000 | tf_op jit(solution)/shard_map/pallas_call | solution.py:376
  36.0 2.1 %collective-permute-start.4 = (bf16[288,256]{1,0:T(8,128)(2,1)S(1)}, bf16[288,256]{1,0:T(8,128)(2,1)S(1)}, u32[]{:S(2)}, u32[]{:S(2)}) collective-permute-start(bf16[288,256]{1,0:T(8,128)(2,1)S(1)} %get-tuple-element.36), channel_id=1, source_target_pairs={{0,31},{1,24},{2,25},{3,26},{4,27},{5,28},{6,29},{7,30},{8,23},{9,... | collective-permute-start | bytes 442376 | tf_op jit(solution)/shard_map/ppermute | solution.py:480
  38.0 0.0 collective-permute-done.14.rest_0_
  38.0 0.4 collective-permute-start.5
  38.4 0.0 collective-permute-done.15.rest_1_
  38.4 0.0 collective-permute-start.6
  38.4 0.0 collective-permute-done.16.rest_2_
  38.4 3.8 %collective-permute-start.7 = (bf16[288,256]{1,0:T(8,128)(2,1)S(1)}, bf16[288,256]{1,0:T(8,128)(2,1)S(1)}, u32[]{:S(2)}, u32[]{:S(2)}) collective-permute-start(bf16[288,256]{1,0:T(8,128)(2,1)S(1)} %get-tuple-element.39), channel_id=1, source_target_pairs={{0,23},{1,16},{2,17},{3,18},{4,19},{5,20},{6,21},{7,22},{8,31},{9,... | collective-permute-start | bytes 442376 | tf_op jit(solution)/shard_map/ppermute | solution.py:480
  42.2 0.0 collective-permute-done.17.rest_3_
  42.2 0.8 %shard_map.107 = (bf16[1,256,1024]{2,1,0:T(8,128)(2,1)}, bf16[1,256,1024]{2,1,0:T(8,128)(2,1)}, bf16[2,128,256]{2,1,0:T(8,128)(2,1)S(1)}) custom-call(bf16[288,256]{1,0:T(8,128)(2,1)S(1)} %collective-permute-done.14.rest_0_, bf16[288,256]{1,0:T(8,128)(2,1)S(1)} %collective-permute-done.15.rest_1_, bf16[288,256]{1,0:T(8,128)(2,1)S(1)} %collective-permute-done.16.rest_2_, ...), custom_call_target="tpu_custom_call" | custom-call | flops 1000000000 | bytes 3000000 | tf_op jit(solution)/shard_map/pallas_call | solution.py:445
  43.1 0.1 collective-permute-done.4.rest_0_
  43.2 0.0 collective-permute-done.5.rest_1_
  43.2 3.2 %collective-permute-done.6.rest_2_ = bf16[288,256]{1,0:T(8,128)(2,1)S(1)} collective-permute-done((bf16[288,256]{1,0:T(8,128)(2,1)S(1)}, bf16[288,256]{1,0:T(8,128)(2,1)S(1)}, u32[]{:S(2)}, u32[]{:S(2)}) %collective-permute-start.6) | collective-permute-done | bytes 147488 | tf_op jit(solution)/shard_map/ppermute | solution.py:480
  46.3 0.0 collective-permute-done.7.rest_3_
  46.3 0.9 %shard_map.108 = (bf16[1,256,1024]{2,1,0:T(8,128)(2,1)}, bf16[1,256,1024]{2,1,0:T(8,128)(2,1)}, bf16[1,256,128]{2,1,0:T(8,128)(2,1)}, bf16[1,256,128]{2,1,0:T(8,128)(2,1)}) custom-call(bf16[288,256]{1,0:T(8,128)(2,1)S(1)} %collective-permute-done.4.rest_0_, ...), custom_call_target="tpu_custom_call", output_to_operand_aliasing={{0}: (5, {}), {1}: (6, {})} | custom-call | flops 1000000000 | bytes 3000000 | tf_op jit(solution)/shard_map/pallas_call | solution.py:445
  (9 shorter events, 0.0 us)
Async XLA Ops:
  0.6 11.6 %collective-permute-start = (bf16[1,256,1024]{2,1,0:T(8,128)(2,1)}, bf16[1,256,1024]{2,1,0:T(8,128)(2,1)S(1)}, u32[]{:S(2)}, u32[]{:S(2)}) collective-permute-start(bf16[1,256,1024]{2,1,0:T(8,128)(2,1)} %param.11), channel_id=1, source_target_pairs={{0,7},{1,0},{2,1},{3,2},{4,3},{5,4},{6,5},{7,6},{8,15},{9,8},{10,9... | collective-permute-start | bytes 1572872 | tf_op jit(solution)/shard_map/ppermute | solution.py:484
  7.3 8.0 %collective-permute-start.8 = (bf16[288,256]{1,0:T(8,128)(2,1)}, bf16[288,256]{1,0:T(8,128)(2,1)S(1)}, u32[]{:S(2)}, u32[]{:S(2)}) collective-permute-start(bf16[288,256]{1,0:T(8,128)(2,1)} %get-tuple-element.40), channel_id=1, source_target_pairs={{0,24},{8,16},{16,8},{24,0},{1,25},{9,17},{17,9},{25,1},{2,26},{10... | collective-permute-start | bytes 442376 | tf_op jit(solution)/shard_map/ppermute | solution.py:472
  9.8 6.8 %collective-permute-start.9 = (bf16[288,256]{1,0:T(8,128)(2,1)}, bf16[288,256]{1,0:T(8,128)(2,1)S(1)}, u32[]{:S(2)}, u32[]{:S(2)}) collective-permute-start(bf16[288,256]{1,0:T(8,128)(2,1)} %get-tuple-element.41), channel_id=1, source_target_pairs={{0,8},{8,0},{16,24},{24,16},{1,9},{9,1},{17,25},{25,17},{2,10},{10... | collective-permute-start | bytes 442376 | tf_op jit(solution)/shard_map/ppermute | solution.py:472
  10.3 5.5 %copy-start = (bf16[1,256,1024]{2,1,0:T(8,128)(2,1)S(1)}, bf16[1,256,1024]{2,1,0:T(8,128)(2,1)}, u32[]{:S(2)}) copy-start(bf16[1,256,1024]{2,1,0:T(8,128)(2,1)} %v_ref.3) | copy-start | bytes 1572868
  10.3 5.5 %copy-start.1 = (bf16[1,256,1024]{2,1,0:T(8,128)(2,1)S(1)}, bf16[1,256,1024]{2,1,0:T(8,128)(2,1)}, u32[]{:S(2)}) copy-start(bf16[1,256,1024]{2,1,0:T(8,128)(2,1)} %gate_ref.3) | copy-start | bytes 1572868
  10.3 5.5 %copy-start.2 = (bf16[1,256,128]{2,1,0:T(8,128)(2,1)S(1)}, bf16[1,256,128]{2,1,0:T(8,128)(2,1)}, u32[]{:S(2)}) copy-start(bf16[1,256,128]{2,1,0:T(8,128)(2,1)} %q_ref.3) | copy-start | bytes 196612
  10.3 5.5 %copy-start.3 = (bf16[1,256,128]{2,1,0:T(8,128)(2,1)S(1)}, bf16[1,256,128]{2,1,0:T(8,128)(2,1)}, u32[]{:S(2)}) copy-start(bf16[1,256,128]{2,1,0:T(8,128)(2,1)} %k_ref.3) | copy-start | bytes 196612
  10.3 8.8 %collective-permute-start.10 = (bf16[288,256]{1,0:T(8,128)(2,1)}, bf16[288,256]{1,0:T(8,128)(2,1)S(1)}, u32[]{:S(2)}, u32[]{:S(2)}) collective-permute-start(bf16[288,256]{1,0:T(8,128)(2,1)} %get-tuple-element.42), channel_id=1, source_target_pairs={{0,16},{8,24},{16,0},{24,8},{1,17},{9,25},{17,1},{25,9},{2,18},{10... | collective-permute-start | bytes 442376 | tf_op jit(solution)/shard_map/ppermute | solution.py:472
  12.3 7.4 %collective-permute-start.11 = (bf16[128,256]{1,0:T(8,128)(2,1)S(1)}, bf16[128,256]{1,0:T(8,128)(2,1)S(1)}, u32[]{:S(2)}, u32[]{:S(2)}) collective-permute-start(bf16[128,256]{1,0:T(8,128)(2,1)S(1)} %get-tuple-element.44), channel_id=1, source_target_pairs={{0,24},{8,16},{16,8},{24,0},{1,25},{9,17},{17,9},{25,1},{2,26},{10... | collective-permute-start | bytes 196616 | tf_op jit(solution)/shard_map/ppermute | solution.py:472
  14.8 5.4 %collective-permute-start.12 = (bf16[128,256]{1,0:T(8,128)(2,1)S(1)}, bf16[128,256]{1,0:T(8,128)(2,1)S(1)}, u32[]{:S(2)}, u32[]{:S(2)}) collective-permute-start(bf16[128,256]{1,0:T(8,128)(2,1)S(1)} %get-tuple-element.45), channel_id=1, source_target_pairs={{0,8},{8,0},{16,24},{24,16},{1,9},{9,1},{17,25},{25,17},{2,10},{10... | collective-permute-start | bytes 196616 | tf_op jit(solution)/shard_map/ppermute | solution.py:472
  15.3 6.9 %collective-permute-start.13 = (bf16[128,256]{1,0:T(8,128)(2,1)S(1)}, bf16[128,256]{1,0:T(8,128)(2,1)S(1)}, u32[]{:S(2)}, u32[]{:S(2)}) collective-permute-start(bf16[128,256]{1,0:T(8,128)(2,1)S(1)} %get-tuple-element.46), channel_id=1, source_target_pairs={{0,16},{8,24},{16,0},{24,8},{1,17},{9,25},{17,1},{25,9},{2,18},{10... | collective-permute-start | bytes 196616 | tf_op jit(solution)/shard_map/ppermute | solution.py:472
  15.8 6.4 %copy-start.4 = (bf16[1,3,1024]{2,1,0:T(4,128)(2,1)S(1)}, bf16[1,3,1024]{2,1,0:T(4,128)(2,1)}, u32[]{:S(2)}) copy-start(bf16[1,3,1024]{2,1,0:T(4,128)(2,1)} %taps_ref.3) | copy-start | bytes 18436
  15.8 6.4 %copy-start.6 = (bf16[288,256]{1,0:T(8,128)(2,1)S(1)}, bf16[288,256]{1,0:T(8,128)(2,1)}, u32[]{:S(2)}) copy-start(bf16[288,256]{1,0:T(8,128)(2,1)} %get-tuple-element.43.rest_3_) | copy-start | bytes 442372
  16.6 12.5 %collective-permute-start.1 = (bf16[416,256]{1,0:T(8,128)(2,1)S(1)}, bf16[416,256]{1,0:T(8,128)(2,1)S(1)}, u32[]{:S(2)}, u32[]{:S(2)}) collective-permute-start(bf16[416,256]{1,0:T(8,128)(2,1)S(1)} %get-tuple-element.32), channel_id=1, source_target_pairs={{0,24},{8,16},{16,8},{24,0},{1,25},{9,17},{17,9},{25,1},{2,26},{10... | collective-permute-start | bytes 638984 | tf_op jit(solution)/shard_map/ppermute | solution.py:472
  19.1 10.4 %collective-permute-start.2 = (bf16[416,256]{1,0:T(8,128)(2,1)S(1)}, bf16[416,256]{1,0:T(8,128)(2,1)S(1)}, u32[]{:S(2)}, u32[]{:S(2)}) collective-permute-start(bf16[416,256]{1,0:T(8,128)(2,1)S(1)} %get-tuple-element.33), channel_id=1, source_target_pairs={{0,8},{8,0},{16,24},{24,16},{1,9},{9,1},{17,25},{25,17},{2,10},{10... | collective-permute-start | bytes 638984 | tf_op jit(solution)/shard_map/ppermute | solution.py:472
  19.7 2.6 %copy-start.5 = (s32[1,4]{1,0:T(1,128)S(1)}, s32[1,4]{1,0:T(1,128)}, u32[]{:S(2)}) copy-start(s32[1,4]{1,0:T(1,128)} %bounds.3) | copy-start | bytes 52
  19.7 11.2 %collective-permute-start.3 = (bf16[416,256]{1,0:T(8,128)(2,1)S(1)}, bf16[416,256]{1,0:T(8,128)(2,1)S(1)}, u32[]{:S(2)}, u32[]{:S(2)}) collective-permute-start(bf16[416,256]{1,0:T(8,128)(2,1)S(1)} %get-tuple-element.34), channel_id=1, source_target_pairs={{0,16},{8,24},{16,0},{24,8},{1,17},{9,25},{17,1},{25,9},{2,18},{10... | collective-permute-start | bytes 638984 | tf_op jit(solution)/shard_map/ppermute | solution.py:472
  27.3 10.7 %collective-permute-start.14 = (bf16[288,256]{1,0:T(8,128)(2,1)S(1)}, bf16[288,256]{1,0:T(8,128)(2,1)S(1)}, u32[]{:S(2)}, u32[]{:S(2)}) collective-permute-start(bf16[288,256]{1,0:T(8,128)(2,1)S(1)} %get-tuple-element.47), channel_id=1, source_target_pairs={{0,31},{1,24},{2,25},{3,26},{4,27},{5,28},{6,29},{7,30},{8,23},{9,... | collective-permute-start | bytes 442376 | tf_op jit(solution)/shard_map/ppermute | solution.py:480
  29.1 9.3 %collective-permute-start.15 = (bf16[288,256]{1,0:T(8,128)(2,1)S(1)}, bf16[288,256]{1,0:T(8,128)(2,1)S(1)}, u32[]{:S(2)}, u32[]{:S(2)}) collective-permute-start(bf16[288,256]{1,0:T(8,128)(2,1)S(1)} %get-tuple-element.48), channel_id=1, source_target_pairs={{0,15},{1,8},{2,9},{3,10},{4,11},{5,12},{6,13},{7,14},{8,7},{9,0},... | collective-permute-start | bytes 442376 | tf_op jit(solution)/shard_map/ppermute | solution.py:480
  29.1 9.3 %collective-permute-start.16 = (bf16[288,256]{1,0:T(8,128)(2,1)S(1)}, bf16[288,256]{1,0:T(8,128)(2,1)S(1)}, u32[]{:S(2)}, u32[]{:S(2)}) collective-permute-start(bf16[288,256]{1,0:T(8,128)(2,1)S(1)} %get-tuple-element.49), channel_id=1, source_target_pairs={{0,23},{1,16},{2,17},{3,18},{4,19},{5,20},{6,21},{7,22},{8,31},{9,... | collective-permute-start | bytes 442376 | tf_op jit(solution)/shard_map/ppermute | solution.py:480
  29.5 12.7 %collective-permute-start.17 = (bf16[288,256]{1,0:T(8,128)(2,1)S(1)}, bf16[288,256]{1,0:T(8,128)(2,1)S(1)}, u32[]{:S(2)}, u32[]{:S(2)}) collective-permute-start(bf16[288,256]{1,0:T(8,128)(2,1)S(1)} %get-tuple-element.50), channel_id=1, source_target_pairs={{0,7},{1,0},{2,1},{3,2},{4,3},{5,4},{6,5},{7,6},{8,15},{9,8},{10,9... | collective-permute-start | bytes 442376 | tf_op jit(solution)/shard_map/ppermute | solution.py:480
  36.0 7.2 %collective-permute-start.4 = (bf16[288,256]{1,0:T(8,128)(2,1)S(1)}, bf16[288,256]{1,0:T(8,128)(2,1)S(1)}, u32[]{:S(2)}, u32[]{:S(2)}) collective-permute-start(bf16[288,256]{1,0:T(8,128)(2,1)S(1)} %get-tuple-element.36), channel_id=1, source_target_pairs={{0,31},{1,24},{2,25},{3,26},{4,27},{5,28},{6,29},{7,30},{8,23},{9,... | collective-permute-start | bytes 442376 | tf_op jit(solution)/shard_map/ppermute | solution.py:480
  38.0 5.1 %collective-permute-start.5 = (bf16[288,256]{1,0:T(8,128)(2,1)S(1)}, bf16[288,256]{1,0:T(8,128)(2,1)S(1)}, u32[]{:S(2)}, u32[]{:S(2)}) collective-permute-start(bf16[288,256]{1,0:T(8,128)(2,1)S(1)} %get-tuple-element.37), channel_id=1, source_target_pairs={{0,7},{1,0},{2,1},{3,2},{4,3},{5,4},{6,5},{7,6},{8,15},{9,8},{10,9... | collective-permute-start | bytes 442376 | tf_op jit(solution)/shard_map/ppermute | solution.py:480
  38.4 7.9 %collective-permute-start.6 = (bf16[288,256]{1,0:T(8,128)(2,1)S(1)}, bf16[288,256]{1,0:T(8,128)(2,1)S(1)}, u32[]{:S(2)}, u32[]{:S(2)}) collective-permute-start(bf16[288,256]{1,0:T(8,128)(2,1)S(1)} %get-tuple-element.38), channel_id=1, source_target_pairs={{0,15},{1,8},{2,9},{3,10},{4,11},{5,12},{6,13},{7,14},{8,7},{9,0},... | collective-permute-start | bytes 442376 | tf_op jit(solution)/shard_map/ppermute | solution.py:480
  38.4 7.9 %collective-permute-start.7 = (bf16[288,256]{1,0:T(8,128)(2,1)S(1)}, bf16[288,256]{1,0:T(8,128)(2,1)S(1)}, u32[]{:S(2)}, u32[]{:S(2)}) collective-permute-start(bf16[288,256]{1,0:T(8,128)(2,1)S(1)} %get-tuple-element.39), channel_id=1, source_target_pairs={{0,23},{1,16},{2,17},{3,18},{4,19},{5,20},{6,21},{7,22},{8,31},{9,... | collective-permute-start | bytes 442376 | tf_op jit(solution)/shard_map/ppermute | solution.py:480

commit v6 on v5

--- a/solution.py
+++ b/solution.py
@@ -287,8 +287,9 @@
             moved = gates[pl.ds(8 - shift + i * TOK, TOK)]
             mixed += jnp.where(depth >= shift, taps[shift : shift + 1] * moved, 0.0)
         incoming = grad[i].astype(F32)
-        gate = 1.0 / (1.0 + jnp.exp(-mixed))
-        scale = 1.0 / den
+        spread_mixed = 1.0 + jnp.exp(-mixed)
+        shared = 1.0 / (spread_mixed * den)
+        gate, scale = shared * den, shared * spread_mixed
         attended = num * scale
         d_num = incoming * mixed * gate * scale
         d_den = -jnp.sum(d_num * attended, axis=1, keepdims=True)

time: 47.4 us -> 47.6 us (level)
  transfers between devices with their start and end apart: 18 -> 18, of which waited for: 5 -> 4; matrix products, arithmetic and copies ran while one was open for 0% -> 0% of each run, Pallas kernels for 29% -> 30%
where the time goes in v6:
time: 47.6 us; the launch traced here: 47.4 us
  starting transfers between devices  24.9 us (52%)
  Pallas kernels  15 us (32%)
  waiting for transfers between devices  6.76 us (14%)
  between operations  0.73 us (2%)
    ppermute x9, starting transfers between devices, across(): return lax.ppermute(value, 'ctx', [(c, c ^ partner) for c in range(count)])  10.7 us
    pallas_call x2, Pallas kernels, attend(): pl.pallas_call(functools.partial(attend_kernel, count, phase), cost_estim...  10.3 us
    ppermute x8, starting transfers between devices, across_back(): return lax.ppermute(value, ('ctx', 'pipe'), pairs)  9.62 us
    ppermute x1, starting transfers between devices, on_device(): cotangent = lax.ppermute(out_grad, 'pipe', shift)  4.54 us
    ppermute x8, waiting for transfers between devices, across_back(): return lax.ppermute(value, ('ctx', 'pipe'), pairs)  3.25 us
    pallas_call x2, Pallas kernels, pack(): pl.pallas_call(functools.partial(pack_kernel, count, phase), cost_estimat...  2.83 us
    ppermute x9, waiting for transfers between devices, across(): return lax.ppermute(value, 'ctx', [(c, c ^ partner) for c in range(count)])  2.22 us
    pallas_call x2, Pallas kernels, unpack(): pl.pallas_call(functools.partial(unpack_kernel, count, phase), cost_estim...  1.79 us
  transfers between devices with their start and end apart: 18, of which 4 were waited for; matrix products, arithmetic and copies ran while one was open for 0% of the time, Pallas kernels for 30%

profile of v6, /device:TPU:0, one launch (start us, length us, event | category | flops | bytes accessed | tf_op | source)
XLA Modules:
  0.0 47.4 jit_solution(6445472033210057827)
XLA Ops:
  0.6 4.5 %collective-permute-start = (bf16[1,256,1024]{2,1,0:T(8,128)(2,1)}, bf16[1,256,1024]{2,1,0:T(8,128)(2,1)S(1)}, u32[]{:S(2)}, u32[]{:S(2)}) collective-permute-start(bf16[1,256,1024]{2,1,0:T(8,128)(2,1)} %param.11), channel_id=1, source_target_pairs={{0,7},{1,0},{2,1},{3,2},{4,3},{5,4},{6,5},{7,6},{8,15},{9,8},{10,9... | collective-permute-start | bytes 1572872 | tf_op jit(solution)/shard_map/ppermute | solution.py:485
  5.2 2.1 %shard_map.105 = (bf16[288,256]{1,0:T(8,128)(2,1)}, bf16[288,256]{1,0:T(8,128)(2,1)}, bf16[288,256]{1,0:T(8,128)(2,1)}, bf16[288,256]{1,0:T(8,128)(2,1)}) custom-call(bf16[1,256,128]{2,1,0:T(8,128)(2,1)} %q_ref.3, bf16[1,256,128]{2,1,0:T(8,128)(2,1)} %k_ref.3, bf16[1,256,1024]{2,1,0:T(8,128)(2,1)} %v_ref.3, bf16[1,256,1024]{2,1,0:T(8,128)(2,1)} %gate_ref.3), custom_call_target="tpu_custom_call" | custom-call | flops 2000000000 | bytes 6000000 | tf_op jit(solution)/shard_map/pallas_call | solution.py:102
  7.3 2.5 %collective-permute-start.8 = (bf16[288,256]{1,0:T(8,128)(2,1)}, bf16[288,256]{1,0:T(8,128)(2,1)S(1)}, u32[]{:S(2)}, u32[]{:S(2)}) collective-permute-start(bf16[288,256]{1,0:T(8,128)(2,1)} %get-tuple-element.40), channel_id=1, source_target_pairs={{0,24},{8,16},{16,8},{24,0},{1,25},{9,17},{17,9},{25,1},{2,26},{10... | collective-permute-start | bytes 442376 | tf_op jit(solution)/shard_map/ppermute | solution.py:473
  9.8 0.5 %collective-permute-start.9 = (bf16[288,256]{1,0:T(8,128)(2,1)}, bf16[288,256]{1,0:T(8,128)(2,1)S(1)}, u32[]{:S(2)}, u32[]{:S(2)}) collective-permute-start(bf16[288,256]{1,0:T(8,128)(2,1)} %get-tuple-element.41), channel_id=1, source_target_pairs={{0,8},{8,0},{16,24},{24,16},{1,9},{9,1},{17,25},{25,17},{2,10},{10... | collective-permute-start | bytes 442376 | tf_op jit(solution)/shard_map/ppermute | solution.py:473
  10.3 0.6 %collective-permute-start.10 = (bf16[288,256]{1,0:T(8,128)(2,1)}, bf16[288,256]{1,0:T(8,128)(2,1)S(1)}, u32[]{:S(2)}, u32[]{:S(2)}) collective-permute-start(bf16[288,256]{1,0:T(8,128)(2,1)} %get-tuple-element.42), channel_id=1, source_target_pairs={{0,16},{8,24},{16,0},{24,8},{1,17},{9,25},{17,1},{25,9},{2,18},{10... | collective-permute-start | bytes 442376 | tf_op jit(solution)/shard_map/ppermute | solution.py:473
  10.9 1.3 %collective-permute-done.grad_ref.rest_0_ = bf16[1,256,1024]{2,1,0:T(8,128)(2,1)S(1)} collective-permute-done((bf16[1,256,1024]{2,1,0:T(8,128)(2,1)}, bf16[1,256,1024]{2,1,0:T(8,128)(2,1)S(1)}, u32[]{:S(2)}, u32[]{:S(2)}) %collective-permute-start) | collective-permute-done | bytes 524320 | tf_op jit(solution)/shard_map/ppermute | solution.py:485
  12.2 0.1 shard_map.102
  12.3 2.5 %collective-permute-start.11 = (bf16[128,256]{1,0:T(8,128)(2,1)S(1)}, bf16[128,256]{1,0:T(8,128)(2,1)S(1)}, u32[]{:S(2)}, u32[]{:S(2)}) collective-permute-start(bf16[128,256]{1,0:T(8,128)(2,1)S(1)} %get-tuple-element.44), channel_id=1, source_target_pairs={{0,24},{8,16},{16,8},{24,0},{1,25},{9,17},{17,9},{25,1},{2,26},{10... | collective-permute-start | bytes 196616 | tf_op jit(solution)/shard_map/ppermute | solution.py:473
  14.8 0.5 %collective-permute-start.12 = (bf16[128,256]{1,0:T(8,128)(2,1)S(1)}, bf16[128,256]{1,0:T(8,128)(2,1)S(1)}, u32[]{:S(2)}, u32[]{:S(2)}) collective-permute-start(bf16[128,256]{1,0:T(8,128)(2,1)S(1)} %get-tuple-element.45), channel_id=1, source_target_pairs={{0,8},{8,0},{16,24},{24,16},{1,9},{9,1},{17,25},{25,17},{2,10},{10... | collective-permute-start | bytes 196616 | tf_op jit(solution)/shard_map/ppermute | solution.py:473
  15.3 0.0 collective-permute-done.8.rest_0_
  15.3 0.5 %collective-permute-start.13 = (bf16[128,256]{1,0:T(8,128)(2,1)S(1)}, bf16[128,256]{1,0:T(8,128)(2,1)S(1)}, u32[]{:S(2)}, u32[]{:S(2)}) collective-permute-start(bf16[128,256]{1,0:T(8,128)(2,1)S(1)} %get-tuple-element.46), channel_id=1, source_target_pairs={{0,16},{8,24},{16,0},{24,8},{1,17},{9,25},{17,1},{25,9},{2,18},{10... | collective-permute-start | bytes 196616 | tf_op jit(solution)/shard_map/ppermute | solution.py:473
  15.8 0.0 copy-done
  15.8 0.0 copy-done.1
  15.8 0.0 copy-done.2
  15.8 0.0 copy-start.4
  15.8 0.0 copy-start.6
  15.9 0.7 %shard_map.103 = (bf16[416,256]{1,0:T(8,128)(2,1)S(1)}, bf16[416,256]{1,0:T(8,128)(2,1)S(1)}, bf16[416,256]{1,0:T(8,128)(2,1)S(1)}, bf16[416,256]{1,0:T(8,128)(2,1)S(1)}) custom-call(bf16[1,256,128]{2,1,0:T(8,128)(2,1)S(1)} %copy-done.2, bf16[1,256,128]{2,1,0:T(8,128)(2,1)S(1)} %copy-done.3, bf16[1,256,1024]{2,1,0:T(8,128)(2,1)S(1)} %copy-done, ...), custom_call_target="tpu_custom_call" | custom-call | flops 2000000000 | bytes 6000000 | tf_op jit(solution)/shard_map/pallas_call | solution.py:102
  16.6 0.0 collective-permute-done.9.rest_1_
  16.6 2.5 %collective-permute-start.1 = (bf16[416,256]{1,0:T(8,128)(2,1)S(1)}, bf16[416,256]{1,0:T(8,128)(2,1)S(1)}, u32[]{:S(2)}, u32[]{:S(2)}) collective-permute-start(bf16[416,256]{1,0:T(8,128)(2,1)S(1)} %get-tuple-element.32), channel_id=1, source_target_pairs={{0,24},{8,16},{16,8},{24,0},{1,25},{9,17},{17,9},{25,1},{2,26},{10... | collective-permute-start | bytes 638984 | tf_op jit(solution)/shard_map/ppermute | solution.py:473
  19.1 0.0 collective-permute-done.10.rest_2_
  19.1 0.5 %collective-permute-start.2 = (bf16[416,256]{1,0:T(8,128)(2,1)S(1)}, bf16[416,256]{1,0:T(8,128)(2,1)S(1)}, u32[]{:S(2)}, u32[]{:S(2)}) collective-permute-start(bf16[416,256]{1,0:T(8,128)(2,1)S(1)} %get-tuple-element.33), channel_id=1, source_target_pairs={{0,8},{8,0},{16,24},{24,16},{1,9},{9,1},{17,25},{25,17},{2,10},{10... | collective-permute-start | bytes 638984 | tf_op jit(solution)/shard_map/ppermute | solution.py:473
  19.7 0.0 collective-permute-done.11.rest_4_
  19.7 0.5 %collective-permute-start.3 = (bf16[416,256]{1,0:T(8,128)(2,1)S(1)}, bf16[416,256]{1,0:T(8,128)(2,1)S(1)}, u32[]{:S(2)}, u32[]{:S(2)}) collective-permute-start(bf16[416,256]{1,0:T(8,128)(2,1)S(1)} %get-tuple-element.34), channel_id=1, source_target_pairs={{0,16},{8,24},{16,0},{24,8},{1,17},{9,25},{17,1},{25,9},{2,18},{10... | collective-permute-start | bytes 638984 | tf_op jit(solution)/shard_map/ppermute | solution.py:473
  20.2 0.0 collective-permute-done.12.rest_5_
  20.2 2.0 %collective-permute-done.13.rest_6_ = bf16[128,256]{1,0:T(8,128)(2,1)S(1)} collective-permute-done((bf16[128,256]{1,0:T(8,128)(2,1)S(1)}, bf16[128,256]{1,0:T(8,128)(2,1)S(1)}, u32[]{:S(2)}, u32[]{:S(2)}) %collective-permute-start.13) | collective-permute-done | bytes 65568 | tf_op jit(solution)/shard_map/ppermute | solution.py:473
  22.2 5.1 %shard_map.106 = (bf16[288,256]{1,0:T(8,128)(2,1)S(1)}, bf16[288,256]{1,0:T(8,128)(2,1)S(1)}, bf16[288,256]{1,0:T(8,128)(2,1)S(1)}, bf16[288,256]{1,0:T(8,128)(2,1)S(1)}) custom-call(s32[1,4]{1,0:T(1,128)S(1)} %copy-done.5, bf16[1,3,1024]{2,1,0:T(4,128)(2,1)S(1)} %copy-done.4, bf16[288,256]{1,0:T(8,128)(2,1)S(1)} %collective-permute-done.8.rest_0_, ...), custom_call_target="tpu_custom_call" | custom-call | flops 5000000000 | bytes 15000000 | tf_op jit(solution)/shard_map/pallas_call | solution.py:377
  27.4 1.8 %collective-permute-start.14 = (bf16[288,256]{1,0:T(8,128)(2,1)S(1)}, bf16[288,256]{1,0:T(8,128)(2,1)S(1)}, u32[]{:S(2)}, u32[]{:S(2)}) collective-permute-start(bf16[288,256]{1,0:T(8,128)(2,1)S(1)} %get-tuple-element.47), channel_id=1, source_target_pairs={{0,31},{1,24},{2,25},{3,26},{4,27},{5,28},{6,29},{7,30},{8,23},{9,... | collective-permute-start | bytes 442376 | tf_op jit(solution)/shard_map/ppermute | solution.py:481
  29.2 0.0 collective-permute-start.15
  29.2 0.0 collective-permute-done.1.rest_0_
  29.2 0.1 collective-permute-start.16
  29.4 0.2 collective-permute-done.2.rest_1_
  29.5 1.3 %collective-permute-start.17 = (bf16[288,256]{1,0:T(8,128)(2,1)S(1)}, bf16[288,256]{1,0:T(8,128)(2,1)S(1)}, u32[]{:S(2)}, u32[]{:S(2)}) collective-permute-start(bf16[288,256]{1,0:T(8,128)(2,1)S(1)} %get-tuple-element.50), channel_id=1, source_target_pairs={{0,7},{1,0},{2,1},{3,2},{4,3},{5,4},{6,5},{7,6},{8,15},{9,8},{10,9... | collective-permute-start | bytes 442376 | tf_op jit(solution)/shard_map/ppermute | solution.py:481
  30.8 0.0 collective-permute-done.3.rest_2_
  30.8 5.2 %shard_map.104 = (bf16[288,256]{1,0:T(8,128)(2,1)S(1)}, bf16[288,256]{1,0:T(8,128)(2,1)S(1)}, bf16[288,256]{1,0:T(8,128)(2,1)S(1)}, bf16[288,256]{1,0:T(8,128)(2,1)S(1)}) custom-call(s32[1,4]{1,0:T(1,128)S(1)} %copy-done.5, bf16[1,3,1024]{2,1,0:T(4,128)(2,1)S(1)} %copy-done.4, bf16[416,256]{1,0:T(8,128)(2,1)S(1)} %collective-permute-done.1.rest_0_, ...), custom_call_target="tpu_custom_call" | custom-call | flops 5000000000 | bytes 15000000 | tf_op jit(solution)/shard_map/pallas_call | solution.py:377
  36.0 2.1 %collective-permute-start.4 = (bf16[288,256]{1,0:T(8,128)(2,1)S(1)}, bf16[288,256]{1,0:T(8,128)(2,1)S(1)}, u32[]{:S(2)}, u32[]{:S(2)}) collective-permute-start(bf16[288,256]{1,0:T(8,128)(2,1)S(1)} %get-tuple-element.36), channel_id=1, source_target_pairs={{0,31},{1,24},{2,25},{3,26},{4,27},{5,28},{6,29},{7,30},{8,23},{9,... | collective-permute-start | bytes 442376 | tf_op jit(solution)/shard_map/ppermute | solution.py:481
  38.1 0.0 collective-permute-done.14.rest_0_
  38.1 0.4 collective-permute-start.5
  38.5 0.0 collective-permute-done.15.rest_1_
  38.5 0.0 collective-permute-start.6
  38.5 0.0 collective-permute-done.16.rest_2_
  38.5 3.8 %collective-permute-start.7 = (bf16[288,256]{1,0:T(8,128)(2,1)S(1)}, bf16[288,256]{1,0:T(8,128)(2,1)S(1)}, u32[]{:S(2)}, u32[]{:S(2)}) collective-permute-start(bf16[288,256]{1,0:T(8,128)(2,1)S(1)} %get-tuple-element.39), channel_id=1, source_target_pairs={{0,23},{1,16},{2,17},{3,18},{4,19},{5,20},{6,21},{7,22},{8,31},{9,... | collective-permute-start | bytes 442376 | tf_op jit(solution)/shard_map/ppermute | solution.py:481
  42.3 0.0 collective-permute-done.17.rest_3_
  42.3 0.8 %shard_map.107 = (bf16[1,256,1024]{2,1,0:T(8,128)(2,1)}, bf16[1,256,1024]{2,1,0:T(8,128)(2,1)}, bf16[2,128,256]{2,1,0:T(8,128)(2,1)S(1)}) custom-call(bf16[288,256]{1,0:T(8,128)(2,1)S(1)} %collective-permute-done.14.rest_0_, bf16[288,256]{1,0:T(8,128)(2,1)S(1)} %collective-permute-done.15.rest_1_, bf16[288,256]{1,0:T(8,128)(2,1)S(1)} %collective-permute-done.16.rest_2_, ...), custom_call_target="tpu_custom_call" | custom-call | flops 1000000000 | bytes 3000000 | tf_op jit(solution)/shard_map/pallas_call | solution.py:446
  43.2 0.0 collective-permute-done.4.rest_0_
  43.2 0.0 collective-permute-done.5.rest_1_
  43.2 3.2 %collective-permute-done.6.rest_2_ = bf16[288,256]{1,0:T(8,128)(2,1)S(1)} collective-permute-done((bf16[288,256]{1,0:T(8,128)(2,1)S(1)}, bf16[288,256]{1,0:T(8,128)(2,1)S(1)}, u32[]{:S(2)}, u32[]{:S(2)}) %collective-permute-start.6) | collective-permute-done | bytes 147488 | tf_op jit(solution)/shard_map/ppermute | solution.py:481
  46.4 0.0 collective-permute-done.7.rest_3_
  46.4 0.9 %shard_map.108 = (bf16[1,256,1024]{2,1,0:T(8,128)(2,1)}, bf16[1,256,1024]{2,1,0:T(8,128)(2,1)}, bf16[1,256,128]{2,1,0:T(8,128)(2,1)}, bf16[1,256,128]{2,1,0:T(8,128)(2,1)}) custom-call(bf16[288,256]{1,0:T(8,128)(2,1)S(1)} %collective-permute-done.4.rest_0_, ...), custom_call_target="tpu_custom_call", output_to_operand_aliasing={{0}: (5, {}), {1}: (6, {})} | custom-call | flops 1000000000 | bytes 3000000 | tf_op jit(solution)/shard_map/pallas_call | solution.py:446
  (9 shorter events, 0.0 us)
Async XLA Ops:
  0.6 11.6 %collective-permute-start = (bf16[1,256,1024]{2,1,0:T(8,128)(2,1)}, bf16[1,256,1024]{2,1,0:T(8,128)(2,1)S(1)}, u32[]{:S(2)}, u32[]{:S(2)}) collective-permute-start(bf16[1,256,1024]{2,1,0:T(8,128)(2,1)} %param.11), channel_id=1, source_target_pairs={{0,7},{1,0},{2,1},{3,2},{4,3},{5,4},{6,5},{7,6},{8,15},{9,8},{10,9... | collective-permute-start | bytes 1572872 | tf_op jit(solution)/shard_map/ppermute | solution.py:485
  7.3 8.0 %collective-permute-start.8 = (bf16[288,256]{1,0:T(8,128)(2,1)}, bf16[288,256]{1,0:T(8,128)(2,1)S(1)}, u32[]{:S(2)}, u32[]{:S(2)}) collective-permute-start(bf16[288,256]{1,0:T(8,128)(2,1)} %get-tuple-element.40), channel_id=1, source_target_pairs={{0,24},{8,16},{16,8},{24,0},{1,25},{9,17},{17,9},{25,1},{2,26},{10... | collective-permute-start | bytes 442376 | tf_op jit(solution)/shard_map/ppermute | solution.py:473
  9.8 6.8 %collective-permute-start.9 = (bf16[288,256]{1,0:T(8,128)(2,1)}, bf16[288,256]{1,0:T(8,128)(2,1)S(1)}, u32[]{:S(2)}, u32[]{:S(2)}) collective-permute-start(bf16[288,256]{1,0:T(8,128)(2,1)} %get-tuple-element.41), channel_id=1, source_target_pairs={{0,8},{8,0},{16,24},{24,16},{1,9},{9,1},{17,25},{25,17},{2,10},{10... | collective-permute-start | bytes 442376 | tf_op jit(solution)/shard_map/ppermute | solution.py:473
  10.3 5.5 %copy-start = (bf16[1,256,1024]{2,1,0:T(8,128)(2,1)S(1)}, bf16[1,256,1024]{2,1,0:T(8,128)(2,1)}, u32[]{:S(2)}) copy-start(bf16[1,256,1024]{2,1,0:T(8,128)(2,1)} %v_ref.3) | copy-start | bytes 1572868
  10.3 5.5 %copy-start.1 = (bf16[1,256,1024]{2,1,0:T(8,128)(2,1)S(1)}, bf16[1,256,1024]{2,1,0:T(8,128)(2,1)}, u32[]{:S(2)}) copy-start(bf16[1,256,1024]{2,1,0:T(8,128)(2,1)} %gate_ref.3) | copy-start | bytes 1572868
  10.3 5.5 %copy-start.2 = (bf16[1,256,128]{2,1,0:T(8,128)(2,1)S(1)}, bf16[1,256,128]{2,1,0:T(8,128)(2,1)}, u32[]{:S(2)}) copy-start(bf16[1,256,128]{2,1,0:T(8,128)(2,1)} %q_ref.3) | copy-start | bytes 196612
  10.3 5.5 %copy-start.3 = (bf16[1,256,128]{2,1,0:T(8,128)(2,1)S(1)}, bf16[1,256,128]{2,1,0:T(8,128)(2,1)}, u32[]{:S(2)}) copy-start(bf16[1,256,128]{2,1,0:T(8,128)(2,1)} %k_ref.3) | copy-start | bytes 196612
  10.3 8.8 %collective-permute-start.10 = (bf16[288,256]{1,0:T(8,128)(2,1)}, bf16[288,256]{1,0:T(8,128)(2,1)S(1)}, u32[]{:S(2)}, u32[]{:S(2)}) collective-permute-start(bf16[288,256]{1,0:T(8,128)(2,1)} %get-tuple-element.42), channel_id=1, source_target_pairs={{0,16},{8,24},{16,0},{24,8},{1,17},{9,25},{17,1},{25,9},{2,18},{10... | collective-permute-start | bytes 442376 | tf_op jit(solution)/shard_map/ppermute | solution.py:473
  12.3 7.4 %collective-permute-start.11 = (bf16[128,256]{1,0:T(8,128)(2,1)S(1)}, bf16[128,256]{1,0:T(8,128)(2,1)S(1)}, u32[]{:S(2)}, u32[]{:S(2)}) collective-permute-start(bf16[128,256]{1,0:T(8,128)(2,1)S(1)} %get-tuple-element.44), channel_id=1, source_target_pairs={{0,24},{8,16},{16,8},{24,0},{1,25},{9,17},{17,9},{25,1},{2,26},{10... | collective-permute-start | bytes 196616 | tf_op jit(solution)/shard_map/ppermute | solution.py:473
  14.8 5.4 %collective-permute-start.12 = (bf16[128,256]{1,0:T(8,128)(2,1)S(1)}, bf16[128,256]{1,0:T(8,128)(2,1)S(1)}, u32[]{:S(2)}, u32[]{:S(2)}) collective-permute-start(bf16[128,256]{1,0:T(8,128)(2,1)S(1)} %get-tuple-element.45), channel_id=1, source_target_pairs={{0,8},{8,0},{16,24},{24,16},{1,9},{9,1},{17,25},{25,17},{2,10},{10... | collective-permute-start | bytes 196616 | tf_op jit(solution)/shard_map/ppermute | solution.py:473
  15.3 6.9 %collective-permute-start.13 = (bf16[128,256]{1,0:T(8,128)(2,1)S(1)}, bf16[128,256]{1,0:T(8,128)(2,1)S(1)}, u32[]{:S(2)}, u32[]{:S(2)}) collective-permute-start(bf16[128,256]{1,0:T(8,128)(2,1)S(1)} %get-tuple-element.46), channel_id=1, source_target_pairs={{0,16},{8,24},{16,0},{24,8},{1,17},{9,25},{17,1},{25,9},{2,18},{10... | collective-permute-start | bytes 196616 | tf_op jit(solution)/shard_map/ppermute | solution.py:473
  15.8 6.4 %copy-start.4 = (bf16[1,3,1024]{2,1,0:T(4,128)(2,1)S(1)}, bf16[1,3,1024]{2,1,0:T(4,128)(2,1)}, u32[]{:S(2)}) copy-start(bf16[1,3,1024]{2,1,0:T(4,128)(2,1)} %taps_ref.3) | copy-start | bytes 18436
  15.8 6.4 %copy-start.6 = (bf16[288,256]{1,0:T(8,128)(2,1)S(1)}, bf16[288,256]{1,0:T(8,128)(2,1)}, u32[]{:S(2)}) copy-start(bf16[288,256]{1,0:T(8,128)(2,1)} %get-tuple-element.43.rest_3_) | copy-start | bytes 442372
  16.6 12.6 %collective-permute-start.1 = (bf16[416,256]{1,0:T(8,128)(2,1)S(1)}, bf16[416,256]{1,0:T(8,128)(2,1)S(1)}, u32[]{:S(2)}, u32[]{:S(2)}) collective-permute-start(bf16[416,256]{1,0:T(8,128)(2,1)S(1)} %get-tuple-element.32), channel_id=1, source_target_pairs={{0,24},{8,16},{16,8},{24,0},{1,25},{9,17},{17,9},{25,1},{2,26},{10... | collective-permute-start | bytes 638984 | tf_op jit(solution)/shard_map/ppermute | solution.py:473
  19.1 10.4 %collective-permute-start.2 = (bf16[416,256]{1,0:T(8,128)(2,1)S(1)}, bf16[416,256]{1,0:T(8,128)(2,1)S(1)}, u32[]{:S(2)}, u32[]{:S(2)}) collective-permute-start(bf16[416,256]{1,0:T(8,128)(2,1)S(1)} %get-tuple-element.33), channel_id=1, source_target_pairs={{0,8},{8,0},{16,24},{24,16},{1,9},{9,1},{17,25},{25,17},{2,10},{10... | collective-permute-start | bytes 638984 | tf_op jit(solution)/shard_map/ppermute | solution.py:473
  19.7 2.6 %copy-start.5 = (s32[1,4]{1,0:T(1,128)S(1)}, s32[1,4]{1,0:T(1,128)}, u32[]{:S(2)}) copy-start(s32[1,4]{1,0:T(1,128)} %bounds.3) | copy-start | bytes 52
  19.7 11.2 %collective-permute-start.3 = (bf16[416,256]{1,0:T(8,128)(2,1)S(1)}, bf16[416,256]{1,0:T(8,128)(2,1)S(1)}, u32[]{:S(2)}, u32[]{:S(2)}) collective-permute-start(bf16[416,256]{1,0:T(8,128)(2,1)S(1)} %get-tuple-element.34), channel_id=1, source_target_pairs={{0,16},{8,24},{16,0},{24,8},{1,17},{9,25},{17,1},{25,9},{2,18},{10... | collective-permute-start | bytes 638984 | tf_op jit(solution)/shard_map/ppermute | solution.py:473
  27.4 10.7 %collective-permute-start.14 = (bf16[288,256]{1,0:T(8,128)(2,1)S(1)}, bf16[288,256]{1,0:T(8,128)(2,1)S(1)}, u32[]{:S(2)}, u32[]{:S(2)}) collective-permute-start(bf16[288,256]{1,0:T(8,128)(2,1)S(1)} %get-tuple-element.47), channel_id=1, source_target_pairs={{0,31},{1,24},{2,25},{3,26},{4,27},{5,28},{6,29},{7,30},{8,23},{9,... | collective-permute-start | bytes 442376 | tf_op jit(solution)/shard_map/ppermute | solution.py:481
  29.2 9.3 %collective-permute-start.15 = (bf16[288,256]{1,0:T(8,128)(2,1)S(1)}, bf16[288,256]{1,0:T(8,128)(2,1)S(1)}, u32[]{:S(2)}, u32[]{:S(2)}) collective-permute-start(bf16[288,256]{1,0:T(8,128)(2,1)S(1)} %get-tuple-element.48), channel_id=1, source_target_pairs={{0,15},{1,8},{2,9},{3,10},{4,11},{5,12},{6,13},{7,14},{8,7},{9,0},... | collective-permute-start | bytes 442376 | tf_op jit(solution)/shard_map/ppermute | solution.py:481
  29.2 9.3 %collective-permute-start.16 = (bf16[288,256]{1,0:T(8,128)(2,1)S(1)}, bf16[288,256]{1,0:T(8,128)(2,1)S(1)}, u32[]{:S(2)}, u32[]{:S(2)}) collective-permute-start(bf16[288,256]{1,0:T(8,128)(2,1)S(1)} %get-tuple-element.49), channel_id=1, source_target_pairs={{0,23},{1,16},{2,17},{3,18},{4,19},{5,20},{6,21},{7,22},{8,31},{9,... | collective-permute-start | bytes 442376 | tf_op jit(solution)/shard_map/ppermute | solution.py:481
  29.5 12.8 %collective-permute-start.17 = (bf16[288,256]{1,0:T(8,128)(2,1)S(1)}, bf16[288,256]{1,0:T(8,128)(2,1)S(1)}, u32[]{:S(2)}, u32[]{:S(2)}) collective-permute-start(bf16[288,256]{1,0:T(8,128)(2,1)S(1)} %get-tuple-element.50), channel_id=1, source_target_pairs={{0,7},{1,0},{2,1},{3,2},{4,3},{5,4},{6,5},{7,6},{8,15},{9,8},{10,9... | collective-permute-start | bytes 442376 | tf_op jit(solution)/shard_map/ppermute | solution.py:481
  36.0 7.2 %collective-permute-start.4 = (bf16[288,256]{1,0:T(8,128)(2,1)S(1)}, bf16[288,256]{1,0:T(8,128)(2,1)S(1)}, u32[]{:S(2)}, u32[]{:S(2)}) collective-permute-start(bf16[288,256]{1,0:T(8,128)(2,1)S(1)} %get-tuple-element.36), channel_id=1, source_target_pairs={{0,31},{1,24},{2,25},{3,26},{4,27},{5,28},{6,29},{7,30},{8,23},{9,... | collective-permute-start | bytes 442376 | tf_op jit(solution)/shard_map/ppermute | solution.py:481
  38.1 5.1 %collective-permute-start.5 = (bf16[288,256]{1,0:T(8,128)(2,1)S(1)}, bf16[288,256]{1,0:T(8,128)(2,1)S(1)}, u32[]{:S(2)}, u32[]{:S(2)}) collective-permute-start(bf16[288,256]{1,0:T(8,128)(2,1)S(1)} %get-tuple-element.37), channel_id=1, source_target_pairs={{0,7},{1,0},{2,1},{3,2},{4,3},{5,4},{6,5},{7,6},{8,15},{9,8},{10,9... | collective-permute-start | bytes 442376 | tf_op jit(solution)/shard_map/ppermute | solution.py:481
  38.5 8.0 %collective-permute-start.6 = (bf16[288,256]{1,0:T(8,128)(2,1)S(1)}, bf16[288,256]{1,0:T(8,128)(2,1)S(1)}, u32[]{:S(2)}, u32[]{:S(2)}) collective-permute-start(bf16[288,256]{1,0:T(8,128)(2,1)S(1)} %get-tuple-element.38), channel_id=1, source_target_pairs={{0,15},{1,8},{2,9},{3,10},{4,11},{5,12},{6,13},{7,14},{8,7},{9,0},... | collective-permute-start | bytes 442376 | tf_op jit(solution)/shard_map/ppermute | solution.py:481
  38.5 7.9 %collective-permute-start.7 = (bf16[288,256]{1,0:T(8,128)(2,1)S(1)}, bf16[288,256]{1,0:T(8,128)(2,1)S(1)}, u32[]{:S(2)}, u32[]{:S(2)}) collective-permute-start(bf16[288,256]{1,0:T(8,128)(2,1)S(1)} %get-tuple-element.39), channel_id=1, source_target_pairs={{0,23},{1,16},{2,17},{3,18},{4,19},{5,20},{6,21},{7,22},{8,31},{9,... | collective-permute-start | bytes 442376 | tf_op jit(solution)/shard_map/ppermute | solution.py:481
